TPU v7x, 32 devices: a whole 2x2x4 slice. The times are simulated.
32 devices in a mesh: gx: 2 (over x), gy: 4 (over z), gz: 4 (over y, core).
Axes of the slice: x: 2, y: 2, z: 4, core: 2. Of those that a mesh axis runs over, the one named last changes fastest.
Arguments:
- gas: float32 [64, 8, 32, 512], P(None, 'gx', 'gy', 'gz'), may hold values from 0 to 1
- droplet: float32 [32, 64, 4096], P(None, None, ('gx', 'gy', 'gz')), may hold values from 0 to 1
- owner: int32 [4096, 1], P(('gx', 'gy', 'gz')), may hold values from 0 to 15; in each aligned block of 128 rows (0 to 127, 128 to 255, ...) at most 16 rows name the same one
- cells: int32 [8, 4096], P(None, ('gx', 'gy', 'gz')), may hold values from 0 to 4095
- weights: float32 [8, 4096], P(None, ('gx', 'gy', 'gz')), may hold values from 0.1 to 1
- mass: float32 [4096], P(('gx', 'gy', 'gz')), may hold values from 0.25 to 4
- liquid_rate: float32 [64], replicated, may hold values from 0.05 to 0.45
- surface_rate: float32 [64], replicated, may hold values from 0.05 to 0.5
- gas_rate: float32 [64], replicated, may hold values from 0.04 to 0.16
Outputs:
- gas_next: float32 [64, 8, 32, 512], P(None, 'gx', 'gy', 'gz')
- droplet_next: float32 [32, 64, 4096], P(None, None, ('gx', 'gy', 'gz'))
Inputs may be any that keep to these rules, and one draw needn't show every extreme that they name: `owner`: among the 128 parcels of one device at most 16 name the same gas device, and some gas device is named by exactly 16 of them.
All inputs are finite; a program needn't handle non-finite values.
Results may differ from a plain program's by a relative error of at most 0.00002.
Values sent between devices are 32-bit elements; how exact they have to be, the bound alone decides.
No kernel may reach another device: no remote copies, remote signals or barrier semaphores. Data moves between devices by JAX's collectives and lax.ppermute only.
A program may use at most 64 MiB of HBM per device.

v0:
```python
import jax
import jax.numpy as jnp
from jax import lax
from jax.sharding import PartitionSpec as P

STENCIL = 8
DROP_STEPS = 4
GAS_STEPS = 2


def with_halo(block, sides, width):
    for axis, dim in sides:
        count = lax.axis_size(axis)
        forward = [(i, i + 1) for i in range(count - 1)]
        backward = [(target, source) for source, target in forward]
        low = lax.ppermute(
            lax.slice_in_dim(block, block.shape[dim] - width, None, axis=dim), axis, forward
        )
        high = lax.ppermute(lax.slice_in_dim(block, 0, width, axis=dim), axis, backward)
        block = jnp.concatenate([low, block, high], axis=dim)
    return block


def droplet_steps(state, gas_at, liquid_rate, surface_rate):
    liquid_coef = liquid_rate[None, :, None]
    surface_coef = surface_rate[:, None]
    emitted = jnp.zeros(gas_at.shape, jnp.float32)
    for substep in range(DROP_STEPS):
        surface_flux = surface_coef * (state[-1] - gas_at)
        upper_node = jnp.concatenate([state[1:], state[-1:]], axis=0)
        lower_node = jnp.concatenate([state[1:2], state[:-1]], axis=0)
        state = state + liquid_coef * (upper_node - 2.0 * state + lower_node)
        state = state.at[-1].add(-surface_flux)
        emitted = emitted + surface_flux
    return (state, emitted)


def stencil_update(padded, field, gas_rate):
    beside = padded[:, 2:, 1:-1, 1:-1] + padded[:, :-2, 1:-1, 1:-1]
    beside = beside + padded[:, 1:-1, 2:, 1:-1] + padded[:, 1:-1, :-2, 1:-1]
    beside = beside + padded[:, 1:-1, 1:-1, 2:] + padded[:, 1:-1, 1:-1, :-2]
    return field + gas_rate[:, None, None, None] * (beside - 6.0 * field)


def gas_step(field, gas_rate):
    padded = with_halo(field, (("gx", 1), ("gy", 2), ("gz", 3)), 1)
    return stencil_update(padded, field, gas_rate)


def on_device(gas, droplet, owner, cells, weights, mass, liquid_rate, surface_rate, gas_rate):
    span_first = lax.axis_size("gy")
    span_second = lax.axis_size("gz")
    group_size = span_first * span_second
    parcels = droplet.shape[2]
    capacity = 2 * parcels // group_size
    species = gas.shape[0]
    norm_wts = weights / jnp.sum(weights, axis=0, keepdims=True)
    target = owner[:, 0]
    onehot = (target[:, None] == jnp.arange(group_size, dtype=jnp.int32)[None, :]).astype(jnp.int32)
    slot_rank = jnp.sum(onehot * (jnp.cumsum(onehot, axis=0) - 1), axis=1)
    slot_index = target * capacity + slot_rank
    send_ids = jnp.zeros((STENCIL, group_size * capacity), jnp.int32).at[:, slot_index].set(cells)
    send_ids = send_ids.reshape(STENCIL, group_size, capacity)
    send_wts = (
        jnp.zeros((STENCIL, group_size * capacity), jnp.float32).at[:, slot_index].set(norm_wts)
    )
    send_wts = send_wts.reshape(STENCIL, group_size, capacity)
    gasflat = gas.reshape(species, -1)
    cell_ids = lax.all_to_all(send_ids, ("gy", "gz"), split_axis=1, concat_axis=1, tiled=True)
    cell_wts = lax.all_to_all(send_wts, ("gy", "gz"), split_axis=1, concat_axis=1, tiled=True)
    values = gasflat[:, cell_ids.reshape(-1)].reshape((species,) + cell_ids.shape)
    row_values = jnp.sum(cell_wts[None] * values, axis=1)
    returned = lax.all_to_all(row_values, ("gy", "gz"), split_axis=1, concat_axis=1, tiled=True)
    gas_at = returned.reshape(species, -1)[:, slot_index]
    droplet_next, emitted = droplet_steps(droplet, gas_at, liquid_rate, surface_rate)
    source = mass[None, :] * emitted
    send_source = (
        jnp.zeros((species, group_size * capacity), jnp.float32).at[:, slot_index].set(source)
    )
    recv_source = lax.all_to_all(
        send_source.reshape(species, group_size, capacity),
        ("gy", "gz"),
        split_axis=1,
        concat_axis=1,
        tiled=True,
    )
    field = gas
    for substep in range(GAS_STEPS):
        field = gas_step(field, gas_rate)
    flat_out = field.reshape(species, -1)
    deposit = (cell_wts[None] * recv_source[:, None]).reshape(species, -1)
    flat_out = flat_out.at[:, cell_ids.reshape(-1)].add(deposit)
    return (flat_out.reshape(gas.shape), droplet_next)


def solution(mesh):
    return jax.shard_map(
        on_device,
        mesh=mesh,
        in_specs=(
            P(None, "gx", "gy", "gz"),
            P(None, None, ("gx", "gy", "gz")),
            P(("gx", "gy", "gz"), None),
            P(None, ("gx", "gy", "gz")),
            P(None, ("gx", "gy", "gz")),
            P(("gx", "gy", "gz")),
            P(),
            P(),
            P(),
        ),
        out_specs=(P(None, "gx", "gy", "gz"), P(None, None, ("gx", "gy", "gz"))),
        check_vma=False,
    )
```

profile of v0, /device:TPU:1, one launch (start us, length us, event | category | flops | bytes accessed | tf_op | source)
XLA Modules:
  0.0 177.2 jit_solution(17783845816552102356)
XLA Ops:
  0.6 0.8 fusion.54
  1.6 0.8 select_reduce_fusion
  4.6 0.9 scatter_custom_fusion.1
  6.4 7.3 %all-to-all-start.1 = ((f32[16,1,128]{2,1,0:T(1,128)}), f32[16,1,128]{2,1,0:T(1,128)S(1)}, u32[]{:S(2)}, u32[]{:S(2)}) async-start(f32[16,1,128]{2,1,0:T(1,128)} %reshape.270), calls=%async_computation.1 | async-start | bytes 16384 | tf_op jit(solution)/shard_map/all_to_all | solution.py:70
  13.7 1.8 %copy.48 = f32[64,4,8,128]{3,0,2,1:T(8,128)S(1)} copy(f32[64,4,8,128]{3,2,1,0:T(8,128)} %param.17) | data formatting | bytes 2097152 | tf_op args[0]
  15.6 1.0 fusion.70
  16.5 3.8 %collective-permute-start.1 = (f32[64,1,8,128]{3,0,2,1:T(8,128)}, f32[64,1,8,128]{3,0,2,1:T(8,128)}, u32[]{:S(2)}, u32[]{:S(2)}) collective-permute-start(f32[64,1,8,128]{3,0,2,1:T(8,128)} %get-tuple-element.83), channel_id=1, source_target_pairs={{0,16},{1,17},{2,18},{3,19},{4,20},{5,21},{6,22},{7,23},{8,24},{9,... | collective-permute-start | bytes 786440 | tf_op jit(solution)/shard_map/ppermute | solution.py:16
  20.3 1.3 collective-permute-start
  22.3 2.5 %fusion.65 = (f32[31,64,128]{1,2,0:T(8,128)}, f32[31,64,128]{1,2,0:T(8,128)}) fusion(f32[32,64,128]{1,2,0:T(8,128)S(1)} %copy.60), kind=kLoop, calls=%fused_computation.133 | loop fusion | bytes 4063232 | tf_op jit(solution)/shard_map/slice | solution.py:31
  24.9 0.9 scatter_custom_fusion
  26.6 6.3 %all-to-all-start = ((s32[16,1,128]{2,1,0:T(1,128)}), s32[16,1,128]{2,1,0:T(1,128)S(1)}, u32[]{:S(2)}, u32[]{:S(2)}) async-start(s32[16,1,128]{2,1,0:T(1,128)} %reshape.268), calls=%async_computation | async-start | bytes 16384 | tf_op jit(solution)/shard_map/all_to_all | solution.py:69
  32.9 2.0 %copy.62 = f32[64,4,8,128]{0,3,2,1:T(8,128)} copy(f32[64,4,8,128]{3,2,1,0:T(8,128)S(1)} %copy-done.2) | data formatting | bytes 2097152 | tf_op args[0]
  36.2 2.4 %all-to-all-done = s32[16,1,128]{2,1,0:T(1,128)S(1)} async-done(((s32[16,1,128]{2,1,0:T(1,128)}), s32[16,1,128]{2,1,0:T(1,128)S(1)}, u32[]{:S(2)}, u32[]{:S(2)}) %all-to-all-start) | async-done | bytes 8224 | tf_op jit(solution)/shard_map/all_to_all | solution.py:69
  40.0 9.2 %gather_fusion = f32[2048,64]{1,0:T(8,128)} fusion(f32[64,4096]{0,1:T(8,128)} %bitcast.109, s32[2048]{0:T(1024)S(1)} %broadcast_clamp_fusion), kind=kCustom, calls=%fused_computation | custom fusion | bytes 1056768 | tf_op jit(solution)/shard_map/gather | solution.py:71
  49.2 1.6 multiply_reduce_fusion
  50.8 0.8 reshape.272
  51.5 4.0 %all-to-all-start.2 = ((f32[16,1,1024]{2,1,0:T(1,128)}), f32[16,1,1024]{2,1,0:T(1,128)S(1)}, u32[]{:S(2)}, u32[]{:S(2)}) async-start(f32[16,1,1024]{2,1,0:T(1,128)} %reshape.272), calls=%async_computation.2 | async-start | bytes 131072 | tf_op jit(solution)/shard_map/all_to_all | solution.py:73
  55.6 4.2 %fusion.2 = f32[32,64,128]{1,2,0:T(8,128)} fusion(f32[32,64,128]{1,2,0:T(8,128)S(1)} %copy.60, f32[1,64,128]{1,2,0:T(8,128)S(1)} %get-tuple-element.69, f32[31,64,128]{1,2,0:T(8,128)} %get-tuple-element.71, f32[31,64,128]{1,2,0:T(8,128)} %get-tuple-element.70, f32[1,64,128]{1,2,0:T(8,128)S(1)} %get-tuple-element.68, f32[64]{0:T(128)S(1)} %copy-done.14), kind=kLoop, calls=%fused_computation.9 | loop fusion | flops 1835008 | bytes 4194560 | tf_op jit(solution)/shard_map/add | solution.py:32
  59.8 1.8 %all-to-all-done.2 = f32[16,1,1024]{2,1,0:T(1,128)S(1)} async-done(((f32[16,1,1024]{2,1,0:T(1,128)}), f32[16,1,1024]{2,1,0:T(1,128)S(1)}, u32[]{:S(2)}, u32[]{:S(2)}) %all-to-all-start.2) | async-done | bytes 65568 | tf_op jit(solution)/shard_map/all_to_all | solution.py:73
  61.7 0.8 reduce.10
  63.2 1.5 constant_dynamic-update-slice_fusion.5
  64.7 2.6 %fusion.63 = (f32[31,64,128]{1,2,0:T(8,128)S(1)}, f32[31,64,128]{1,2,0:T(8,128)S(1)}) fusion(f32[32,64,128]{1,2,0:T(8,128)} %get-tuple-element.60), kind=kLoop, calls=%fused_computation.131 | loop fusion | bytes 4063232 | tf_op jit(solution)/shard_map/slice | solution.py:31
  67.5 0.8 fusion.5
  68.9 1.0 constant_dynamic-update-slice_fusion.2
  70.5 1.0 constant_dynamic-update-slice_fusion
  71.5 1.3 collective-permute-start.2
  72.8 4.0 %collective-permute-start.3 = (f32[64,6,1,128]{3,0,2,1:T(8,128)S(1)}, f32[64,6,1,128]{3,0,2,1:T(8,128)S(1)}, u32[]{:S(2)}, u32[]{:S(2)}) collective-permute-start(f32[64,6,1,128]{3,0,2,1:T(8,128)S(1)} %get-tuple-element.78), channel_id=1, source_target_pairs={{0,4},{4,8},{8,12},{1,5},{5,9},{9,13},{2,6},{6,10},{10,14},{3,7},{... | collective-permute-start | bytes 589832 | tf_op jit(solution)/shard_map/ppermute | solution.py:16
  76.8 2.0 %fusion.8 = f32[32,64,128]{1,2,0:T(8,128)} fusion(f32[32,64,128]{1,2,0:T(8,128)S(1)} %get-tuple-element.58, f32[1,64,128]{1,2,0:T(8,128)S(1)} %get-tuple-element.59, f32[31,64,128]{1,2,0:T(8,128)S(1)} %get-tuple-element.65, f32[31,64,128]{1,2,0:T(8,128)S(1)} %get-tuple-element.64, f32[1,64,128]{1,2,0:T(8,128)S(1)} %slice.283, f32[64]{0:T(128)S(1)} %copy-done.14), kind=kLoop, calls=%fused_computation.17 | loop fusion | flops 1835008 | bytes 4194560 | tf_op jit(solution)/shard_map/add | solution.py:32
  78.8 0.9 collective-permute-done.3
  79.9 2.6 %fusion.67 = (f32[64,6,10,1]{3,0,2,1:T(8,128)}, f32[64,6,10,1]{3,0,2,1:T(8,128)}) fusion(f32[64,6,10,128]{3,0,2,1:T(8,128)S(1)} %pad_maximum_fusion), kind=kLoop, calls=%fused_computation.135 | loop fusion | bytes 61440 | tf_op jit(solution)/shard_map/slice | solution.py:19
  82.5 2.4 %copy.43 = f32[64,6,10,1]{0,1,3,2:T(8,128)S(1)} copy(f32[64,6,10,1]{3,0,2,1:T(8,128)} %get-tuple-element.74) | data formatting | bytes 30720 | tf_op jit(solution)/shard_map/slice | solution.py:19
  84.9 4.1 %collective-permute-start.4 = (f32[64,6,10,1]{0,1,3,2:T(8,128)S(1)}, f32[64,6,10,1]{0,1,3,2:T(8,128)S(1)}, u32[]{:S(2)}, u32[]{:S(2)}) collective-permute-start(f32[64,6,10,1]{0,1,3,2:T(8,128)S(1)} %copy.43), channel_id=1, source_target_pairs={{1,0},{2,1},{3,2},{5,4},{6,5},{7,6},{9,8},{10,9},{11,10},{13,12},{... | collective-permute-start | bytes 46088 | tf_op jit(solution)/shard_map/ppermute | solution.py:19
  89.0 2.4 %copy.45 = f32[64,6,10,1]{0,1,3,2:T(8,128)S(1)} copy(f32[64,6,10,1]{3,0,2,1:T(8,128)} %get-tuple-element.75) | data formatting | bytes 30720 | tf_op jit(solution)/shard_map/slice | solution.py:17
  91.4 2.2 %collective-permute-start.5 = (f32[64,6,10,1]{0,1,3,2:T(8,128)S(1)}, f32[64,6,10,1]{0,1,3,2:T(8,128)}, u32[]{:S(2)}, u32[]{:S(2)}) collective-permute-start(f32[64,6,10,1]{0,1,3,2:T(8,128)S(1)} %copy.45), channel_id=1, source_target_pairs={{0,1},{1,2},{2,3},{4,5},{5,6},{6,7},{8,9},{9,10},{10,11},{12,13},{... | collective-permute-start | bytes 46088 | tf_op jit(solution)/shard_map/ppermute | solution.py:16
  93.6 1.5 constant_dynamic-update-slice_fusion.3
  95.1 1.5 slice.287
  96.5 1.1 scatter_custom_fusion.2
  97.7 0.8 reshape.274
  98.4 5.3 %all-to-all-start.3 = ((f32[16,1,1024]{2,1,0:T(1,128)}), f32[16,1,1024]{2,1,0:T(1,128)}, u32[]{:S(2)}, u32[]{:S(2)}) async-start(f32[16,1,1024]{2,1,0:T(1,128)} %reshape.274), calls=%async_computation.3 | async-start | bytes 131072 | tf_op jit(solution)/shard_map/all_to_all | solution.py:80
  103.7 1.9 %copy.44 = f32[64,6,10,1]{3,0,2,1:T(8,128)} copy(f32[64,6,10,1]{0,1,3,2:T(8,128)S(1)} %collective-permute-done.4) | data formatting | bytes 30720 | tf_op jit(solution)/shard_map/ppermute | solution.py:19
  105.6 2.7 %copy.46 = f32[64,6,10,1]{3,0,2,1:T(8,128)} copy(f32[64,6,10,1]{0,1,3,2:T(8,128)} %collective-permute-done.5) | data formatting | bytes 30720 | tf_op jit(solution)/shard_map/ppermute | solution.py:16
  108.3 3.7 %fusion.23 = f32[64,4,8,128]{3,0,2,1:T(8,128)S(1)} fusion(f32[64,4,8,128]{3,0,2,1:T(8,128)} %copy-done.5, f32[64,6,10,1]{3,0,2,1:T(8,128)} %copy.46, f32[64,6,1,128]{3,0,2,1:T(8,128)S(1)} %collective-permute-done.2, f32[64,6,8,128]{3,0,2,1:T(8,128)S(1)} %copy-done.4, f32[64,6,1,128]{3,0,2,1:T(8,128)S(1)} %collective-permute-done.3, ...), kind=kLoop, calls=%fused_computation.54 | loop fusion | flops 4980736 | bytes 4618496 | tf_op jit(solution)/shard_map/add | solution.py:42
  112.1 1.3 collective-permute-start.6
  113.5 5.2 %collective-permute-start.7 = (f32[64,1,8,128]{3,0,2,1:T(8,128)S(1)}, f32[64,1,8,128]{3,0,2,1:T(8,128)S(1)}, u32[]{:S(2)}, u32[]{:S(2)}) collective-permute-start(f32[64,1,8,128]{3,0,2,1:T(8,128)S(1)} %get-tuple-element.80), channel_id=1, source_target_pairs={{0,16},{1,17},{2,18},{3,19},{4,20},{5,21},{6,22},{7,23},{8,24},{9,... | collective-permute-start | bytes 786440 | tf_op jit(solution)/shard_map/ppermute | solution.py:16
  119.3 3.8 %collective-permute-done.6 = f32[64,1,8,128]{3,0,2,1:T(8,128)S(1)} collective-permute-done((f32[64,1,8,128]{3,0,2,1:T(8,128)S(1)}, f32[64,1,8,128]{3,0,2,1:T(8,128)S(1)}, u32[]{:S(2)}, u32[]{:S(2)}) %collective-permute-start.6) | collective-permute-done | bytes 262176 | tf_op jit(solution)/shard_map/ppermute | solution.py:19
  123.1 1.0 collective-permute-done.7
  124.2 1.3 collective-permute-start.8
  125.5 4.0 %collective-permute-start.9 = (f32[64,6,1,128]{3,0,2,1:T(8,128)S(1)}, f32[64,6,1,128]{3,0,2,1:T(8,128)S(1)}, u32[]{:S(2)}, u32[]{:S(2)}) collective-permute-start(f32[64,6,1,128]{3,0,2,1:T(8,128)S(1)} %get-tuple-element.76), channel_id=1, source_target_pairs={{0,4},{4,8},{8,12},{1,5},{5,9},{9,13},{2,6},{6,10},{10,14},{3,7},{... | collective-permute-start | bytes 589832 | tf_op jit(solution)/shard_map/ppermute | solution.py:16
  130.2 1.3 collective-permute-done.8
  131.5 0.9 collective-permute-done.9
  132.5 2.6 %fusion.66 = (f32[64,6,10,1]{3,0,2,1:T(8,128)}, f32[64,6,10,1]{3,0,2,1:T(8,128)}) fusion(f32[64,6,10,128]{3,0,2,1:T(8,128)S(1)} %pad_maximum_fusion.1), kind=kLoop, calls=%fused_computation.134 | loop fusion | bytes 61440 | tf_op jit(solution)/shard_map/slice | solution.py:19
  135.1 3.0 %copy.49 = f32[64,6,10,1]{0,1,3,2:T(8,128)} copy(f32[64,6,10,1]{3,0,2,1:T(8,128)} %get-tuple-element.72) | data formatting | bytes 30720 | tf_op jit(solution)/shard_map/slice | solution.py:19
  138.1 4.1 %collective-permute-start.10 = (f32[64,6,10,1]{0,1,3,2:T(8,128)}, f32[64,6,10,1]{0,1,3,2:T(8,128)}, u32[]{:S(2)}, u32[]{:S(2)}) collective-permute-start(f32[64,6,10,1]{0,1,3,2:T(8,128)} %copy.49), channel_id=1, source_target_pairs={{1,0},{2,1},{3,2},{5,4},{6,5},{7,6},{9,8},{10,9},{11,10},{13,12},{... | collective-permute-start | bytes 46088 | tf_op jit(solution)/shard_map/ppermute | solution.py:19
  142.2 3.0 %copy.51 = f32[64,6,10,1]{0,1,3,2:T(8,128)} copy(f32[64,6,10,1]{3,0,2,1:T(8,128)} %get-tuple-element.73) | data formatting | bytes 30720 | tf_op jit(solution)/shard_map/slice | solution.py:17
  145.2 3.0 %collective-permute-start.11 = (f32[64,6,10,1]{0,1,3,2:T(8,128)}, f32[64,6,10,1]{0,1,3,2:T(8,128)}, u32[]{:S(2)}, u32[]{:S(2)}) collective-permute-start(f32[64,6,10,1]{0,1,3,2:T(8,128)} %copy.51), channel_id=1, source_target_pairs={{0,1},{1,2},{2,3},{4,5},{5,6},{6,7},{8,9},{9,10},{10,11},{12,13},{... | collective-permute-start | bytes 46088 | tf_op jit(solution)/shard_map/ppermute | solution.py:16
  148.8 1.6 copy.69
  150.4 1.6 reduce.11
  152.1 1.3 bitcast_multiply_fusion
  153.4 1.4 copy.50
  154.9 2.7 %copy.52 = f32[64,6,10,1]{3,0,2,1:T(8,128)} copy(f32[64,6,10,1]{0,1,3,2:T(8,128)} %collective-permute-done.11) | data formatting | bytes 30720 | tf_op jit(solution)/shard_map/ppermute | solution.py:16
  157.6 3.6 %fusion.15 = f32[64,4,8,128]{3,0,2,1:T(8,128)} fusion(f32[64,4,8,128]{3,0,2,1:T(8,128)S(1)} %fusion.23, f32[64,6,10,1]{3,0,2,1:T(8,128)} %copy.52, f32[64,6,1,128]{3,0,2,1:T(8,128)} %copy-done.9, f32[64,6,1,128]{3,0,2,1:T(8,128)} %copy-done.10, f32[64,1,8,128]{3,0,2,1:T(8,128)S(1)} %collective-permute-done.6, f32[64,1,8,128]{3,0,2,1:T(8,128)} %copy-done.7, ...), kind=kLoop, calls=%fused_computation.28 | loop fusion | flops 7077888 | bytes 3045632 | tf_op jit(solution)/shard_map/add | solution.py:42
  161.2 1.9 %copy.53 = f32[64,4,8,128]{0,3,2,1:T(8,128)S(1)} copy(f32[64,4,8,128]{3,0,2,1:T(8,128)} %fusion.15) | data formatting | bytes 2097152 | tf_op jit(solution)/shard_map/add | solution.py:42
  163.1 12.3 %scatter_custom_fusion.3 = f32[64,4096]{0,1:T(8,128)S(1)} fusion(f32[64,4096]{0,1:T(8,128)S(1)} %bitcast.110, s32[2048]{0:T(1024)S(1)} %bitcast.124, f32[64,2048]{0,1:T(8,128)S(1)} %copy-done.6), kind=kCustom, calls=%fused_computation.68 | custom fusion | flops 131072 | bytes 2097152 | tf_op jit(solution)/shard_map/scatter-add | solution.py:92
  175.4 1.8 copy.68
  (92 shorter events, 12.0 us)
Async XLA Ops:
  0.6 21.0 %copy-start.8 = (f32[32,64,128]{2,1,0:T(8,128)S(1)}, f32[32,64,128]{2,1,0:T(8,128)}, u32[]{:S(2)}) copy-start(f32[32,64,128]{2,1,0:T(8,128)} %param.18) | copy-start | bytes 3145732
  3.1 56.6 %copy-start.19 = (s32[128]{0:T(128)}, s32[128]{0:T(128)S(1)}, u32[]{:S(2)}) copy-start(s32[128]{0:T(128)S(1)} %fusion.59) | copy-start | bytes 1540
  6.4 20.2 %all-to-all-start.1 = ((f32[16,1,128]{2,1,0:T(1,128)}), f32[16,1,128]{2,1,0:T(1,128)S(1)}, u32[]{:S(2)}, u32[]{:S(2)}) async-start(f32[16,1,128]{2,1,0:T(1,128)} %reshape.270), calls=%async_computation.1 | async-start | bytes 16384 | tf_op jit(solution)/shard_map/all_to_all | solution.py:70
  15.5 4.8 %copy-start.5 = (f32[64,4,8,128]{3,0,2,1:T(8,128)}, f32[64,4,8,128]{3,0,2,1:T(8,128)S(1)}, u32[]{:S(2)}) copy-start(f32[64,4,8,128]{3,0,2,1:T(8,128)S(1)} %copy.48) | copy-start | bytes 3145732
  16.5 52.4 %collective-permute-start.1 = (f32[64,1,8,128]{3,0,2,1:T(8,128)}, f32[64,1,8,128]{3,0,2,1:T(8,128)}, u32[]{:S(2)}, u32[]{:S(2)}) collective-permute-start(f32[64,1,8,128]{3,0,2,1:T(8,128)} %get-tuple-element.83), channel_id=1, source_target_pairs={{0,16},{1,17},{2,18},{3,19},{4,20},{5,21},{6,22},{7,23},{8,24},{9,... | collective-permute-start | bytes 786440 | tf_op jit(solution)/shard_map/ppermute | solution.py:16
  20.3 50.1 %collective-permute-start = (f32[64,1,8,128]{3,0,2,1:T(8,128)}, f32[64,1,8,128]{3,0,2,1:T(8,128)}, u32[]{:S(2)}, u32[]{:S(2)}) collective-permute-start(f32[64,1,8,128]{3,0,2,1:T(8,128)} %get-tuple-element.82), channel_id=1, source_target_pairs={{16,0},{17,1},{18,2},{19,3},{20,4},{21,5},{22,6},{23,7},{24,8},{25... | collective-permute-start | bytes 786440 | tf_op jit(solution)/shard_map/ppermute | solution.py:19
  22.3 2.5 %copy-start.16 = (s32[8,128]{1,0:T(8,128)S(1)}, s32[8,128]{1,0:T(8,128)}, u32[]{:S(2)}) copy-start(s32[8,128]{1,0:T(8,128)} %param.20) | copy-start | bytes 12292
  22.3 10.6 %copy-start.2 = (f32[64,4,8,128]{3,2,1,0:T(8,128)S(1)}, f32[64,4,8,128]{3,2,1,0:T(8,128)}, u32[]{:S(2)}) copy-start(f32[64,4,8,128]{3,2,1,0:T(8,128)} %param.17) | copy-start | bytes 3145732
  26.6 12.0 %all-to-all-start = ((s32[16,1,128]{2,1,0:T(1,128)}), s32[16,1,128]{2,1,0:T(1,128)S(1)}, u32[]{:S(2)}, u32[]{:S(2)}) async-start(s32[16,1,128]{2,1,0:T(1,128)} %reshape.268), calls=%async_computation | async-start | bytes 16384 | tf_op jit(solution)/shard_map/all_to_all | solution.py:69
  40.0 15.6 %copy-start.14 = (f32[64]{0:T(128)S(1)}, f32[64]{0:T(128)}, u32[]{:S(2)}) copy-start(f32[64]{0:T(128)} %param.23) | copy-start | bytes 772
  51.5 10.1 %all-to-all-start.2 = ((f32[16,1,1024]{2,1,0:T(1,128)}), f32[16,1,1024]{2,1,0:T(1,128)S(1)}, u32[]{:S(2)}, u32[]{:S(2)}) async-start(f32[16,1,1024]{2,1,0:T(1,128)} %reshape.272), calls=%async_computation.2 | async-start | bytes 131072 | tf_op jit(solution)/shard_map/all_to_all | solution.py:73
  55.6 7.6 %copy-start.12 = (f32[64]{0:T(128)S(1)}, f32[64]{0:T(128)}, u32[]{:S(2)}) copy-start(f32[64]{0:T(128)} %param.24) | copy-start | bytes 772
  64.7 2.8 %copy-start.1 = (f32[32,64,128]{1,2,0:T(8,128)S(1)}, f32[32,64,128]{1,2,0:T(8,128)}, u32[]{:S(2)}) copy-start(f32[32,64,128]{1,2,0:T(8,128)} %get-tuple-element.60) | copy-start | bytes 3145732
  71.5 8.3 %copy-start.3 = (f32[64,6,8,128]{3,0,2,1:T(8,128)}, f32[64,6,8,128]{3,0,2,1:T(8,128)S(1)}, u32[]{:S(2)}) copy-start(f32[64,6,8,128]{3,0,2,1:T(8,128)S(1)} %constant_dynamic-update-slice_fusion) | copy-start | bytes 4718596
  71.5 7.3 %collective-permute-start.2 = (f32[64,6,1,128]{3,0,2,1:T(8,128)S(1)}, f32[64,6,1,128]{3,0,2,1:T(8,128)S(1)}, u32[]{:S(2)}, u32[]{:S(2)}) collective-permute-start(f32[64,6,1,128]{3,0,2,1:T(8,128)S(1)} %get-tuple-element.79), channel_id=1, source_target_pairs={{4,0},{8,4},{12,8},{5,1},{9,5},{13,9},{6,2},{10,6},{14,10},{7,3},{... | collective-permute-start | bytes 589832 | tf_op jit(solution)/shard_map/ppermute | solution.py:19
  72.8 6.9 %collective-permute-start.3 = (f32[64,6,1,128]{3,0,2,1:T(8,128)S(1)}, f32[64,6,1,128]{3,0,2,1:T(8,128)S(1)}, u32[]{:S(2)}, u32[]{:S(2)}) collective-permute-start(f32[64,6,1,128]{3,0,2,1:T(8,128)S(1)} %get-tuple-element.78), channel_id=1, source_target_pairs={{0,4},{4,8},{8,12},{1,5},{5,9},{9,13},{2,6},{6,10},{10,14},{3,7},{... | collective-permute-start | bytes 589832 | tf_op jit(solution)/shard_map/ppermute | solution.py:16
  82.5 11.1 %copy-start.13 = (f32[64]{0:T(128)S(1)}, f32[64]{0:T(128)}, u32[]{:S(2)}) copy-start(f32[64]{0:T(128)} %param.24) | copy-start | bytes 772
  82.5 14.0 %copy-start.20 = (f32[128]{0:T(128)S(1)}, f32[128]{0:T(128)}, u32[]{:S(2)}) copy-start(f32[128]{0:T(128)} %param.22) | copy-start | bytes 1540
  84.9 18.8 %collective-permute-start.4 = (f32[64,6,10,1]{0,1,3,2:T(8,128)S(1)}, f32[64,6,10,1]{0,1,3,2:T(8,128)S(1)}, u32[]{:S(2)}, u32[]{:S(2)}) collective-permute-start(f32[64,6,10,1]{0,1,3,2:T(8,128)S(1)} %copy.43), channel_id=1, source_target_pairs={{1,0},{2,1},{3,2},{5,4},{6,5},{7,6},{9,8},{10,9},{11,10},{13,12},{... | collective-permute-start | bytes 46088 | tf_op jit(solution)/shard_map/ppermute | solution.py:19
  91.4 14.2 %collective-permute-start.5 = (f32[64,6,10,1]{0,1,3,2:T(8,128)S(1)}, f32[64,6,10,1]{0,1,3,2:T(8,128)}, u32[]{:S(2)}, u32[]{:S(2)}) collective-permute-start(f32[64,6,10,1]{0,1,3,2:T(8,128)S(1)} %copy.45), channel_id=1, source_target_pairs={{0,1},{1,2},{2,3},{4,5},{5,6},{6,7},{8,9},{9,10},{10,11},{12,13},{... | collective-permute-start | bytes 46088 | tf_op jit(solution)/shard_map/ppermute | solution.py:16
  98.4 9.9 %copy-start.4 = (f32[64,6,8,128]{3,0,2,1:T(8,128)S(1)}, f32[64,6,8,128]{3,0,2,1:T(8,128)}, u32[]{:S(2)}) copy-start(f32[64,6,8,128]{3,0,2,1:T(8,128)} %copy-done.3) | copy-start | bytes 4718596
  98.4 9.9 %copy-start.17 = (f32[64]{0:T(128)S(1)}, f32[64]{0:T(128)}, u32[]{:S(2)}) copy-start(f32[64]{0:T(128)} %param.25) | copy-start | bytes 772
  98.4 52.0 %all-to-all-start.3 = ((f32[16,1,1024]{2,1,0:T(1,128)}), f32[16,1,1024]{2,1,0:T(1,128)}, u32[]{:S(2)}, u32[]{:S(2)}) async-start(f32[16,1,1024]{2,1,0:T(1,128)} %reshape.274), calls=%async_computation.3 | async-start | bytes 131072 | tf_op jit(solution)/shard_map/all_to_all | solution.py:80
  108.3 10.3 %copy-start = (f32[32,64,128]{1,2,0:T(8,128)S(1)}, f32[32,64,128]{1,2,0:T(8,128)}, u32[]{:S(2)}) copy-start(f32[32,64,128]{1,2,0:T(8,128)} %get-tuple-element.56) | copy-start | bytes 3145732
  112.1 11.0 %collective-permute-start.6 = (f32[64,1,8,128]{3,0,2,1:T(8,128)S(1)}, f32[64,1,8,128]{3,0,2,1:T(8,128)S(1)}, u32[]{:S(2)}, u32[]{:S(2)}) collective-permute-start(f32[64,1,8,128]{3,0,2,1:T(8,128)S(1)} %get-tuple-element.81), channel_id=1, source_target_pairs={{16,0},{17,1},{18,2},{19,3},{20,4},{21,5},{22,6},{23,7},{24,8},{25... | collective-permute-start | bytes 786440 | tf_op jit(solution)/shard_map/ppermute | solution.py:19
  113.4 16.1 %copy-start.11 = (f32[1,64,128]{1,2,0:T(8,128)S(1)}, f32[1,64,128]{1,2,0:T(8,128)}, u32[]{:S(2)}) copy-start(f32[1,64,128]{1,2,0:T(8,128)} %slice.287) | copy-start | bytes 98308
  113.5 16.1 %copy-start.15 = (f32[64]{0:T(128)S(1)}, f32[64]{0:T(128)}, u32[]{:S(2)}) copy-start(f32[64]{0:T(128)} %param.23) | copy-start | bytes 772
  113.5 10.7 %collective-permute-start.7 = (f32[64,1,8,128]{3,0,2,1:T(8,128)S(1)}, f32[64,1,8,128]{3,0,2,1:T(8,128)S(1)}, u32[]{:S(2)}, u32[]{:S(2)}) collective-permute-start(f32[64,1,8,128]{3,0,2,1:T(8,128)S(1)} %get-tuple-element.80), channel_id=1, source_target_pairs={{0,16},{1,17},{2,18},{3,19},{4,20},{5,21},{6,22},{7,23},{8,24},{9,... | collective-permute-start | bytes 786440 | tf_op jit(solution)/shard_map/ppermute | solution.py:16
  124.2 8.3 %copy-start.7 = (f32[64,1,8,128]{3,0,2,1:T(8,128)}, f32[64,1,8,128]{3,0,2,1:T(8,128)S(1)}, u32[]{:S(2)}) copy-start(f32[64,1,8,128]{3,0,2,1:T(8,128)S(1)} %collective-permute-done.7) | copy-start | bytes 786436
  124.2 7.3 %collective-permute-start.8 = (f32[64,6,1,128]{3,0,2,1:T(8,128)S(1)}, f32[64,6,1,128]{3,0,2,1:T(8,128)S(1)}, u32[]{:S(2)}, u32[]{:S(2)}) collective-permute-start(f32[64,6,1,128]{3,0,2,1:T(8,128)S(1)} %get-tuple-element.77), channel_id=1, source_target_pairs={{4,0},{8,4},{12,8},{5,1},{9,5},{13,9},{6,2},{10,6},{14,10},{7,3},{... | collective-permute-start | bytes 589832 | tf_op jit(solution)/shard_map/ppermute | solution.py:19
  125.5 6.9 %collective-permute-start.9 = (f32[64,6,1,128]{3,0,2,1:T(8,128)S(1)}, f32[64,6,1,128]{3,0,2,1:T(8,128)S(1)}, u32[]{:S(2)}, u32[]{:S(2)}) collective-permute-start(f32[64,6,1,128]{3,0,2,1:T(8,128)S(1)} %get-tuple-element.76), channel_id=1, source_target_pairs={{0,4},{4,8},{8,12},{1,5},{5,9},{9,13},{2,6},{6,10},{10,14},{3,7},{... | collective-permute-start | bytes 589832 | tf_op jit(solution)/shard_map/ppermute | solution.py:16
  131.5 3.6 %copy-start.9 = (f32[64,6,1,128]{3,0,2,1:T(8,128)}, f32[64,6,1,128]{3,0,2,1:T(8,128)S(1)}, u32[]{:S(2)}) copy-start(f32[64,6,1,128]{3,0,2,1:T(8,128)S(1)} %collective-permute-done.8) | copy-start | bytes 589828
  132.4 2.7 %copy-start.10 = (f32[64,6,1,128]{3,0,2,1:T(8,128)}, f32[64,6,1,128]{3,0,2,1:T(8,128)S(1)}, u32[]{:S(2)}) copy-start(f32[64,6,1,128]{3,0,2,1:T(8,128)S(1)} %collective-permute-done.9) | copy-start | bytes 589828
  138.1 15.3 %collective-permute-start.10 = (f32[64,6,10,1]{0,1,3,2:T(8,128)}, f32[64,6,10,1]{0,1,3,2:T(8,128)}, u32[]{:S(2)}, u32[]{:S(2)}) collective-permute-start(f32[64,6,10,1]{0,1,3,2:T(8,128)} %copy.49), channel_id=1, source_target_pairs={{1,0},{2,1},{3,2},{5,4},{6,5},{7,6},{9,8},{10,9},{11,10},{13,12},{... | collective-permute-start | bytes 46088 | tf_op jit(solution)/shard_map/ppermute | solution.py:19
  145.2 9.7 %collective-permute-start.11 = (f32[64,6,10,1]{0,1,3,2:T(8,128)}, f32[64,6,10,1]{0,1,3,2:T(8,128)}, u32[]{:S(2)}, u32[]{:S(2)}) collective-permute-start(f32[64,6,10,1]{0,1,3,2:T(8,128)} %copy.51), channel_id=1, source_target_pairs={{0,1},{1,2},{2,3},{4,5},{5,6},{6,7},{8,9},{9,10},{10,11},{12,13},{... | collective-permute-start | bytes 46088 | tf_op jit(solution)/shard_map/ppermute | solution.py:16
  153.4 4.2 %copy-start.18 = (f32[64]{0:T(128)S(1)}, f32[64]{0:T(128)}, u32[]{:S(2)}) copy-start(f32[64]{0:T(128)} %param.25) | copy-start | bytes 772
  161.2 1.9 %copy-start.6 = (f32[64,2048]{0,1:T(8,128)S(1)}, f32[64,2048]{0,1:T(8,128)}, u32[]{:S(2)}) copy-start(f32[64,2048]{0,1:T(8,128)} %bitcast_multiply_fusion) | copy-start | bytes 1572868
where the time goes:
time: 180 us; the launch traced here: 177 us
  local copies, waits for them, and re-layouts  62.6 us (35%)
  starting transfers between devices  58.4 us (32%)
  other arithmetic  42.8 us (24%)
  waiting for transfers between devices  12.2 us (7%)
    ppermute x6, starting transfers between devices, with_halo(): lax.ppermute(lax.slice_in_dim(block, block.shape[dim] - width, None, axis...  22.2 us
    ppermute x6, starting transfers between devices, with_halo(): lax.ppermute(lax.slice_in_dim(block, 0, width, axis=dim), axis, backward)  13.3 us
    unnamed x58, local copies, waits for them, and re-layouts  13 us
    scatter-add x1, other arithmetic, on_device(): flat_out = flat_out.at[:, cell_ids.reshape(-1)].add(deposit)  12.3 us
    slice x5, local copies, waits for them, and re-layouts, with_halo(): lax.slice_in_dim(block, 0, width, axis=dim)  11.6 us
    gather x1, local copies, waits for them, and re-layouts, on_device(): gasflat[:, cell_ids.reshape(-1)].reshape((species,) + cell_ids.shape)  9.23 us
    slice x8, local copies, waits for them, and re-layouts, droplet_steps(): lower_node = jnp.concatenate([state[1:2], state[:-1]], axis=0)  7.7 us
    add x4, other arithmetic, droplet_steps(): state = state + liquid_coef * (upper_node - 2.0 * state + lower_node)  7.67 us
  transfers between devices with their start and end apart: 16, of which 7 were waited for; matrix products, arithmetic and copies ran while one was open for 40% of the time, Pallas kernels for 0%

commit v1 on v0

v1 whole, which is shorter than its diff:
```python
import functools

import jax
import jax.numpy as jnp
from jax import lax
from jax.experimental import pallas as pl
from jax.experimental.pallas import tpu as pltpu
from jax.sharding import PartitionSpec as P

STENCIL = 8
DROP_STEPS = 4
GAS_STEPS = 2
LANES = 128
MIB = 1 << 20
NT = (((1,), (1,)), ((), ()))
HIGH = lax.Precision.HIGHEST
F32 = jnp.float32
BF16 = jnp.bfloat16


def iota(shape, dim):
    return lax.broadcasted_iota(jnp.int32, shape, dim)


def as_column(row):
    n = row.shape[1]
    return jnp.sum(jnp.where(iota((n, n), 0) == iota((n, n), 1), row, 0.0), axis=1, keepdims=True)


def split(value):
    scaled = value * 65537.0
    high = scaled - (scaled - value)
    return high.astype(BF16), (value - high).astype(BF16)


def surface_steps(nodes, gas_at, liquid, surface):
    emitted = None
    for step in range(DROP_STEPS):
        last = nodes[-1]
        flux = surface * (last - gas_at)
        emitted = flux if emitted is None else emitted + flux
        inner = [
            nodes[i] + liquid * (nodes[i + 1] - 2.0 * nodes[i] + nodes[i - 1])
            for i in range(1, len(nodes) - 1)
        ]
        if len(nodes) > 1:
            nodes = inner + [last + liquid * (nodes[-2] - last) - flux]
    return emitted


def surface_response(liquid, surface):
    zero = jnp.zeros_like(liquid)
    nodes = [zero] * (DROP_STEPS + 1)
    emitted = zero
    for step in range(DROP_STEPS):
        last = nodes[-1]
        flux = surface * (last - 1.0)
        emitted = emitted + flux
        inner = [
            nodes[i] + liquid * (nodes[i + 1] - 2.0 * nodes[i] + nodes[i - 1])
            for i in range(1, DROP_STEPS)
        ]
        nodes = [zero] + inner + [last + liquid * (nodes[-2] - last) - flux]
    return emitted, nodes[1:]


def pack_kernel(cap, tail, owner, cells, weights, mass, liquid, surface, send, slots):
    parcels = owner.shape[1]
    emitted = surface_steps(
        [tail[i] for i in range(DROP_STEPS)], 0.0, as_column(liquid[...]), as_column(surface[...])
    )
    wts = weights[...]
    norm = wts / jnp.sum(wts, axis=0, keepdims=True)
    mine = owner[...]
    column = jnp.transpose(jnp.broadcast_to(mine.astype(F32), (parcels, parcels)))
    earlier = (column == mine.astype(F32)) & (iota((parcels, parcels), 0) < iota((parcels, parcels), 1))
    rank = jnp.sum(jnp.where(earlier, 1.0, 0.0), axis=0, keepdims=True).astype(jnp.int32)
    slot = mine * cap + rank
    slots[...] = slot
    species = tail.shape[1]
    rest = jnp.zeros((LANES - species - 2 * STENCIL - 8, parcels), F32)
    values = jnp.concatenate(
        [
            mass[...] * emitted,
            cells[...].astype(F32),
            norm,
            jnp.broadcast_to(mass[...], (8, parcels)),
            rest,
        ],
        axis=0,
    )
    place = jnp.where(iota((send.shape[0], parcels), 0) == slot, 1.0, 0.0)
    send[...] = lax.dot_general(place, values, NT, precision=HIGH, preferred_element_type=F32)


def couple_kernel(cap, packed, rows, gas, liquid, surface, back, deposit, w_high, w_low, t_all):
    slots = rows.shape[0]
    species = liquid.shape[1]
    lines = gas.shape[0] // species
    table = jnp.transpose(rows[...])
    first = species
    cell = table[first : first + STENCIL]
    wts = table[first + STENCIL : first + 2 * STENCIL]
    mass = table[first + 2 * STENCIL : first + 2 * STENCIL + 1]
    cell_rows = [cell[k : k + 1] for k in range(STENCIL)]
    wts_rows = [wts[k : k + 1] for k in range(STENCIL)]
    whole = []
    for k in range(STENCIL):
        total = wts_rows[k]
        for other in range(STENCIL):
            if other != k:
                total = total + jnp.where(cell_rows[other] == cell_rows[k], wts_rows[other], 0.0)
        whole.append(total)
    line_of = jnp.floor(cell * (1.0 / LANES))
    lane_of = cell - LANES * line_of
    along = iota((LANES, slots), 0).astype(F32).astype(BF16)
    halves = [split(w) for w in whole]
    highs = [jnp.broadcast_to(h, (LANES, slots)) for h, _ in halves]
    lows = [jnp.broadcast_to(l, (LANES, slots)) for _, l in halves]

    @pl.loop(0, lines)
    def _(line):
        code = jnp.where(line_of == line.astype(F32), lane_of, -1.0).astype(BF16)
        high = jnp.zeros((LANES, slots), BF16)
        low = jnp.zeros((LANES, slots), BF16)
        for k in range(STENCIL):
            hit = jnp.broadcast_to(code[k : k + 1], (LANES, slots)) == along
            high = jnp.where(hit, highs[k], high)
            low = jnp.where(hit, lows[k], low)
        w_high[line] = high
        w_low[line] = low
        t_high, t_low = split(gas[pl.ds(line, species, stride=lines), :])
        t_all[line] = jnp.concatenate([t_high, t_low], axis=0)

    gathered = jnp.zeros((species, slots), F32)
    for line in range(lines):
        both = jnp.dot(t_all[line], w_high[line], preferred_element_type=F32)
        extra = jnp.dot(t_all[line, :species], w_low[line], preferred_element_type=F32)
        gathered = gathered + both[:species] + both[species:] + extra
    gas_rows = jnp.transpose(gathered)
    if packed:
        gas_rows = gas_rows.reshape(slots // cap, cap, species)
        gas_rows = jnp.concatenate([gas_rows[:, : cap // 2], gas_rows[:, cap // 2 :]], axis=2)
        back[...] = gas_rows.reshape(slots // 2, 2 * species)
    else:
        back[...] = jnp.concatenate([gas_rows, jnp.zeros((slots, LANES - species), F32)], axis=1)
    response, _ = surface_response(as_column(liquid[...]), as_column(surface[...]))
    source = table[:species] + mass * (response * gathered)
    s_high, s_low = split(source)
    s_all = jnp.concatenate([s_high, s_low], axis=0)
    for line in range(lines):
        both = lax.dot_general(s_all, w_high[line], NT, preferred_element_type=F32)
        extra = lax.dot_general(s_high, w_low[line], NT, preferred_element_type=F32)
        deposit[pl.ds(line, species, stride=lines), :] = both[:species] + both[species:] + extra


def droplet_kernel(state_in, liquid, surface, state_out):
    nodes, block, _ = state_in.shape
    species = liquid.shape[1]
    at = pl.program_id(0) * block + iota((block, species), 0)
    pick = at == iota((block, species), 1)
    liquid_col = jnp.sum(jnp.where(pick, liquid[...], 0.0), axis=1, keepdims=True)
    surface_col = jnp.sum(jnp.where(pick, surface[...], 0.0), axis=1, keepdims=True)
    state = state_in[...]
    for step in range(DROP_STEPS):
        upper = jnp.concatenate([state[1:], state[-1:]], axis=0)
        lower = jnp.concatenate([state[1:2], state[:-1]], axis=0)
        flux = surface_col * state[-1]
        state = state + liquid_col * (upper - 2.0 * state + lower)
        state = jnp.concatenate([state[:-1], (state[-1] - flux)[None]], axis=0)
    state_out[...] = state


def finish_kernel(cap, packed, tail, rows, slots, liquid, surface, out):
    species = liquid.shape[1]
    table = jnp.transpose(rows[...])
    count = rows.shape[0]
    parcels = slots.shape[1]
    at = iota((count, parcels), 0)
    slot = slots[...]
    if packed:
        half = cap // 2
        at = at // half * cap + at % half
        parts = [(table[:species], at), (table[species:], at + half)]
    else:
        parts = [(table[:species], at)]
    gas_at = jnp.zeros((species, parcels), F32)
    for values, index in parts:
        place = jnp.where(index == slot, 1.0, 0.0)
        gas_at = gas_at + jnp.dot(values, place, precision=HIGH, preferred_element_type=F32)
    _, response = surface_response(as_column(liquid[...]), as_column(surface[...]))
    for i in range(DROP_STEPS):
        out[i] = tail[i] + response[i] * gas_at


def with_halo(block, sides, width):
    for axis, dim in sides:
        count = lax.axis_size(axis)
        forward = [(i, i + 1) for i in range(count - 1)]
        backward = [(target, source) for source, target in forward]
        low = lax.ppermute(
            lax.slice_in_dim(block, block.shape[dim] - width, None, axis=dim), axis, forward
        )
        high = lax.ppermute(lax.slice_in_dim(block, 0, width, axis=dim), axis, backward)
        block = jnp.concatenate([low, block, high], axis=dim)
    return block


def stencil_update(padded, field, gas_rate):
    beside = padded[:, 2:, 1:-1, 1:-1] + padded[:, :-2, 1:-1, 1:-1]
    beside = beside + padded[:, 1:-1, 2:, 1:-1] + padded[:, 1:-1, :-2, 1:-1]
    beside = beside + padded[:, 1:-1, 1:-1, 2:] + padded[:, 1:-1, 1:-1, :-2]
    return field + gas_rate[:, None, None, None] * (beside - 6.0 * field)


def gas_step(field, gas_rate):
    padded = with_halo(field, (("gx", 1), ("gy", 2), ("gz", 3)), 1)
    return stencil_update(padded, field, gas_rate)


def full(shape):
    return pl.BlockSpec(shape, lambda *_: (0,) * len(shape))


def exchange(rows, group):
    width = rows.shape[1]
    chunks = rows.reshape(group, -1, width)
    chunks = lax.all_to_all(chunks, ("gy", "gz"), split_axis=0, concat_axis=0, tiled=True)
    return chunks.reshape(-1, width)


def on_device(gas, droplet, owner, cells, weights, mass, liquid_rate, surface_rate, gas_rate):
    group = lax.axis_size("gy") * lax.axis_size("gz")
    nodes, species, parcels = droplet.shape
    cap = 2 * parcels // group
    slots = group * cap
    packed = cap % 16 == 0
    lines = gas.shape[1] * gas.shape[2]
    flat = gas.reshape(species * lines, LANES)
    liquid = liquid_rate.reshape(1, species)
    surface = surface_rate.reshape(1, species)
    tail_block = nodes // DROP_STEPS - 1
    tail_spec = pl.BlockSpec((DROP_STEPS, species, parcels), lambda *_: (tail_block, 0, 0))
    rate_spec = full((1, species))

    send, slot = pl.pallas_call(
        functools.partial(pack_kernel, cap),
        grid=(1,),
        out_shape=(
            jax.ShapeDtypeStruct((slots, LANES), F32),
            jax.ShapeDtypeStruct((1, parcels), jnp.int32),
        ),
        in_specs=[
            tail_spec,
            full((1, parcels)),
            full((STENCIL, parcels)),
            full((STENCIL, parcels)),
            full((1, parcels)),
            rate_spec,
            rate_spec,
        ],
        out_specs=(full((slots, LANES)), full((1, parcels))),
        compiler_params=pltpu.CompilerParams(vmem_limit_bytes=16 * MIB),
        name="pack_parcels",
    )(droplet, owner.reshape(1, parcels), cells, weights, mass.reshape(1, parcels), liquid, surface)

    rows = exchange(send, group)

    back_rows = slots // 2 if packed else slots
    back, deposit = pl.pallas_call(
        functools.partial(couple_kernel, cap, packed),
        out_shape=(
            jax.ShapeDtypeStruct((back_rows, LANES), F32),
            jax.ShapeDtypeStruct((species * lines, LANES), F32),
        ),
        scratch_shapes=[
            pltpu.VMEM((lines, LANES, slots), BF16),
            pltpu.VMEM((lines, LANES, slots), BF16),
            pltpu.VMEM((lines, 2 * species, LANES), BF16),
        ],
        compiler_params=pltpu.CompilerParams(vmem_limit_bytes=32 * MIB),
        name="couple_gas",
    )(rows, flat, liquid, surface)

    returned = exchange(back, group)

    block = 16
    drop_spec = pl.BlockSpec((nodes, block, parcels), lambda i: (0, i, 0))
    evolved = pl.pallas_call(
        droplet_kernel,
        grid=(species // block,),
        out_shape=jax.ShapeDtypeStruct(droplet.shape, F32),
        in_specs=[drop_spec, rate_spec, rate_spec],
        out_specs=drop_spec,
        compiler_params=pltpu.CompilerParams(vmem_limit_bytes=16 * MIB),
        cost_estimate=pl.CostEstimate(flops=20 * droplet.size, bytes_accessed=8 * droplet.size, transcendentals=0),
        name="evolve_droplets",
    )(droplet, liquid, surface)

    droplet_next = pl.pallas_call(
        functools.partial(finish_kernel, cap, packed),
        grid=(1,),
        out_shape=jax.ShapeDtypeStruct(droplet.shape, F32),
        in_specs=[tail_spec, full((back_rows, LANES)), full((1, parcels)), rate_spec, rate_spec],
        out_specs=tail_spec,
        input_output_aliases={0: 0},
        compiler_params=pltpu.CompilerParams(vmem_limit_bytes=16 * MIB),
        name="finish_droplets",
    )(evolved, returned, slot, liquid, surface)

    field = gas
    for substep in range(GAS_STEPS):
        field = gas_step(field, gas_rate)
    return (field + deposit.reshape(gas.shape), droplet_next)


def solution(mesh):
    return jax.shard_map(
        on_device,
        mesh=mesh,
        in_specs=(
            P(None, "gx", "gy", "gz"),
            P(None, None, ("gx", "gy", "gz")),
            P(("gx", "gy", "gz"), None),
            P(None, ("gx", "gy", "gz")),
            P(None, ("gx", "gy", "gz")),
            P(("gx", "gy", "gz")),
            P(),
            P(),
            P(),
        ),
        out_specs=(P(None, "gx", "gy", "gz"), P(None, None, ("gx", "gy", "gz"))),
        check_vma=False,
    )
```

time: 180 us -> 113 us (0.63); the launches traced: 177 us -> 113 us
  local copies, waits for them, and re-layouts: 62.6 us -> 27.1 us
  other arithmetic: 42.8 us -> 12 us
  Pallas kernels: 0 us -> 13.6 us
  starting transfers between devices: 58.4 us -> 49.7 us
  waiting for transfers between devices: 12.2 us -> 9.4 us
    scatter-add x5 -> x0, other arithmetic: 16 us -> none  [the longest x1 12.3 us: on_device(): flat_out = flat_out.at[:, cell_ids.reshape(-1)].add(deposit)]
    pallas_call x0 -> x4, Pallas kernels: none -> 13.6 us  [the longest x1 8.21 us: on_device(): pl.pallas_call(functools.partial(couple_kernel, cap, packed), out_shape=(...]
    gather x2 -> x0, local copies, waits for them, and re-layouts: 9.87 us -> none  [the longest x1 9.23 us: on_device(): gasflat[:, cell_ids.reshape(-1)].reshape((species,) + cell_ids.shape)]
    all_to_all x4 -> x2, starting transfers between devices: 22.9 us -> 13.3 us  [exchange(): lax.all_to_all(chunks, ('gy', 'gz'), split_axis=0, concat_axis=0, tiled=T...]
    unnamed x58 -> x36, local copies, waits for them, and re-layouts: 13 us -> 4.89 us
    slice x8 -> x0, local copies, waits for them, and re-layouts: 7.7 us -> none  [droplet_steps(): lower_node = jnp.concatenate([state[1:2], state[:-1]], axis=0)]
    add x4 -> x1, other arithmetic: 7.67 us -> 3.14 us  [on_device(): return (field + deposit.reshape(gas.shape), droplet_next)]
    all_to_all x4 -> x2, waiting for transfers between devices: 4.23 us -> 0.01 us  [exchange(): lax.all_to_all(chunks, ('gy', 'gz'), split_axis=0, concat_axis=0, tiled=T...]
  transfers between devices with their start and end apart: 16 -> 14, of which waited for: 7 -> 4; matrix products, arithmetic and copies ran while one was open for 40% -> 14% of each run, Pallas kernels for 0% -> 12%
where the time goes in v1:
time: 113 us
  starting transfers between devices  49.7 us (44%)
  local copies, waits for them, and re-layouts  27.1 us (24%)
  Pallas kernels  13.6 us (12%)
  other arithmetic  12 us (11%)
  waiting for transfers between devices  9.4 us (8%)
    ppermute x6, starting transfers between devices, with_halo(): lax.ppermute(lax.slice_in_dim(block, block.shape[dim] - width, None, axis...  24.3 us
    all_to_all x2, starting transfers between devices, exchange(): lax.all_to_all(chunks, ('gy', 'gz'), split_axis=0, concat_axis=0, tiled=T...  13.3 us
    ppermute x6, starting transfers between devices, with_halo(): lax.ppermute(lax.slice_in_dim(block, 0, width, axis=dim), axis, backward)  12.1 us
    slice x5, local copies, waits for them, and re-layouts, with_halo(): lax.slice_in_dim(block, 0, width, axis=dim)  9.45 us
    pallas_call x1, Pallas kernels, on_device(): pl.pallas_call(functools.partial(couple_kernel, cap, packed), out_shape=(...  8.21 us
    add x1, other arithmetic, stencil_update(): return field + gas_rate[:, None, None, None] * (beside - 6.0 * field)  5.25 us
    ppermute x6, waiting for transfers between devices, with_halo(): lax.ppermute(lax.slice_in_dim(block, block.shape[dim] - width, None, axis...  5.11 us
    unnamed x36, local copies, waits for them, and re-layouts  4.89 us
  transfers between devices with their start and end apart: 14, of which 4 were waited for; matrix products, arithmetic and copies ran while one was open for 14% of the time, Pallas kernels for 12%

profile of v1, /device:TPU:1, one launch (start us, length us, event | category | flops | bytes accessed | tf_op | source)
XLA Modules:
  0.0 112.6 jit_solution(4226803346365916981)
XLA Ops:
  0.6 1.9 %copy.22 = f32[64,4,8,128]{3,0,2,1:T(8,128)S(1)} copy(f32[64,4,8,128]{3,2,1,0:T(8,128)} %param.9) | data formatting | bytes 2097152 | tf_op args[0]
  2.6 0.0 copy-start.11
  2.6 4.0 %collective-permute-start.1 = (f32[64,1,8,128]{3,0,2,1:T(8,128)S(1)}, f32[64,1,8,128]{3,0,2,1:T(8,128)S(1)}, u32[]{:S(2)}, u32[]{:S(2)}) collective-permute-start(f32[64,1,8,128]{3,0,2,1:T(8,128)S(1)} %get-tuple-element.23), channel_id=1, source_target_pairs={{0,16},{1,17},{2,18},{3,19},{4,20},{5,21},{6,22},{7,23},{8,24},{9,... | collective-permute-start | bytes 786440 | tf_op jit(solution)/shard_map/ppermute | solution.py:201
  6.6 1.3 %collective-permute-start = (f32[64,1,8,128]{3,0,2,1:T(8,128)S(1)}, f32[64,1,8,128]{3,0,2,1:T(8,128)S(1)}, u32[]{:S(2)}, u32[]{:S(2)}) collective-permute-start(f32[64,1,8,128]{3,0,2,1:T(8,128)S(1)} %get-tuple-element.22), channel_id=1, source_target_pairs={{16,0},{17,1},{18,2},{19,3},{20,4},{21,5},{22,6},{23,7},{24,8},{25... | collective-permute-start | bytes 786440 | tf_op jit(solution)/shard_map/ppermute | solution.py:204
  7.9 3.6 %collective-permute-done.1 = f32[64,1,8,128]{3,0,2,1:T(8,128)S(1)} collective-permute-done((f32[64,1,8,128]{3,0,2,1:T(8,128)S(1)}, f32[64,1,8,128]{3,0,2,1:T(8,128)S(1)}, u32[]{:S(2)}, u32[]{:S(2)}) %collective-permute-start.1) | collective-permute-done | bytes 262176 | tf_op jit(solution)/shard_map/ppermute | solution.py:201
  11.6 0.6 constant_dynamic-update-slice_fusion.1
  12.2 3.2 %collective-permute-done = f32[64,1,8,128]{3,0,2,1:T(8,128)S(1)} collective-permute-done((f32[64,1,8,128]{3,0,2,1:T(8,128)S(1)}, f32[64,1,8,128]{3,0,2,1:T(8,128)S(1)}, u32[]{:S(2)}, u32[]{:S(2)}) %collective-permute-start) | collective-permute-done | bytes 262176 | tf_op jit(solution)/shard_map/ppermute | solution.py:204
  15.4 1.3 %collective-permute-start.2 = (f32[64,6,1,128]{3,0,2,1:T(8,128)S(1)}, f32[64,6,1,128]{3,0,2,1:T(8,128)S(1)}, u32[]{:S(2)}, u32[]{:S(2)}) collective-permute-start(f32[64,6,1,128]{3,0,2,1:T(8,128)S(1)} %get-tuple-element.19), channel_id=1, source_target_pairs={{4,0},{8,4},{12,8},{5,1},{9,5},{13,9},{6,2},{10,6},{14,10},{7,3},{... | collective-permute-start | bytes 589832 | tf_op jit(solution)/shard_map/ppermute | solution.py:204
  16.7 4.0 %collective-permute-start.3 = (f32[64,6,1,128]{3,0,2,1:T(8,128)S(1)}, f32[64,6,1,128]{3,0,2,1:T(8,128)S(1)}, u32[]{:S(2)}, u32[]{:S(2)}) collective-permute-start(f32[64,6,1,128]{3,0,2,1:T(8,128)S(1)} %get-tuple-element.18), channel_id=1, source_target_pairs={{0,4},{4,8},{8,12},{1,5},{5,9},{9,13},{2,6},{6,10},{10,14},{3,7},{... | collective-permute-start | bytes 589832 | tf_op jit(solution)/shard_map/ppermute | solution.py:201
  20.7 1.1 collective-permute-done.2
  21.8 1.5 %collective-permute-done.3 = f32[64,6,1,128]{3,0,2,1:T(8,128)S(1)} collective-permute-done((f32[64,6,1,128]{3,0,2,1:T(8,128)S(1)}, f32[64,6,1,128]{3,0,2,1:T(8,128)S(1)}, u32[]{:S(2)}, u32[]{:S(2)}) %collective-permute-start.3) | collective-permute-done | bytes 196640 | tf_op jit(solution)/shard_map/ppermute | solution.py:201
  23.3 0.7 copy-done.14
  24.0 0.1 pad_maximum_fusion
  24.1 2.0 %fusion.18 = (f32[64,6,10,1]{3,0,2,1:T(8,128)}, f32[64,6,10,1]{3,0,2,1:T(8,128)S(1)}) fusion(f32[64,6,10,128]{3,0,2,1:T(8,128)S(1)} %pad_maximum_fusion), kind=kLoop, calls=%fused_computation.54 | loop fusion | bytes 61440 | tf_op jit(solution)/shard_map/slice | solution.py:204
  26.2 2.4 %copy.17 = f32[64,6,10,1]{0,1,3,2:T(8,128)S(1)} copy(f32[64,6,10,1]{3,0,2,1:T(8,128)} %get-tuple-element.14) | data formatting | bytes 30720 | tf_op jit(solution)/shard_map/slice | solution.py:204
  28.5 4.9 %collective-permute-start.4 = (f32[64,6,10,1]{0,1,3,2:T(8,128)S(1)}, f32[64,6,10,1]{0,1,3,2:T(8,128)S(1)}, u32[]{:S(2)}, u32[]{:S(2)}) collective-permute-start(f32[64,6,10,1]{0,1,3,2:T(8,128)S(1)} %copy.17), channel_id=1, source_target_pairs={{1,0},{2,1},{3,2},{5,4},{6,5},{7,6},{9,8},{10,9},{11,10},{13,12},{... | collective-permute-start | bytes 46088 | tf_op jit(solution)/shard_map/ppermute | solution.py:204
  33.5 0.8 copy.19
  34.3 3.2 %collective-permute-start.5 = (f32[64,6,10,1]{0,1,3,2:T(8,128)S(1)}, f32[64,6,10,1]{0,1,3,2:T(8,128)S(1)}, u32[]{:S(2)}, u32[]{:S(2)}) collective-permute-start(f32[64,6,10,1]{0,1,3,2:T(8,128)S(1)} %copy.19), channel_id=1, source_target_pairs={{0,1},{1,2},{2,3},{4,5},{5,6},{6,7},{8,9},{9,10},{10,11},{12,13},{... | collective-permute-start | bytes 46088 | tf_op jit(solution)/shard_map/ppermute | solution.py:201
  37.5 0.0 collective-permute-done.4
  37.5 1.9 %copy.18 = f32[64,6,10,1]{3,0,2,1:T(8,128)} copy(f32[64,6,10,1]{0,1,3,2:T(8,128)S(1)} %collective-permute-done.4) | data formatting | bytes 30720 | tf_op jit(solution)/shard_map/ppermute | solution.py:204
  39.4 0.0 collective-permute-done.5
  39.4 2.0 %copy.20 = f32[64,6,10,1]{3,0,2,1:T(8,128)} copy(f32[64,6,10,1]{0,1,3,2:T(8,128)S(1)} %collective-permute-done.5) | data formatting | bytes 30720 | tf_op jit(solution)/shard_map/ppermute | solution.py:201
  41.4 0.0 copy-done.15
  41.4 0.0 copy-start.4
  41.4 0.0 copy-start.5
  41.4 0.0 copy-start.6
  41.4 0.0 copy-start.7
  41.4 5.3 %fusion.12 = f32[64,4,8,128]{3,0,2,1:T(8,128)S(1)} fusion(f32[64,4,8,128]{3,0,2,1:T(8,128)} %copy-done.11, f32[64,6,10,1]{3,0,2,1:T(8,128)} %copy.20, f32[64,6,1,128]{3,0,2,1:T(8,128)} %copy-done.13, f32[64,6,8,128]{3,0,2,1:T(8,128)} %copy-done.10, f32[64,6,1,128]{3,0,2,1:T(8,128)} %copy-done.14, f32[64,6,10,1]{3,0,2,1:T(8,128)} %copy.18, ...), kind=kLoop, calls=%fused_computation.33 | loop fusion | flops 4980736 | bytes 4618496 | tf_op jit(solution)/shard_map/add | solution.py:213
  46.7 0.0 copy-start.8
  46.7 1.0 fusion.20
  47.7 1.3 %collective-permute-start.6 = (f32[64,1,8,128]{3,0,2,1:T(8,128)}, f32[64,1,8,128]{3,0,2,1:T(8,128)S(1)}, u32[]{:S(2)}, u32[]{:S(2)}) collective-permute-start(f32[64,1,8,128]{3,0,2,1:T(8,128)} %get-tuple-element.21), channel_id=1, source_target_pairs={{16,0},{17,1},{18,2},{19,3},{20,4},{21,5},{22,6},{23,7},{24,8},{25... | collective-permute-start | bytes 786440 | tf_op jit(solution)/shard_map/ppermute | solution.py:204
  49.0 4.7 %collective-permute-start.7 = (f32[64,1,8,128]{3,0,2,1:T(8,128)}, f32[64,1,8,128]{3,0,2,1:T(8,128)}, u32[]{:S(2)}, u32[]{:S(2)}) collective-permute-start(f32[64,1,8,128]{3,0,2,1:T(8,128)} %get-tuple-element.20), channel_id=1, source_target_pairs={{0,16},{1,17},{2,18},{3,19},{4,20},{5,21},{6,22},{7,23},{8,24},{9,... | collective-permute-start | bytes 786440 | tf_op jit(solution)/shard_map/ppermute | solution.py:201
  53.7 0.0 copy-done.1
  53.7 0.0 copy-done.5
  53.7 0.0 copy-done.6
  53.7 0.0 copy-done.7
  53.7 1.1 pack_parcels.1
  54.8 0.0 copy-done.8
  54.8 7.7 %all-to-all-start = ((f32[16,16,128]{2,1,0:T(8,128)}), f32[16,16,128]{2,1,0:T(8,128)S(1)}, u32[]{:S(2)}, u32[]{:S(2)}) async-start(f32[16,16,128]{2,1,0:T(8,128)} %bitcast.4), calls=%async_computation | async-start | bytes 262144 | tf_op jit(solution)/shard_map/all_to_all | solution.py:228
  62.5 0.0 collective-permute-done.6
  62.5 0.0 collective-permute-done.7
  62.5 1.7 %pad_maximum_fusion.30 = (f32[64,6,1,128]{3,0,2,1:T(8,128)}, f32[64,6,1,128]{3,0,2,1:T(8,128)}) fusion(f32[64,1,8,128]{3,0,2,1:T(8,128)S(1)} %collective-permute-done.6, f32[64,4,8,128]{3,0,2,1:T(8,128)} %copy-done.8, f32[64,1,8,128]{3,0,2,1:T(8,128)} %collective-permute-done.7), kind=kLoop, calls=%fused_computation.47 | loop fusion | flops 196608 | bytes 1966080 | tf_op jit(solution)/shard_map/concatenate | solution.py:205
  64.2 1.3 %collective-permute-start.8 = (f32[64,6,1,128]{3,0,2,1:T(8,128)}, f32[64,6,1,128]{3,0,2,1:T(8,128)}, u32[]{:S(2)}, u32[]{:S(2)}) collective-permute-start(f32[64,6,1,128]{3,0,2,1:T(8,128)} %get-tuple-element.17), channel_id=1, source_target_pairs={{4,0},{8,4},{12,8},{5,1},{9,5},{13,9},{6,2},{10,6},{14,10},{7,3},{... | collective-permute-start | bytes 589832 | tf_op jit(solution)/shard_map/ppermute | solution.py:204
  65.5 4.7 %collective-permute-start.9 = (f32[64,6,1,128]{3,0,2,1:T(8,128)}, f32[64,6,1,128]{3,0,2,1:T(8,128)}, u32[]{:S(2)}, u32[]{:S(2)}) collective-permute-start(f32[64,6,1,128]{3,0,2,1:T(8,128)} %get-tuple-element.16), channel_id=1, source_target_pairs={{0,4},{4,8},{8,12},{1,5},{5,9},{9,13},{2,6},{6,10},{10,14},{3,7},{... | collective-permute-start | bytes 589832 | tf_op jit(solution)/shard_map/ppermute | solution.py:201
  70.2 0.0 all-to-all-done
  70.2 8.2 %couple_gas.1 = (f32[128,128]{1,0:T(8,128)}, f32[2048,128]{1,0:T(8,128)S(1)}) custom-call(f32[256,128]{1,0:T(8,128)S(1)} %bitcast.12, f32[2048,128]{1,0:T(8,128)S(1)} %bitcast.10, f32[1,64]{1,0:T(1,128)S(1)} %bitcast.15, f32[1,64]{1,0:T(1,128)S(1)} %bitcast.19), custom_call_target="tpu_custom_call" | custom-call | tf_op jit(solution)/shard_map/couple_gas/pallas_call | solution.py:270
  78.4 5.6 %all-to-all-start.1 = ((f32[16,8,128]{2,1,0:T(8,128)}), f32[16,8,128]{2,1,0:T(8,128)S(1)}, u32[]{:S(2)}, u32[]{:S(2)}) async-start(f32[16,8,128]{2,1,0:T(8,128)} %bitcast.8), calls=%async_computation.1 | async-start | bytes 131072 | tf_op jit(solution)/shard_map/all_to_all | solution.py:228
  84.1 0.0 collective-permute-done.8
  84.1 0.0 collective-permute-done.9
  84.1 1.7 %pad_maximum_fusion.1 = f32[64,6,10,128]{3,0,2,1:T(8,128)S(1)} fusion(f32[64,6,1,128]{3,0,2,1:T(8,128)} %collective-permute-done.8, f32[64,1,8,128]{3,0,2,1:T(8,128)S(1)} %collective-permute-done.6, f32[64,4,8,128]{3,0,2,1:T(8,128)} %copy-done.8, f32[64,1,8,128]{3,0,2,1:T(8,128)} %collective-permute-done.7, f32[64,6,1,128]{3,0,2,1:T(8,128)} %collective-permute-done.9), kind=kLoop, calls=%fused_computation.1 | loop fusion | flops 1966080 | bytes 3932160 | tf_op jit(solution)/shard_map/concatenate | solution.py:205
  85.8 2.6 %fusion.17 = (f32[64,6,10,1]{3,0,2,1:T(8,128)}, f32[64,6,10,1]{3,0,2,1:T(8,128)}) fusion(f32[64,6,10,128]{3,0,2,1:T(8,128)S(1)} %pad_maximum_fusion.1), kind=kLoop, calls=%fused_computation.53 | loop fusion | bytes 61440 | tf_op jit(solution)/shard_map/slice | solution.py:204
  88.4 2.4 %copy.23 = f32[64,6,10,1]{0,1,3,2:T(8,128)S(1)} copy(f32[64,6,10,1]{3,0,2,1:T(8,128)} %get-tuple-element.12) | data formatting | bytes 30720 | tf_op jit(solution)/shard_map/slice | solution.py:204
  90.8 2.0 %collective-permute-start.10 = (f32[64,6,10,1]{0,1,3,2:T(8,128)S(1)}, f32[64,6,10,1]{0,1,3,2:T(8,128)S(1)}, u32[]{:S(2)}, u32[]{:S(2)}) collective-permute-start(f32[64,6,10,1]{0,1,3,2:T(8,128)S(1)} %copy.23), channel_id=1, source_target_pairs={{1,0},{2,1},{3,2},{5,4},{6,5},{7,6},{9,8},{10,9},{11,10},{13,12},{... | collective-permute-start | bytes 46088 | tf_op jit(solution)/shard_map/ppermute | solution.py:204
  92.8 2.4 %copy.25 = f32[64,6,10,1]{0,1,3,2:T(8,128)S(1)} copy(f32[64,6,10,1]{3,0,2,1:T(8,128)} %get-tuple-element.13) | data formatting | bytes 30720 | tf_op jit(solution)/shard_map/slice | solution.py:202
  95.2 3.7 %collective-permute-start.11 = (f32[64,6,10,1]{0,1,3,2:T(8,128)S(1)}, f32[64,6,10,1]{0,1,3,2:T(8,128)}, u32[]{:S(2)}, u32[]{:S(2)}) collective-permute-start(f32[64,6,10,1]{0,1,3,2:T(8,128)S(1)} %copy.25), channel_id=1, source_target_pairs={{0,1},{1,2},{2,3},{4,5},{5,6},{6,7},{8,9},{9,10},{10,11},{12,13},{... | collective-permute-start | bytes 46088 | tf_op jit(solution)/shard_map/ppermute | solution.py:201
  99.0 2.4 %evolve_droplets.1.tail = f32[32,64,128]{2,1,0:T(8,128)} custom-call(f32[32,64,128]{2,1,0:T(8,128)S(1)} %copy-done.1, f32[1,64]{1,0:T(1,128)S(1)} %bitcast.16, f32[1,64]{1,0:T(1,128)S(1)} %bitcast.20), custom_call_target="tpu_custom_call" | custom-call | flops 5242880 | bytes 2097152 | tf_op jit(solution)/shard_map/evolve_droplets/pallas_call | solution.py:289
  101.4 0.0 all-to-all-done.1
  101.4 1.9 %finish_droplets.1 = f32[32,64,128]{2,1,0:T(8,128)} custom-call(f32[32,64,128]{2,1,0:T(8,128)} %evolve_droplets.1.tail, f32[128,128]{1,0:T(8,128)S(1)} %bitcast.13, s32[1,128]{1,0:T(1,128)S(1)} %get-tuple-element.9.slots, f32[1,64]{1,0:T(1,128)S(1)} %bitcast.17, f32[1,64]{1,0:T(1,128)S(1)} %bitcast.21), custom_call_target="tpu_custom_call", output_to_operand_aliasing={{}: (0, {})} | custom-call | tf_op jit(solution)/shard_map/finish_droplets/pallas_call | solution.py:300
  103.2 0.0 collective-permute-done.10
  103.2 1.9 %copy.24 = f32[64,6,10,1]{3,0,2,1:T(8,128)} copy(f32[64,6,10,1]{0,1,3,2:T(8,128)S(1)} %collective-permute-done.10) | data formatting | bytes 30720 | tf_op jit(solution)/shard_map/ppermute | solution.py:204
  105.2 0.0 collective-permute-done.11
  105.2 2.7 %copy.26 = f32[64,6,10,1]{3,0,2,1:T(8,128)} copy(f32[64,6,10,1]{0,1,3,2:T(8,128)} %collective-permute-done.11) | data formatting | bytes 30720 | tf_op jit(solution)/shard_map/ppermute | solution.py:201
  107.9 3.1 %fusion.4 = f32[64,4,8,128]{3,0,2,1:T(8,128)S(1)} fusion(f32[64,4,8,128]{3,0,2,1:T(8,128)S(1)} %copy-done.9, f32[64,6,10,1]{3,0,2,1:T(8,128)} %copy.26, f32[64,6,1,128]{3,0,2,1:T(8,128)} %collective-permute-done.8, f32[64,6,1,128]{3,0,2,1:T(8,128)} %collective-permute-done.9, f32[64,1,8,128]{3,0,2,1:T(8,128)S(1)} %collective-permute-done.6, ...), kind=kLoop, calls=%fused_computation.7 | loop fusion | flops 7340032 | bytes 4094208 | tf_op jit(solution)/shard_map/add | solution.py:314
  111.1 1.6 %copy.28 = f32[64,4,8,128]{3,2,1,0:T(8,128)} copy(f32[64,4,8,128]{3,0,2,1:T(8,128)S(1)} %fusion.4) | data formatting | bytes 2097152
  (23 shorter events, 0.1 us)
Async XLA Ops:
  0.6 10.9 %copy-start = (f32[64,4,8,128]{3,2,1,0:T(8,128)S(1)}, f32[64,4,8,128]{3,2,1,0:T(8,128)}, u32[]{:S(2)}) copy-start(f32[64,4,8,128]{3,2,1,0:T(8,128)} %param.9) | copy-start | bytes 3145732
  2.6 5.3 %copy-start.11 = (f32[64,4,8,128]{3,0,2,1:T(8,128)}, f32[64,4,8,128]{3,0,2,1:T(8,128)S(1)}, u32[]{:S(2)}) copy-start(f32[64,4,8,128]{3,0,2,1:T(8,128)S(1)} %copy.22) | copy-start | bytes 3145732
  2.6 8.9 %collective-permute-start.1 = (f32[64,1,8,128]{3,0,2,1:T(8,128)S(1)}, f32[64,1,8,128]{3,0,2,1:T(8,128)S(1)}, u32[]{:S(2)}, u32[]{:S(2)}) collective-permute-start(f32[64,1,8,128]{3,0,2,1:T(8,128)S(1)} %get-tuple-element.23), channel_id=1, source_target_pairs={{0,16},{1,17},{2,18},{3,19},{4,20},{5,21},{6,22},{7,23},{8,24},{9,... | collective-permute-start | bytes 786440 | tf_op jit(solution)/shard_map/ppermute | solution.py:201
  6.6 8.8 %collective-permute-start = (f32[64,1,8,128]{3,0,2,1:T(8,128)S(1)}, f32[64,1,8,128]{3,0,2,1:T(8,128)S(1)}, u32[]{:S(2)}, u32[]{:S(2)}) collective-permute-start(f32[64,1,8,128]{3,0,2,1:T(8,128)S(1)} %get-tuple-element.22), channel_id=1, source_target_pairs={{16,0},{17,1},{18,2},{19,3},{20,4},{21,5},{22,6},{23,7},{24,8},{25... | collective-permute-start | bytes 786440 | tf_op jit(solution)/shard_map/ppermute | solution.py:204
  15.3 8.0 %copy-start.12 = (f32[64,1,8,128]{3,0,2,1:T(8,128)}, f32[64,1,8,128]{3,0,2,1:T(8,128)S(1)}, u32[]{:S(2)}) copy-start(f32[64,1,8,128]{3,0,2,1:T(8,128)S(1)} %collective-permute-done) | copy-start | bytes 786436
  15.4 7.9 %copy-start.10 = (f32[64,6,8,128]{3,0,2,1:T(8,128)}, f32[64,6,8,128]{3,0,2,1:T(8,128)S(1)}, u32[]{:S(2)}) copy-start(f32[64,6,8,128]{3,0,2,1:T(8,128)S(1)} %constant_dynamic-update-slice_fusion) | copy-start | bytes 4718596
  15.4 6.4 %collective-permute-start.2 = (f32[64,6,1,128]{3,0,2,1:T(8,128)S(1)}, f32[64,6,1,128]{3,0,2,1:T(8,128)S(1)}, u32[]{:S(2)}, u32[]{:S(2)}) collective-permute-start(f32[64,6,1,128]{3,0,2,1:T(8,128)S(1)} %get-tuple-element.19), channel_id=1, source_target_pairs={{4,0},{8,4},{12,8},{5,1},{9,5},{13,9},{6,2},{10,6},{14,10},{7,3},{... | collective-permute-start | bytes 589832 | tf_op jit(solution)/shard_map/ppermute | solution.py:204
  16.7 6.6 %collective-permute-start.3 = (f32[64,6,1,128]{3,0,2,1:T(8,128)S(1)}, f32[64,6,1,128]{3,0,2,1:T(8,128)S(1)}, u32[]{:S(2)}, u32[]{:S(2)}) collective-permute-start(f32[64,6,1,128]{3,0,2,1:T(8,128)S(1)} %get-tuple-element.18), channel_id=1, source_target_pairs={{0,4},{4,8},{8,12},{1,5},{5,9},{9,13},{2,6},{6,10},{10,14},{3,7},{... | collective-permute-start | bytes 589832 | tf_op jit(solution)/shard_map/ppermute | solution.py:201
  21.8 1.5 %copy-start.13 = (f32[64,6,1,128]{3,0,2,1:T(8,128)}, f32[64,6,1,128]{3,0,2,1:T(8,128)S(1)}, u32[]{:S(2)}) copy-start(f32[64,6,1,128]{3,0,2,1:T(8,128)S(1)} %collective-permute-done.2) | copy-start | bytes 589828
  23.3 0.7 copy-start.14
  28.5 9.0 %collective-permute-start.4 = (f32[64,6,10,1]{0,1,3,2:T(8,128)S(1)}, f32[64,6,10,1]{0,1,3,2:T(8,128)S(1)}, u32[]{:S(2)}, u32[]{:S(2)}) collective-permute-start(f32[64,6,10,1]{0,1,3,2:T(8,128)S(1)} %copy.17), channel_id=1, source_target_pairs={{1,0},{2,1},{3,2},{5,4},{6,5},{7,6},{9,8},{10,9},{11,10},{13,12},{... | collective-permute-start | bytes 46088 | tf_op jit(solution)/shard_map/ppermute | solution.py:204
  34.3 7.1 %copy-start.15 = (f32[64]{0:T(128)S(1)}, f32[64]{0:T(128)}, u32[]{:S(2)}) copy-start(f32[64]{0:T(128)} %param.17) | copy-start | bytes 772
  34.3 5.1 %collective-permute-start.5 = (f32[64,6,10,1]{0,1,3,2:T(8,128)S(1)}, f32[64,6,10,1]{0,1,3,2:T(8,128)S(1)}, u32[]{:S(2)}, u32[]{:S(2)}) collective-permute-start(f32[64,6,10,1]{0,1,3,2:T(8,128)S(1)} %copy.19), channel_id=1, source_target_pairs={{0,1},{1,2},{2,3},{4,5},{5,6},{6,7},{8,9},{9,10},{10,11},{12,13},{... | collective-permute-start | bytes 46088 | tf_op jit(solution)/shard_map/ppermute | solution.py:201
  41.4 12.3 %copy-start.1 = (f32[32,64,128]{2,1,0:T(8,128)S(1)}, f32[32,64,128]{2,1,0:T(8,128)}, u32[]{:S(2)}) copy-start(f32[32,64,128]{2,1,0:T(8,128)} %state_in.1) | copy-start | bytes 3145732
  41.4 12.3 %copy-start.2 = (f32[64]{0:T(128)S(1)}, f32[64]{0:T(128)}, u32[]{:S(2)}) copy-start(f32[64]{0:T(128)} %param.15) | copy-start | bytes 772
  41.4 12.3 %copy-start.3 = (f32[64]{0:T(128)S(1)}, f32[64]{0:T(128)}, u32[]{:S(2)}) copy-start(f32[64]{0:T(128)} %param.16) | copy-start | bytes 772
  41.4 12.3 %copy-start.4 = (s32[8,128]{1,0:T(8,128)S(1)}, s32[8,128]{1,0:T(8,128)}, u32[]{:S(2)}) copy-start(s32[8,128]{1,0:T(8,128)} %cells.1) | copy-start | bytes 12292
  41.4 12.3 %copy-start.5 = (f32[8,128]{1,0:T(8,128)S(1)}, f32[8,128]{1,0:T(8,128)}, u32[]{:S(2)}) copy-start(f32[8,128]{1,0:T(8,128)} %weights.1) | copy-start | bytes 12292
  41.4 12.3 %copy-start.6 = (s32[128,1]{0,1:T(1,128)S(1)}, s32[128,1]{0,1:T(1,128)}, u32[]{:S(2)}) copy-start(s32[128,1]{0,1:T(1,128)} %param.11) | copy-start | bytes 1540
  41.4 12.3 %copy-start.7 = (f32[128]{0:T(128)S(1)}, f32[128]{0:T(128)}, u32[]{:S(2)}) copy-start(f32[128]{0:T(128)} %param.14) | copy-start | bytes 1540
  46.7 8.1 %copy-start.8 = (f32[64,4,8,128]{3,0,2,1:T(8,128)}, f32[64,4,8,128]{3,0,2,1:T(8,128)S(1)}, u32[]{:S(2)}) copy-start(f32[64,4,8,128]{3,0,2,1:T(8,128)S(1)} %fusion.12) | copy-start | bytes 3145732
  47.7 14.8 %collective-permute-start.6 = (f32[64,1,8,128]{3,0,2,1:T(8,128)}, f32[64,1,8,128]{3,0,2,1:T(8,128)S(1)}, u32[]{:S(2)}, u32[]{:S(2)}) collective-permute-start(f32[64,1,8,128]{3,0,2,1:T(8,128)} %get-tuple-element.21), channel_id=1, source_target_pairs={{16,0},{17,1},{18,2},{19,3},{20,4},{21,5},{22,6},{23,7},{24,8},{25... | collective-permute-start | bytes 786440 | tf_op jit(solution)/shard_map/ppermute | solution.py:204
  49.0 13.5 %collective-permute-start.7 = (f32[64,1,8,128]{3,0,2,1:T(8,128)}, f32[64,1,8,128]{3,0,2,1:T(8,128)}, u32[]{:S(2)}, u32[]{:S(2)}) collective-permute-start(f32[64,1,8,128]{3,0,2,1:T(8,128)} %get-tuple-element.20), channel_id=1, source_target_pairs={{0,16},{1,17},{2,18},{3,19},{4,20},{5,21},{6,22},{7,23},{8,24},{9,... | collective-permute-start | bytes 786440 | tf_op jit(solution)/shard_map/ppermute | solution.py:201
  54.8 15.4 %all-to-all-start = ((f32[16,16,128]{2,1,0:T(8,128)}), f32[16,16,128]{2,1,0:T(8,128)S(1)}, u32[]{:S(2)}, u32[]{:S(2)}) async-start(f32[16,16,128]{2,1,0:T(8,128)} %bitcast.4), calls=%async_computation | async-start | bytes 262144 | tf_op jit(solution)/shard_map/all_to_all | solution.py:228
  64.2 19.9 %collective-permute-start.8 = (f32[64,6,1,128]{3,0,2,1:T(8,128)}, f32[64,6,1,128]{3,0,2,1:T(8,128)}, u32[]{:S(2)}, u32[]{:S(2)}) collective-permute-start(f32[64,6,1,128]{3,0,2,1:T(8,128)} %get-tuple-element.17), channel_id=1, source_target_pairs={{4,0},{8,4},{12,8},{5,1},{9,5},{13,9},{6,2},{10,6},{14,10},{7,3},{... | collective-permute-start | bytes 589832 | tf_op jit(solution)/shard_map/ppermute | solution.py:204
  65.5 18.6 %collective-permute-start.9 = (f32[64,6,1,128]{3,0,2,1:T(8,128)}, f32[64,6,1,128]{3,0,2,1:T(8,128)}, u32[]{:S(2)}, u32[]{:S(2)}) collective-permute-start(f32[64,6,1,128]{3,0,2,1:T(8,128)} %get-tuple-element.16), channel_id=1, source_target_pairs={{0,4},{4,8},{8,12},{1,5},{5,9},{9,13},{2,6},{6,10},{10,14},{3,7},{... | collective-permute-start | bytes 589832 | tf_op jit(solution)/shard_map/ppermute | solution.py:201
  78.4 22.9 %all-to-all-start.1 = ((f32[16,8,128]{2,1,0:T(8,128)}), f32[16,8,128]{2,1,0:T(8,128)S(1)}, u32[]{:S(2)}, u32[]{:S(2)}) async-start(f32[16,8,128]{2,1,0:T(8,128)} %bitcast.8), calls=%async_computation.1 | async-start | bytes 131072 | tf_op jit(solution)/shard_map/all_to_all | solution.py:228
  90.8 12.4 %collective-permute-start.10 = (f32[64,6,10,1]{0,1,3,2:T(8,128)S(1)}, f32[64,6,10,1]{0,1,3,2:T(8,128)S(1)}, u32[]{:S(2)}, u32[]{:S(2)}) collective-permute-start(f32[64,6,10,1]{0,1,3,2:T(8,128)S(1)} %copy.23), channel_id=1, source_target_pairs={{1,0},{2,1},{3,2},{5,4},{6,5},{7,6},{9,8},{10,9},{11,10},{13,12},{... | collective-permute-start | bytes 46088 | tf_op jit(solution)/shard_map/ppermute | solution.py:204
  95.2 9.9 %collective-permute-start.11 = (f32[64,6,10,1]{0,1,3,2:T(8,128)S(1)}, f32[64,6,10,1]{0,1,3,2:T(8,128)}, u32[]{:S(2)}, u32[]{:S(2)}) collective-permute-start(f32[64,6,10,1]{0,1,3,2:T(8,128)S(1)} %copy.25), channel_id=1, source_target_pairs={{0,1},{1,2},{2,3},{4,5},{5,6},{6,7},{8,9},{9,10},{10,11},{12,13},{... | collective-permute-start | bytes 46088 | tf_op jit(solution)/shard_map/ppermute | solution.py:201
  103.2 4.7 %copy-start.9 = (f32[64,4,8,128]{3,0,2,1:T(8,128)S(1)}, f32[64,4,8,128]{3,0,2,1:T(8,128)}, u32[]{:S(2)}) copy-start(f32[64,4,8,128]{3,0,2,1:T(8,128)} %copy-done.8) | copy-start | bytes 3145732

commit v2 on v1

--- a/solution.py
+++ b/solution.py
@@ -193,29 +193,221 @@
         out[i] = tail[i] + response[i] * gas_at
 
 
-def with_halo(block, sides, width):
-    for axis, dim in sides:
-        count = lax.axis_size(axis)
-        forward = [(i, i + 1) for i in range(count - 1)]
-        backward = [(target, source) for source, target in forward]
-        low = lax.ppermute(
-            lax.slice_in_dim(block, block.shape[dim] - width, None, axis=dim), axis, forward
-        )
-        high = lax.ppermute(lax.slice_in_dim(block, 0, width, axis=dim), axis, backward)
-        block = jnp.concatenate([low, block, high], axis=dim)
-    return block
-
-
-def stencil_update(padded, field, gas_rate):
-    beside = padded[:, 2:, 1:-1, 1:-1] + padded[:, :-2, 1:-1, 1:-1]
-    beside = beside + padded[:, 1:-1, 2:, 1:-1] + padded[:, 1:-1, :-2, 1:-1]
-    beside = beside + padded[:, 1:-1, 1:-1, 2:] + padded[:, 1:-1, 1:-1, :-2]
-    return field + gas_rate[:, None, None, None] * (beside - 6.0 * field)
-
-
-def gas_step(field, gas_rate):
-    padded = with_halo(field, (("gx", 1), ("gy", 2), ("gz", 3)), 1)
-    return stencil_update(padded, field, gas_rate)
+def place_on(axis):
+    index, count = lax.axis_index(axis), lax.axis_size(axis)
+    even = lax.rem(index, 2) == 0
+    below = jnp.where(index > 0, 1.0, 0.0).astype(F32)
+    above = jnp.where(index < count - 1, 1.0, 0.0).astype(F32)
+    return even, below, above
+
+
+def swaps(axis):
+    count = lax.axis_size(axis)
+    rounds = []
+    for first in range(2):
+        pairs = [(i, i + 1) for i in range(first, count - 1, 2)]
+        if pairs:
+            rounds.append(pairs + [(j, i) for i, j in pairs])
+    return rounds
+
+
+def swap_all(messages, axis):
+    return [lax.ppermute(m, axis, pairs) for m, pairs in zip(messages, swaps(axis), strict=True)]
+
+
+def low_high(even, first, second):
+    if second is None:
+        second = jnp.zeros_like(first)
+    return jnp.where(even, second, first), jnp.where(even, first, second)
+
+
+def beside_z(block):
+    axis = block.ndim - 1
+    lane = iota(block.shape, axis)
+    before = jnp.where(lane == 0, 0.0, pltpu.roll(block, 1, axis))
+    after = jnp.where(lane == LANES - 1, 0.0, pltpu.roll(block, LANES - 1, axis))
+    return before + after
+
+
+def beside_y(block, low, high):
+    axis = block.ndim - 2
+    size = block.shape[axis]
+    row = iota(block.shape, axis)
+    before = jnp.where(row == 0, low, pltpu.roll(block, 1, axis))
+    after = jnp.where(row == size - 1, high, pltpu.roll(block, size - 1, axis))
+    return before + after
+
+
+def beside_x(block, low, high):
+    before = jnp.concatenate([low[None], block[:-1]], axis=0)
+    after = jnp.concatenate([block[1:], high[None]], axis=0)
+    return before + after
+
+
+def x_faces_kernel(gas, *refs):
+    sends, sems = refs[:-1], refs[-1]
+    even, _, _ = place_on("gx")
+    top = gas.shape[1] - 2
+    copies = []
+    for turn, send in enumerate(sends):
+        start = jnp.where(even == (turn == 0), top, 0)
+        copies.append(pltpu.make_async_copy(gas.at[:, pl.ds(start, 2)], send, sems.at[turn]))
+    for copy in copies:
+        copy.start()
+    for copy in copies:
+        copy.wait()
+
+
+def y_faces_kernel(size_x, size_y, turns_x, gas, *refs):
+    xs, (send_a, send_b) = refs[:turns_x], refs[turns_x:]
+    species = send_a.shape[1]
+    lines = size_x * size_y
+    even, _, _ = place_on("gy")
+    even_x, _, _ = place_on("gx")
+    for turn, send in enumerate((send_a, send_b)):
+        up = even == (turn == 0)
+        near = jnp.where(up, size_y - 1, 0)
+        far = jnp.where(up, size_y - 2, 1)
+        for x in range(size_x):
+            send[x] = gas[pl.ds(x * size_y + near, species, stride=lines), :]
+            send[size_x + x] = gas[pl.ds(x * size_y + far, species, stride=lines), :]
+        edges = []
+        for layer in (1, 0):
+            parts = [x[pl.ds(layer * size_y + near, species, stride=2 * size_y), :] for x in xs]
+            edges.append(low_high(even_x, parts[0], parts[1] if turns_x == 2 else None))
+        send[2 * size_x] = edges[0][0]
+        send[2 * size_x + 1] = edges[1][1]
+
+
+def first_step_kernel(size_x, size_y, turns_x, gas, *refs):
+    xs, refs = refs[:turns_x], refs[turns_x:]
+    ya, yb, rate_s, rate, field, side_x, side_y, za, zb, y_low, y_high = refs
+    species = rate.shape[1]
+    lines = size_x * size_y
+    even_x, below_x, above_x = place_on("gx")
+    even_y, below_y, above_y = place_on("gy")
+    even_z, _, _ = place_on("gz")
+    for plane in range(2 * size_x + 2):
+        y_low[plane], y_high[plane] = low_high(even_y, ya[plane], yb[plane])
+    column = as_column(rate[...])
+    for side, (halo, row, exists) in enumerate(((y_low, 0, below_y), (y_high, size_y - 1, above_y))):
+        for x in range(size_x):
+            near = halo[x]
+            before = halo[x - 1] if x > 0 else halo[2 * size_x]
+            after = halo[x + 1] if x < size_x - 1 else halo[2 * size_x + 1]
+            own = gas[pl.ds(x * size_y + row, species, stride=lines), :]
+            total = before + after + halo[size_x + x] + exists * own + beside_z(near)
+            side_y[side, x] = near + column * (total - 6.0 * near)
+
+    def x_halo(at):
+        parts = [x[at] for x in xs]
+        return low_high(even_x, parts[0], parts[1] if turns_x == 2 else None)
+
+    @pl.loop(0, species, unroll=2)
+    def _(s):
+        r = rate_s[0, s]
+        own = gas[pl.ds(s * lines, lines), :].reshape(size_x, size_y, LANES)
+        layers = [x_halo(pl.ds((2 * s + i) * size_y, size_y)) for i in range(2)]
+        low, low_far = layers[1][0], layers[0][0]
+        high, high_far = layers[0][1], layers[1][1]
+        here = pl.ds(s, 1)
+        total = beside_x(own, low, high) + beside_z(own)
+        total = total + beside_y(own, y_low[:size_x, here, :], y_high[:size_x, here, :])
+        field[pl.ds(s * lines, lines), :] = (own + r * (total - 6.0 * own)).reshape(lines, LANES)
+        sides = ((low, low_far, own[0], below_x), (high, high_far, own[-1], above_x))
+        for side, (near, far, inner, exists) in enumerate(sides):
+            edge = 2 * size_x + side
+            total = far + exists * inner + beside_z(near)
+            total = total + beside_y(near, y_low[edge, here, :], y_high[edge, here, :])
+            side_x[side, s] = near + r * (total - 6.0 * near)
+
+    low_rows, high_rows = [], []
+
+    def add_columns(block):
+        turned = jnp.transpose(block)
+        low_rows.append(turned[:1])
+        high_rows.append(turned[-1:])
+
+    for ref in (gas, field):
+        for i in range(species * lines // LANES):
+            add_columns(ref[i * LANES : (i + 1) * LANES, :])
+    per = LANES // size_y
+    for side in range(2):
+        for i in range(species // per):
+            parts = []
+            for x in xs:
+                near = x[...].reshape(species, 2, size_y, LANES)[i * per : (i + 1) * per, 1 - side]
+                parts.append(near.reshape(LANES, LANES))
+            add_columns(low_high(even_x, parts[0], parts[1] if turns_x == 2 else None)[side])
+    for halo in (y_low, y_high):
+        for i in range(size_x * species // LANES):
+            each = LANES // species
+            add_columns(halo[i * each : (i + 1) * each].reshape(LANES, LANES))
+    rest = jnp.zeros((za.shape[0] - len(low_rows), LANES), F32)
+    low = jnp.concatenate(low_rows + [rest], axis=0)
+    high = jnp.concatenate(high_rows + [rest], axis=0)
+    za[...] = jnp.where(even_z, high, low)
+    zb[...] = jnp.where(even_z, low, high)
+
+
+def second_step_kernel(
+    size_x, size_y, field, side_x, side_y, za, zb, za_in, zb_in, rate_s, rate, deposit, out, halo, halo_x, halo_y, halo_next
+):
+    species = rate.shape[1]
+    lines = size_x * size_y
+    even, below, above = place_on("gz")
+    low, high = low_high(even, za_in[...], zb_in[...])
+    own_low, own_high = low_high(even, za[...], zb[...])
+    count = species * lines // LANES
+    each = LANES // lines
+    row, lane = iota((count, LANES), 0), iota((count, LANES), 1)
+    rates = jnp.zeros((count, LANES), F32)
+    for part in range(each):
+        pick = iota((count, species), 1) == iota((count, species), 0) * each + part
+        of_row = jnp.sum(jnp.where(pick, rate[...], 0.0), axis=1, keepdims=True)
+        rates = jnp.where(lane // lines == part, of_row, rates)
+    next_low = low[count : 2 * count] + below * rates * own_low[:count]
+    next_high = high[count : 2 * count] + above * rates * own_high[:count]
+
+    def spread(low_row, high_row):
+        turned = iota((LANES, LANES), 0)
+        rows = jnp.where(turned == 0, low_row, jnp.where(turned == LANES - 1, high_row, 0.0))
+        return jnp.transpose(rows)
+
+    for i in range(count):
+        at = slice(i * LANES, (i + 1) * LANES)
+        halo[at, :] = spread(low[i : i + 1], high[i : i + 1])
+        halo_next[at, :] = spread(next_low[i : i + 1], next_high[i : i + 1])
+    first = 2 * count
+    for i in range(2 * species * size_y // LANES):
+        halo_x[i * LANES : (i + 1) * LANES, :] = spread(low[first + i : first + i + 1], high[first + i : first + i + 1])
+    first = first + 2 * species * size_y // LANES
+    for i in range(2 * species * size_x // LANES):
+        halo_y[i * LANES : (i + 1) * LANES, :] = spread(low[first + i : first + i + 1], high[first + i : first + i + 1])
+    column = as_column(rate[...])
+    for side in range(2):
+        for x in range(size_x):
+            at = pl.ds((side * size_x + x) * species, species)
+            halo_y[at, :] = side_y[side, x] + column * halo_y[at, :]
+
+    @pl.loop(0, species, unroll=2)
+    def _(s):
+        r = rate_s[0, s]
+        at = pl.ds(s * lines, lines)
+        now = (field[at, :] + r * halo[at, :]).reshape(size_x, size_y, LANES)
+        x_low, x_high = [
+            side_x[side, s] + r * halo_x[pl.ds((side * species + s) * size_y, size_y), :] for side in range(2)
+        ]
+        y_low, y_high = [
+            jnp.concatenate(
+                [halo_y[pl.ds((side * size_x + x) * species + s, 1), :][None] for x in range(size_x)], axis=0
+            )
+            for side in range(2)
+        ]
+        total = beside_x(now, x_low, x_high) + beside_y(now, y_low, y_high) + beside_z(now)
+        total = total + halo_next[at, :].reshape(now.shape)
+        result = now + r * (total - 6.0 * now)
+        out[at, :] = result.reshape(lines, LANES) + deposit[at, :]
 
 
 def full(shape):
@@ -260,7 +452,7 @@
             rate_spec,
         ],
         out_specs=(full((slots, LANES)), full((1, parcels))),
-        compiler_params=pltpu.CompilerParams(vmem_limit_bytes=16 * MIB),
+        compiler_params=pltpu.CompilerParams(vmem_limit_bytes=4 * MIB),
         name="pack_parcels",
     )(droplet, owner.reshape(1, parcels), cells, weights, mass.reshape(1, parcels), liquid, surface)
 
@@ -278,7 +470,7 @@
             pltpu.VMEM((lines, LANES, slots), BF16),
             pltpu.VMEM((lines, 2 * species, LANES), BF16),
         ],
-        compiler_params=pltpu.CompilerParams(vmem_limit_bytes=32 * MIB),
+        compiler_params=pltpu.CompilerParams(vmem_limit_bytes=12 * MIB),
         name="couple_gas",
     )(rows, flat, liquid, surface)
 
@@ -292,7 +484,7 @@
         out_shape=jax.ShapeDtypeStruct(droplet.shape, F32),
         in_specs=[drop_spec, rate_spec, rate_spec],
         out_specs=drop_spec,
-        compiler_params=pltpu.CompilerParams(vmem_limit_bytes=16 * MIB),
+        compiler_params=pltpu.CompilerParams(vmem_limit_bytes=8 * MIB),
         cost_estimate=pl.CostEstimate(flops=20 * droplet.size, bytes_accessed=8 * droplet.size, transcendentals=0),
         name="evolve_droplets",
     )(droplet, liquid, surface)
@@ -304,14 +496,64 @@
         in_specs=[tail_spec, full((back_rows, LANES)), full((1, parcels)), rate_spec, rate_spec],
         out_specs=tail_spec,
         input_output_aliases={0: 0},
-        compiler_params=pltpu.CompilerParams(vmem_limit_bytes=16 * MIB),
+        compiler_params=pltpu.CompilerParams(vmem_limit_bytes=4 * MIB),
         name="finish_droplets",
     )(evolved, returned, slot, liquid, surface)
 
-    field = gas
-    for substep in range(GAS_STEPS):
-        field = gas_step(field, gas_rate)
-    return (field + deposit.reshape(gas.shape), droplet_next)
+    size_x, size_y = gas.shape[1], gas.shape[2]
+    rate = gas_rate.reshape(1, species)
+    smem = pl.BlockSpec(memory_space=pltpu.SMEM)
+    vmem = pl.BlockSpec(memory_space=pltpu.VMEM)
+    turns_x = len(swaps("gx"))
+    x_shape = jax.ShapeDtypeStruct((species, 2, size_y, LANES), F32)
+    x_sends = pl.pallas_call(
+        x_faces_kernel,
+        out_shape=[x_shape] * turns_x,
+        in_specs=[pl.BlockSpec(memory_space=pl.ANY)],
+        out_specs=[vmem] * turns_x,
+        scratch_shapes=[pltpu.SemaphoreType.DMA((2,))],
+        compiler_params=pltpu.CompilerParams(vmem_limit_bytes=4 * MIB),
+        name="x_faces",
+    )(gas)
+    x_halo = [x.reshape(-1, LANES) for x in swap_all(x_sends, "gx")]
+    y_shape = (2 * size_x + 2, species, LANES)
+    y_sends = pl.pallas_call(
+        functools.partial(y_faces_kernel, size_x, size_y, turns_x),
+        out_shape=[jax.ShapeDtypeStruct(y_shape, F32)] * 2,
+        compiler_params=pltpu.CompilerParams(vmem_limit_bytes=6 * MIB),
+        name="y_faces",
+    )(flat, *x_halo)
+    y_halo = swap_all(y_sends, "gy")
+    z_shape = (48, LANES)
+    field, side_x, side_y, *z_sends = pl.pallas_call(
+        functools.partial(first_step_kernel, size_x, size_y, turns_x),
+        out_shape=(
+            jax.ShapeDtypeStruct(flat.shape, F32),
+            jax.ShapeDtypeStruct((2, species, size_y, LANES), F32),
+            jax.ShapeDtypeStruct((2, size_x, species, LANES), F32),
+            jax.ShapeDtypeStruct(z_shape, F32),
+            jax.ShapeDtypeStruct(z_shape, F32),
+        ),
+        in_specs=[vmem] * (turns_x + 3) + [smem, vmem],
+        scratch_shapes=[pltpu.VMEM(y_shape, F32), pltpu.VMEM(y_shape, F32)],
+        compiler_params=pltpu.CompilerParams(vmem_limit_bytes=10 * MIB),
+        name="first_gas_step",
+    )(flat, *x_halo, *y_halo, rate, rate)
+    z_halo = swap_all(z_sends, "gz")
+    gas_next = pl.pallas_call(
+        functools.partial(second_step_kernel, size_x, size_y),
+        out_shape=jax.ShapeDtypeStruct(flat.shape, F32),
+        in_specs=[vmem] * 7 + [smem, vmem, vmem],
+        scratch_shapes=[
+            pltpu.VMEM(flat.shape, F32),
+            pltpu.VMEM((2 * species * size_y, LANES), F32),
+            pltpu.VMEM((2 * species * size_x, LANES), F32),
+            pltpu.VMEM(flat.shape, F32),
+        ],
+        compiler_params=pltpu.CompilerParams(vmem_limit_bytes=10 * MIB),
+        name="second_gas_step",
+    )(field, side_x, side_y, *z_sends, *z_halo, rate, rate, deposit)
+    return (gas_next.reshape(gas.shape), droplet_next)
 
 
 def solution(mesh):

time: 113 us -> 58.9 us (0.52)
  starting transfers between devices: 49.7 us -> 22.9 us
  local copies, waits for them, and re-layouts: 27.1 us -> 4.93 us
  Pallas kernels: 13.6 us -> 26.1 us
  other arithmetic: 12 us -> 0 us
  waiting for transfers between devices: 9.4 us -> 3.76 us
    ppermute x12 -> x5, starting transfers between devices: 36.4 us -> 8.39 us  [swap_all(): lax.ppermute(m, axis, pairs)]
    slice x9 -> x0, local copies, waits for them, and re-layouts: 13.7 us -> none  [the longest x5 9.45 us: with_halo(): lax.slice_in_dim(block, 0, width, axis=dim)]
    pallas_call x0 -> x4, Pallas kernels: none -> 12.4 us  [the longest x1 5.63 us: on_device(): pl.pallas_call(functools.partial(second_step_kernel, size_x, size_y), out...]
    ppermute x4 -> x0, local copies, waits for them, and re-layouts: 8.54 us -> none  [the longest x2 4.71 us: with_halo(): lax.ppermute(lax.slice_in_dim(block, block.shape[dim] - width, None, axis...]
    add x2 -> x0, other arithmetic: 8.4 us -> none  [the longest x1 5.25 us: stencil_update(): return field + gas_rate[:, None, None, None] * (beside - 6.0 * field)]
    ppermute x12 -> x5, waiting for transfers between devices: 9.39 us -> 3.75 us  [swap_all(): lax.ppermute(m, axis, pairs)]
    concatenate x3 -> x0, other arithmetic: 3.56 us -> none  [with_halo(): block = jnp.concatenate([low, block, high], axis=dim)]
    all_to_all x2, starting transfers between devices: 13.3 us -> 14.6 us  [exchange(): lax.all_to_all(chunks, ('gy', 'gz'), split_axis=0, concat_axis=0, tiled=T...]
  transfers between devices with their start and end apart: 14 -> 7, of which waited for: 4 -> 1; matrix products, arithmetic and copies ran while one was open for 14% -> 0% of each run, Pallas kernels for 12% -> 35%
where the time goes in v2:
time: 58.9 us; the launch traced here: 58.5 us
  Pallas kernels  26.1 us (44%)
  starting transfers between devices  22.9 us (39%)
  local copies, waits for them, and re-layouts  4.93 us (8%)
  waiting for transfers between devices  3.76 us (6%)
  between operations  0.78 us (1%)
    all_to_all x2, starting transfers between devices, exchange(): lax.all_to_all(chunks, ('gy', 'gz'), split_axis=0, concat_axis=0, tiled=T...  14.6 us
    ppermute x5, starting transfers between devices, swap_all(): lax.ppermute(m, axis, pairs)  8.39 us
    pallas_call x1, Pallas kernels, on_device(): pl.pallas_call(functools.partial(couple_kernel, cap, packed), out_shape=(...  8.22 us
    pallas_call x1, Pallas kernels, on_device(): pl.pallas_call(functools.partial(second_step_kernel, size_x, size_y), out...  5.63 us
    pallas_call x1, Pallas kernels, on_device(): pl.pallas_call(functools.partial(first_step_kernel, size_x, size_y, turns...  5.34 us
    unnamed x32, local copies, waits for them, and re-layouts  4.93 us
    ppermute x5, waiting for transfers between devices, swap_all(): lax.ppermute(m, axis, pairs)  3.75 us
    pallas_call x1, Pallas kernels, on_device(): pl.pallas_call(droplet_kernel, grid=(species // block,), out_shape=jax.Sh...  2.41 us
  transfers between devices with their start and end apart: 7, of which 1 were waited for; matrix products, arithmetic and copies ran while one was open for 0% of the time, Pallas kernels for 35%

profile of v2, /device:TPU:1, one launch (start us, length us, event | category | flops | bytes accessed | tf_op | source)
XLA Modules:
  0.0 58.5 jit_solution(13251068282897506927)
XLA Ops:
  0.6 0.0 copy-start
  0.6 1.2 %copy-done = f32[64,4,8,128]{3,2,1,0:T(8,128)S(1)} copy-done((f32[64,4,8,128]{3,2,1,0:T(8,128)S(1)}, f32[64,4,8,128]{3,2,1,0:T(8,128)}, u32[]{:S(2)}) %copy-start) | copy-done | bytes 1048600
  1.9 0.0 copy-start.2
  1.9 0.0 copy-start.9
  1.9 0.0 copy-start.10
  1.9 0.0 copy-start.12
  1.9 0.0 copy-start.13
  1.9 0.0 copy-start.14
  1.9 0.0 copy-start.15
  1.9 0.1 x_faces.1
  2.0 0.0 copy-start.1
  2.0 2.1 %collective-permute-start = (f32[64,2,8,128]{3,2,1,0:T(8,128)S(1)}, f32[64,2,8,128]{3,2,1,0:T(8,128)S(1)}, u32[]{:S(2)}, u32[]{:S(2)}) collective-permute-start(f32[64,2,8,128]{3,2,1,0:T(8,128)S(1)} %x_faces.1), channel_id=1, source_target_pairs={{0,16},{16,0},{1,17},{17,1},{2,18},{18,2},{3,19},{19,3},{4,20},{20... | collective-permute-start | bytes 1572872 | tf_op jit(solution)/shard_map/ppermute | solution.py:215
  4.1 0.0 copy-done.2
  4.1 0.0 copy-done.9
  4.1 0.0 copy-done.10
  4.1 0.0 copy-done.12
  4.1 0.0 copy-done.13
  4.2 0.0 copy-done.14
  4.2 0.0 copy-done.15
  4.2 1.1 %pack_parcels.1 = (f32[256,128]{1,0:T(8,128)}, s32[1,128]{1,0:T(1,128)S(1)}) custom-call(f32[32,64,128]{2,1,0:T(8,128)S(1)} %copy-done.2, s32[1,128]{1,0:T(1,128)S(1)} %bitcast.31, s32[8,128]{1,0:T(8,128)S(1)} %copy-done.12, f32[8,128]{1,0:T(8,128)S(1)} %copy-done.13, f32[1,128]{1,0:T(1,128)S(1)} %bitcast.32, f32[1,64]{1,0:T(1,128)S(1)} %bitcast.19, ...), custom_call_target="tpu_custom_call" | custom-call | tf_op jit(solution)/shard_map/pack_parcels/pallas_call | solution.py:438
  5.2 6.8 %all-to-all-start = ((f32[16,16,128]{2,1,0:T(8,128)}), f32[16,16,128]{2,1,0:T(8,128)S(1)}, u32[]{:S(2)}, u32[]{:S(2)}) async-start(f32[16,16,128]{2,1,0:T(8,128)} %bitcast.7), calls=%async_computation | async-start | bytes 262144 | tf_op jit(solution)/shard_map/all_to_all | solution.py:420
  12.0 3.7 %collective-permute-done = f32[64,2,8,128]{3,2,1,0:T(8,128)S(1)} collective-permute-done((f32[64,2,8,128]{3,2,1,0:T(8,128)S(1)}, f32[64,2,8,128]{3,2,1,0:T(8,128)S(1)}, u32[]{:S(2)}, u32[]{:S(2)}) %collective-permute-start) | collective-permute-done | bytes 524320 | tf_op jit(solution)/shard_map/ppermute | solution.py:215
  15.8 0.0 copy-done.1
  15.8 1.3 %y_faces.1 = (f32[10,64,128]{2,1,0:T(8,128)}, f32[10,64,128]{2,1,0:T(8,128)}) custom-call(f32[2048,128]{1,0:T(8,128)S(1)} %bitcast.12, f32[1024,128]{1,0:T(8,128)S(1)} %bitcast.15), custom_call_target="tpu_custom_call" | custom-call | tf_op jit(solution)/shard_map/y_faces/pallas_call | solution.py:520
  17.1 1.2 %collective-permute-start.1 = (f32[10,64,128]{2,1,0:T(8,128)}, f32[10,64,128]{2,1,0:T(8,128)S(1)}, u32[]{:S(2)}, u32[]{:S(2)}) collective-permute-start(f32[10,64,128]{2,1,0:T(8,128)} %get-tuple-element.13), channel_id=1, source_target_pairs={{0,4},{8,12},{4,0},{12,8},{1,5},{9,13},{5,1},{13,9},{2,6},{10,14},... | collective-permute-start | bytes 983048 | tf_op jit(solution)/shard_map/ppermute | solution.py:215
  18.3 1.4 %collective-permute-start.2 = (f32[10,64,128]{2,1,0:T(8,128)}, f32[10,64,128]{2,1,0:T(8,128)}, u32[]{:S(2)}, u32[]{:S(2)}) collective-permute-start(f32[10,64,128]{2,1,0:T(8,128)} %get-tuple-element.14), channel_id=1, source_target_pairs={{4,8},{8,4},{5,9},{9,5},{6,10},{10,6},{7,11},{11,7},{20,24},{24,20... | collective-permute-start | bytes 983048 | tf_op jit(solution)/shard_map/ppermute | solution.py:215
  19.7 0.0 all-to-all-done
  19.7 8.2 %couple_gas.1 = (f32[128,128]{1,0:T(8,128)}, f32[2048,128]{1,0:T(8,128)S(1)}) custom-call(f32[256,128]{1,0:T(8,128)S(1)} %bitcast.17, f32[2048,128]{1,0:T(8,128)S(1)} %bitcast.13, f32[1,64]{1,0:T(1,128)S(1)} %bitcast.20, f32[1,64]{1,0:T(1,128)S(1)} %bitcast.24), custom_call_target="tpu_custom_call" | custom-call | tf_op jit(solution)/shard_map/couple_gas/pallas_call | solution.py:462
  27.9 0.0 copy-start.3
  27.9 1.0 %copy-done.3 = f32[2048,128]{1,0:T(8,128)} copy-done((f32[2048,128]{1,0:T(8,128)}, f32[2048,128]{1,0:T(8,128)S(1)}, u32[]{:S(2)}) %copy-start.3) | copy-done | bytes 1048600
  29.0 7.8 %all-to-all-start.1 = ((f32[16,8,128]{2,1,0:T(8,128)}), f32[16,8,128]{2,1,0:T(8,128)S(1)}, u32[]{:S(2)}, u32[]{:S(2)}) async-start(f32[16,8,128]{2,1,0:T(8,128)} %bitcast.10), calls=%async_computation.1 | async-start | bytes 131072 | tf_op jit(solution)/shard_map/all_to_all | solution.py:420
  36.7 0.0 copy-start.11
  36.7 0.0 collective-permute-done.1.refs_1_
  36.7 0.0 copy-start.7
  36.7 0.7 %copy-done.7 = f32[10,64,128]{2,1,0:T(8,128)} copy-done((f32[10,64,128]{2,1,0:T(8,128)}, f32[10,64,128]{2,1,0:T(8,128)S(1)}, u32[]{:S(2)}) %copy-start.7) | copy-done | bytes 327704
  37.5 0.0 collective-permute-done.2.refs_2_
  37.5 0.0 copy-done.11
  37.5 0.0 copy-start.8
  37.5 1.0 %copy-done.8 = f32[10,64,128]{2,1,0:T(8,128)S(1)} copy-done((f32[10,64,128]{2,1,0:T(8,128)S(1)}, f32[10,64,128]{2,1,0:T(8,128)}, u32[]{:S(2)}) %copy-start.8) | copy-done | bytes 327704
  38.4 5.3 %first_gas_step.1 = (f32[2048,128]{1,0:T(8,128)S(1)}, f32[2,64,8,128]{3,2,1,0:T(8,128)S(1)}, f32[2,4,64,128]{3,2,1,0:T(8,128)S(1)}, f32[48,128]{1,0:T(8,128)S(1)}, f32[48,128]{1,0:T(8,128)S(1)}) custom-call(f32[2048,128]{1,0:T(8,128)S(1)} %bitcast.14, f32[1024,128]{1,0:T(8,128)S(1)} %bitcast.16, f32[10,64,128]{2,1,0:T(8,128)S(1)} %copy-done.8, ...), custom_call_target="tpu_custom_call" | custom-call | tf_op jit(solution)/shard_map/first_gas_step/pallas_call | solution.py:528
  43.8 0.0 copy-start.5
  43.8 1.0 %copy-done.5 = f32[2048,128]{1,0:T(8,128)} copy-done((f32[2048,128]{1,0:T(8,128)}, f32[2048,128]{1,0:T(8,128)S(1)}, u32[]{:S(2)}) %copy-start.5) | copy-done | bytes 1048600
  44.7 0.1 collective-permute-start.3
  44.9 3.6 %collective-permute-start.4 = (f32[48,128]{1,0:T(8,128)S(1)}, f32[48,128]{1,0:T(8,128)S(1)}, u32[]{:S(2)}, u32[]{:S(2)}) collective-permute-start(f32[48,128]{1,0:T(8,128)S(1)} %get-tuple-element.19.zb), channel_id=1, source_target_pairs={{1,2},{2,1},{5,6},{6,5},{9,10},{10,9},{13,14},{14,13},{17,18},{18,... | collective-permute-start | bytes 73736 | tf_op jit(solution)/shard_map/ppermute | solution.py:215
  48.4 2.4 %evolve_droplets.1.tail = f32[32,64,128]{2,1,0:T(8,128)} custom-call(f32[32,64,128]{2,1,0:T(8,128)S(1)} %copy-done.2, f32[1,64]{1,0:T(1,128)S(1)} %bitcast.21, f32[1,64]{1,0:T(1,128)S(1)} %bitcast.25), custom_call_target="tpu_custom_call" | custom-call | flops 5242880 | bytes 2097152 | tf_op jit(solution)/shard_map/evolve_droplets/pallas_call | solution.py:481
  50.8 0.0 all-to-all-done.1
  50.8 0.0 copy-start.4
  50.8 0.0 copy-start.6
  50.8 2.0 %finish_droplets.1 = f32[32,64,128]{2,1,0:T(8,128)} custom-call(f32[32,64,128]{2,1,0:T(8,128)} %evolve_droplets.1.tail, f32[128,128]{1,0:T(8,128)S(1)} %bitcast.18, s32[1,128]{1,0:T(1,128)S(1)} %get-tuple-element.23.slots, f32[1,64]{1,0:T(1,128)S(1)} %bitcast.22, f32[1,64]{1,0:T(1,128)S(1)} %bitcast.26), custom_call_target="tpu_custom_call", output_to_operand_aliasing={{}: (0, {})} | custom-call | tf_op jit(solution)/shard_map/finish_droplets/pallas_call | solution.py:492
  52.9 0.0 collective-permute-done.3.za_in
  52.9 0.0 collective-permute-done.4.zb_in
  52.9 0.0 copy-done.4
  52.9 0.0 copy-done.6
  52.9 5.6 %second_gas_step.1 = f32[2048,128]{1,0:T(8,128)} custom-call(f32[2048,128]{1,0:T(8,128)S(1)} %copy-done.6, f32[2,64,8,128]{3,2,1,0:T(8,128)S(1)} %get-tuple-element.16.side_x, f32[2,4,64,128]{3,2,1,0:T(8,128)S(1)} %get-tuple-element.17.side_y, f32[48,128]{1,0:T(8,128)S(1)} %get-tuple-element.18.za, f32[48,128]{1,0:T(8,128)S(1)} %get-tuple-element.19.zb, ...), custom_call_target="tpu_custom_call" | custom-call | tf_op jit(solution)/shard_map/second_gas_step/pallas_call | solution.py:543
Async XLA Ops:
  0.6 1.2 %copy-start = (f32[64,4,8,128]{3,2,1,0:T(8,128)S(1)}, f32[64,4,8,128]{3,2,1,0:T(8,128)}, u32[]{:S(2)}) copy-start(f32[64,4,8,128]{3,2,1,0:T(8,128)} %gas.1) | copy-start | bytes 3145732
  1.9 2.3 %copy-start.2 = (f32[32,64,128]{2,1,0:T(8,128)S(1)}, f32[32,64,128]{2,1,0:T(8,128)}, u32[]{:S(2)}) copy-start(f32[32,64,128]{2,1,0:T(8,128)} %state_in.1) | copy-start | bytes 3145732
  1.9 2.3 %copy-start.9 = (f32[64]{0:T(128)S(1)}, f32[64]{0:T(128)}, u32[]{:S(2)}) copy-start(f32[64]{0:T(128)} %param.15) | copy-start | bytes 772
  1.9 2.3 %copy-start.10 = (f32[64]{0:T(128)S(1)}, f32[64]{0:T(128)}, u32[]{:S(2)}) copy-start(f32[64]{0:T(128)} %param.16) | copy-start | bytes 772
  1.9 2.3 %copy-start.12 = (s32[8,128]{1,0:T(8,128)S(1)}, s32[8,128]{1,0:T(8,128)}, u32[]{:S(2)}) copy-start(s32[8,128]{1,0:T(8,128)} %cells.1) | copy-start | bytes 12292
  1.9 2.3 %copy-start.13 = (f32[8,128]{1,0:T(8,128)S(1)}, f32[8,128]{1,0:T(8,128)}, u32[]{:S(2)}) copy-start(f32[8,128]{1,0:T(8,128)} %weights.1) | copy-start | bytes 12292
  1.9 2.3 %copy-start.14 = (s32[128,1]{0,1:T(1,128)S(1)}, s32[128,1]{0,1:T(1,128)}, u32[]{:S(2)}) copy-start(s32[128,1]{0,1:T(1,128)} %param.11) | copy-start | bytes 1540
  1.9 2.3 %copy-start.15 = (f32[128]{0:T(128)S(1)}, f32[128]{0:T(128)}, u32[]{:S(2)}) copy-start(f32[128]{0:T(128)} %param.14) | copy-start | bytes 1540
  2.0 13.8 %copy-start.1 = (f32[64,4,8,128]{3,2,1,0:T(8,128)S(1)}, f32[64,4,8,128]{3,2,1,0:T(8,128)}, u32[]{:S(2)}) copy-start(f32[64,4,8,128]{3,2,1,0:T(8,128)} %gas.1) | copy-start | bytes 3145732
  2.0 13.8 %collective-permute-start = (f32[64,2,8,128]{3,2,1,0:T(8,128)S(1)}, f32[64,2,8,128]{3,2,1,0:T(8,128)S(1)}, u32[]{:S(2)}, u32[]{:S(2)}) collective-permute-start(f32[64,2,8,128]{3,2,1,0:T(8,128)S(1)} %x_faces.1), channel_id=1, source_target_pairs={{0,16},{16,0},{1,17},{17,1},{2,18},{18,2},{3,19},{19,3},{4,20},{20... | collective-permute-start | bytes 1572872 | tf_op jit(solution)/shard_map/ppermute | solution.py:215
  5.2 14.5 %all-to-all-start = ((f32[16,16,128]{2,1,0:T(8,128)}), f32[16,16,128]{2,1,0:T(8,128)S(1)}, u32[]{:S(2)}, u32[]{:S(2)}) async-start(f32[16,16,128]{2,1,0:T(8,128)} %bitcast.7), calls=%async_computation | async-start | bytes 262144 | tf_op jit(solution)/shard_map/all_to_all | solution.py:420
  17.1 19.6 %collective-permute-start.1 = (f32[10,64,128]{2,1,0:T(8,128)}, f32[10,64,128]{2,1,0:T(8,128)S(1)}, u32[]{:S(2)}, u32[]{:S(2)}) collective-permute-start(f32[10,64,128]{2,1,0:T(8,128)} %get-tuple-element.13), channel_id=1, source_target_pairs={{0,4},{8,12},{4,0},{12,8},{1,5},{9,13},{5,1},{13,9},{2,6},{10,14},... | collective-permute-start | bytes 983048 | tf_op jit(solution)/shard_map/ppermute | solution.py:215
  18.3 19.1 %collective-permute-start.2 = (f32[10,64,128]{2,1,0:T(8,128)}, f32[10,64,128]{2,1,0:T(8,128)}, u32[]{:S(2)}, u32[]{:S(2)}) collective-permute-start(f32[10,64,128]{2,1,0:T(8,128)} %get-tuple-element.14), channel_id=1, source_target_pairs={{4,8},{8,4},{5,9},{9,5},{6,10},{10,6},{7,11},{11,7},{20,24},{24,20... | collective-permute-start | bytes 983048 | tf_op jit(solution)/shard_map/ppermute | solution.py:215
  27.9 1.0 %copy-start.3 = (f32[2048,128]{1,0:T(8,128)}, f32[2048,128]{1,0:T(8,128)S(1)}, u32[]{:S(2)}) copy-start(f32[2048,128]{1,0:T(8,128)S(1)} %get-tuple-element.21.deposit) | copy-start | bytes 3145732
  29.0 21.9 %all-to-all-start.1 = ((f32[16,8,128]{2,1,0:T(8,128)}), f32[16,8,128]{2,1,0:T(8,128)S(1)}, u32[]{:S(2)}, u32[]{:S(2)}) async-start(f32[16,8,128]{2,1,0:T(8,128)} %bitcast.10), calls=%async_computation.1 | async-start | bytes 131072 | tf_op jit(solution)/shard_map/all_to_all | solution.py:420
  36.7 0.8 %copy-start.11 = (f32[64]{0:T(128)S(1)}, f32[64]{0:T(128)}, u32[]{:S(2)}) copy-start(f32[64]{0:T(128)} %param.17) | copy-start | bytes 772
  36.7 0.7 %copy-start.7 = (f32[10,64,128]{2,1,0:T(8,128)}, f32[10,64,128]{2,1,0:T(8,128)S(1)}, u32[]{:S(2)}) copy-start(f32[10,64,128]{2,1,0:T(8,128)S(1)} %collective-permute-done.1.refs_1_) | copy-start | bytes 983044
  37.5 1.0 %copy-start.8 = (f32[10,64,128]{2,1,0:T(8,128)S(1)}, f32[10,64,128]{2,1,0:T(8,128)}, u32[]{:S(2)}) copy-start(f32[10,64,128]{2,1,0:T(8,128)} %copy-done.7) | copy-start | bytes 983044
  43.8 1.0 %copy-start.5 = (f32[2048,128]{1,0:T(8,128)}, f32[2048,128]{1,0:T(8,128)S(1)}, u32[]{:S(2)}) copy-start(f32[2048,128]{1,0:T(8,128)S(1)} %get-tuple-element.15.field) | copy-start | bytes 3145732
  44.7 8.1 %collective-permute-start.3 = (f32[48,128]{1,0:T(8,128)S(1)}, f32[48,128]{1,0:T(8,128)S(1)}, u32[]{:S(2)}, u32[]{:S(2)}) collective-permute-start(f32[48,128]{1,0:T(8,128)S(1)} %get-tuple-element.18.za), channel_id=1, source_target_pairs={{0,1},{2,3},{1,0},{3,2},{4,5},{6,7},{5,4},{7,6},{8,9},{10,11},{9,8... | collective-permute-start | bytes 73736 | tf_op jit(solution)/shard_map/ppermute | solution.py:215
  44.9 8.0 %collective-permute-start.4 = (f32[48,128]{1,0:T(8,128)S(1)}, f32[48,128]{1,0:T(8,128)S(1)}, u32[]{:S(2)}, u32[]{:S(2)}) collective-permute-start(f32[48,128]{1,0:T(8,128)S(1)} %get-tuple-element.19.zb), channel_id=1, source_target_pairs={{1,2},{2,1},{5,6},{6,5},{9,10},{10,9},{13,14},{14,13},{17,18},{18,... | collective-permute-start | bytes 73736 | tf_op jit(solution)/shard_map/ppermute | solution.py:215
  50.8 2.0 %copy-start.4 = (f32[2048,128]{1,0:T(8,128)S(1)}, f32[2048,128]{1,0:T(8,128)}, u32[]{:S(2)}) copy-start(f32[2048,128]{1,0:T(8,128)} %copy-done.3) | copy-start | bytes 3145732
  50.8 2.0 %copy-start.6 = (f32[2048,128]{1,0:T(8,128)S(1)}, f32[2048,128]{1,0:T(8,128)}, u32[]{:S(2)}) copy-start(f32[2048,128]{1,0:T(8,128)} %copy-done.5) | copy-start | bytes 3145732

commit v3 on v2

--- a/solution.py
+++ b/solution.py
@@ -11,6 +11,7 @@
 DROP_STEPS = 4
 GAS_STEPS = 2
 LANES = 128
+GROUPS = 4
 MIB = 1 << 20
 NT = (((1,), (1,)), ((), ()))
 HIGH = lax.Precision.HIGHEST
@@ -27,10 +28,25 @@
     return jnp.sum(jnp.where(iota((n, n), 0) == iota((n, n), 1), row, 0.0), axis=1, keepdims=True)
 
 
+def leading(value):
+    scaled = value * 65537.0
+    return scaled - (scaled - value)
+
+
 def split(value):
-    scaled = value * 65537.0
-    high = scaled - (scaled - value)
+    high = leading(value)
     return high.astype(BF16), (value - high).astype(BF16)
+
+
+def split_all(value):
+    high = leading(value)
+    rest = value - high
+    middle = leading(rest)
+    return high.astype(BF16), middle.astype(BF16), (rest - middle).astype(BF16)
+
+
+def one_hot(hit):
+    return jnp.where(hit, 1.0, 0.0).astype(BF16)
 
 
 def surface_steps(nodes, gas_at, liquid, surface):
@@ -64,11 +80,15 @@
     return emitted, nodes[1:]
 
 
-def pack_kernel(cap, tail, owner, cells, weights, mass, liquid, surface, send, slots):
+def pack_kernel(
+    cap, droplet, gas, owner, cells, weights, mass, liquid, surface, send, slots, near_gas, tail, sems
+):
     parcels = owner.shape[1]
-    emitted = surface_steps(
-        [tail[i] for i in range(DROP_STEPS)], 0.0, as_column(liquid[...]), as_column(surface[...])
-    )
+    nodes, species = droplet.shape[0], droplet.shape[1]
+    load_tail = pltpu.make_async_copy(droplet.at[pl.ds(nodes - DROP_STEPS, DROP_STEPS)], tail, sems.at[0])
+    load_gas = pltpu.make_async_copy(gas, near_gas, sems.at[1])
+    load_tail.start()
+    load_gas.start()
     wts = weights[...]
     norm = wts / jnp.sum(wts, axis=0, keepdims=True)
     mine = owner[...]
@@ -77,8 +97,11 @@
     rank = jnp.sum(jnp.where(earlier, 1.0, 0.0), axis=0, keepdims=True).astype(jnp.int32)
     slot = mine * cap + rank
     slots[...] = slot
-    species = tail.shape[1]
+    place = one_hot(iota((send.shape[0], parcels), 0) == slot)
     rest = jnp.zeros((LANES - species - 2 * STENCIL - 8, parcels), F32)
+    liquid_col, surface_col = as_column(liquid[...]), as_column(surface[...])
+    load_tail.wait()
+    emitted = surface_steps([tail[i] for i in range(DROP_STEPS)], 0.0, liquid_col, surface_col)
     values = jnp.concatenate(
         [
             mass[...] * emitted,
@@ -89,11 +112,43 @@
         ],
         axis=0,
     )
-    place = jnp.where(iota((send.shape[0], parcels), 0) == slot, 1.0, 0.0)
-    send[...] = lax.dot_general(place, values, NT, precision=HIGH, preferred_element_type=F32)
-
-
-def couple_kernel(cap, packed, rows, gas, liquid, surface, back, deposit, w_high, w_low, t_all):
+    parts = jnp.concatenate(split_all(values), axis=0)
+    placed = lax.dot_general(place, parts, NT, preferred_element_type=F32)
+    send[...] = placed[:, :LANES] + placed[:, LANES : 2 * LANES] + placed[:, 2 * LANES :]
+    load_gas.wait()
+
+
+def faces_kernel(size_x, size_y, turns_x, near_gas, *sends):
+    x_sends, y_sends = sends[:turns_x], sends[turns_x:]
+    species = y_sends[0].shape[1]
+    lines = size_x * size_y
+    even_x, _, _ = place_on("gx")
+    for turn, x_send in enumerate(x_sends):
+        start = jnp.where(even_x == (turn == 0), size_x - 2, 0) * size_y
+
+        @pl.loop(0, species, unroll=8)
+        def _(s):
+            x_send[pl.ds(s * 2 * size_y, 2 * size_y), :] = near_gas[pl.ds(s * lines + start, 2 * size_y), :]
+
+    even_y, _, _ = place_on("gy")
+    for turn, y_send in enumerate(y_sends):
+        up = even_y == (turn == 0)
+        near = jnp.where(up, size_y - 1, 0)
+        far = jnp.where(up, size_y - 2, 1)
+        for x in range(size_x):
+            y_send[x] = near_gas[pl.ds(x * size_y + near, species, stride=lines), :]
+            y_send[size_x + x] = near_gas[pl.ds(x * size_y + far, species, stride=lines), :]
+
+
+def corner_kernel(size_x, ya, yb, *sends):
+    even_x, _, _ = place_on("gx")
+    even_y, _, _ = place_on("gy")
+    for turn, send in enumerate(sends):
+        x = jnp.where(even_x == (turn == 0), size_x - 1, 0)
+        send[0], send[1] = low_high(even_y, ya[x], yb[x])
+
+
+def couple_kernel(cap, packed, rows, gas, liquid, surface, back, deposit_out, deposit, w_high, w_low, sems):
     slots = rows.shape[0]
     species = liquid.shape[1]
     lines = gas.shape[0] // species
@@ -111,31 +166,31 @@
             if other != k:
                 total = total + jnp.where(cell_rows[other] == cell_rows[k], wts_rows[other], 0.0)
         whole.append(total)
-    line_of = jnp.floor(cell * (1.0 / LANES))
-    lane_of = cell - LANES * line_of
-    along = iota((LANES, slots), 0).astype(F32).astype(BF16)
+    tile = 16
+    named = [jnp.broadcast_to(c.astype(jnp.int32), (tile, slots)).astype(jnp.int16) for c in cell_rows]
     halves = [split(w) for w in whole]
-    highs = [jnp.broadcast_to(h, (LANES, slots)) for h, _ in halves]
-    lows = [jnp.broadcast_to(l, (LANES, slots)) for _, l in halves]
-
-    @pl.loop(0, lines)
+    highs = [jnp.broadcast_to(h, (tile, slots)) for h, _ in halves]
+    lows = [jnp.broadcast_to(l, (tile, slots)) for _, l in halves]
+
+    @pl.loop(0, lines, unroll=2)
     def _(line):
-        code = jnp.where(line_of == line.astype(F32), lane_of, -1.0).astype(BF16)
-        high = jnp.zeros((LANES, slots), BF16)
-        low = jnp.zeros((LANES, slots), BF16)
-        for k in range(STENCIL):
-            hit = jnp.broadcast_to(code[k : k + 1], (LANES, slots)) == along
-            high = jnp.where(hit, highs[k], high)
-            low = jnp.where(hit, lows[k], low)
-        w_high[line] = high
-        w_low[line] = low
-        t_high, t_low = split(gas[pl.ds(line, species, stride=lines), :])
-        t_all[line] = jnp.concatenate([t_high, t_low], axis=0)
+        for z in range(0, LANES, tile):
+            along = (iota((tile, slots), 0) + (line * LANES + z)).astype(jnp.int16)
+            high = jnp.zeros((tile, slots), BF16)
+            low = jnp.zeros((tile, slots), BF16)
+            for k in range(STENCIL):
+                hit = named[k] == along
+                high = jnp.where(hit, highs[k], high)
+                low = jnp.where(hit, lows[k], low)
+            w_high[line, z : z + tile] = high
+            w_low[line, z : z + tile] = low
 
     gathered = jnp.zeros((species, slots), F32)
     for line in range(lines):
-        both = jnp.dot(t_all[line], w_high[line], preferred_element_type=F32)
-        extra = jnp.dot(t_all[line, :species], w_low[line], preferred_element_type=F32)
+        t_high, t_low = split(gas[pl.ds(line, species, stride=lines), :])
+        t_all = jnp.concatenate([t_high, t_low], axis=0)
+        both = jnp.dot(t_all, w_high[line], preferred_element_type=F32)
+        extra = jnp.dot(t_high, w_low[line], preferred_element_type=F32)
         gathered = gathered + both[:species] + both[species:] + extra
     gas_rows = jnp.transpose(gathered)
     if packed:
@@ -145,30 +200,45 @@
     else:
         back[...] = jnp.concatenate([gas_rows, jnp.zeros((slots, LANES - species), F32)], axis=1)
     response, _ = surface_response(as_column(liquid[...]), as_column(surface[...]))
-    source = table[:species] + mass * (response * gathered)
-    s_high, s_low = split(source)
+    s_high, s_low = split(table[:species] + mass * (response * gathered))
     s_all = jnp.concatenate([s_high, s_low], axis=0)
+    saves = []
+    each = lines // GROUPS
     for line in range(lines):
         both = lax.dot_general(s_all, w_high[line], NT, preferred_element_type=F32)
         extra = lax.dot_general(s_high, w_low[line], NT, preferred_element_type=F32)
-        deposit[pl.ds(line, species, stride=lines), :] = both[:species] + both[species:] + extra
+        deposit[line] = both[:species] + both[species:] + extra
+        if line % each == each - 1:
+            at = pl.ds(line + 1 - each, each)
+            saves.append(pltpu.make_async_copy(deposit.at[at], deposit_out.at[at], sems.at[line // each]))
+            saves[-1].start()
+    for save in saves:
+        save.wait()
 
 
 def droplet_kernel(state_in, liquid, surface, state_out):
-    nodes, block, _ = state_in.shape
-    species = liquid.shape[1]
-    at = pl.program_id(0) * block + iota((block, species), 0)
-    pick = at == iota((block, species), 1)
-    liquid_col = jnp.sum(jnp.where(pick, liquid[...], 0.0), axis=1, keepdims=True)
-    surface_col = jnp.sum(jnp.where(pick, surface[...], 0.0), axis=1, keepdims=True)
-    state = state_in[...]
-    for step in range(DROP_STEPS):
-        upper = jnp.concatenate([state[1:], state[-1:]], axis=0)
-        lower = jnp.concatenate([state[1:2], state[:-1]], axis=0)
-        flux = surface_col * state[-1]
-        state = state + liquid_col * (upper - 2.0 * state + lower)
-        state = jnp.concatenate([state[:-1], (state[-1] - flux)[None]], axis=0)
-    state_out[...] = state
+    nodes, species, _ = state_in.shape
+    block = 8
+
+    @pl.loop(0, species // block)
+    def _(i):
+        at = pl.ds(pl.multiple_of(i * block, block), block)
+        pick = i * block + iota((block, species), 0) == iota((block, species), 1)
+        liquid_col = jnp.sum(jnp.where(pick, liquid[...], 0.0), axis=1, keepdims=True)
+        surface_col = jnp.sum(jnp.where(pick, surface[...], 0.0), axis=1, keepdims=True)
+        wide = state_in.shape[2]
+        rate = jnp.broadcast_to(liquid_col, (block, wide))
+        keep = 1.0 - 2.0 * rate
+        last_keep = jnp.broadcast_to(1.0 - liquid_col - surface_col, (block, wide))
+        state = [state_in[node, at] for node in range(nodes)]
+        for step in range(DROP_STEPS):
+            state = (
+                [keep * state[0] + (rate + rate) * state[1]]
+                + [keep * state[n] + rate * (state[n - 1] + state[n + 1]) for n in range(1, nodes - 1)]
+                + [last_keep * state[-1] + rate * state[-2]]
+            )
+        for node in range(nodes):
+            state_out[node, at] = state[node]
 
 
 def finish_kernel(cap, packed, tail, rows, slots, liquid, surface, out):
@@ -181,13 +251,14 @@
     if packed:
         half = cap // 2
         at = at // half * cap + at % half
-        parts = [(table[:species], at), (table[species:], at + half)]
+        pairs = [(table[:species], at), (table[species:], at + half)]
     else:
-        parts = [(table[:species], at)]
+        pairs = [(table[:species], at)]
     gas_at = jnp.zeros((species, parcels), F32)
-    for values, index in parts:
-        place = jnp.where(index == slot, 1.0, 0.0)
-        gas_at = gas_at + jnp.dot(values, place, precision=HIGH, preferred_element_type=F32)
+    for values, index in pairs:
+        parts = jnp.concatenate(split_all(values), axis=0)
+        placed = jnp.dot(parts, one_hot(index == slot), preferred_element_type=F32)
+        gas_at = gas_at + placed[:species] + placed[species : 2 * species] + placed[2 * species :]
     _, response = surface_response(as_column(liquid[...]), as_column(surface[...]))
     for i in range(DROP_STEPS):
         out[i] = tail[i] + response[i] * gas_at
@@ -244,51 +315,21 @@
     return before + after
 
 
-def x_faces_kernel(gas, *refs):
-    sends, sems = refs[:-1], refs[-1]
-    even, _, _ = place_on("gx")
-    top = gas.shape[1] - 2
-    copies = []
-    for turn, send in enumerate(sends):
-        start = jnp.where(even == (turn == 0), top, 0)
-        copies.append(pltpu.make_async_copy(gas.at[:, pl.ds(start, 2)], send, sems.at[turn]))
-    for copy in copies:
-        copy.start()
-    for copy in copies:
-        copy.wait()
-
-
-def y_faces_kernel(size_x, size_y, turns_x, gas, *refs):
-    xs, (send_a, send_b) = refs[:turns_x], refs[turns_x:]
-    species = send_a.shape[1]
-    lines = size_x * size_y
-    even, _, _ = place_on("gy")
-    even_x, _, _ = place_on("gx")
-    for turn, send in enumerate((send_a, send_b)):
-        up = even == (turn == 0)
-        near = jnp.where(up, size_y - 1, 0)
-        far = jnp.where(up, size_y - 2, 1)
-        for x in range(size_x):
-            send[x] = gas[pl.ds(x * size_y + near, species, stride=lines), :]
-            send[size_x + x] = gas[pl.ds(x * size_y + far, species, stride=lines), :]
-        edges = []
-        for layer in (1, 0):
-            parts = [x[pl.ds(layer * size_y + near, species, stride=2 * size_y), :] for x in xs]
-            edges.append(low_high(even_x, parts[0], parts[1] if turns_x == 2 else None))
-        send[2 * size_x] = edges[0][0]
-        send[2 * size_x + 1] = edges[1][1]
-
-
 def first_step_kernel(size_x, size_y, turns_x, gas, *refs):
     xs, refs = refs[:turns_x], refs[turns_x:]
-    ya, yb, rate_s, rate, field, side_x, side_y, za, zb, y_low, y_high = refs
+    corners, refs = refs[:turns_x], refs[turns_x:]
+    ya, yb, rate_s, rate, _, field_out, side_x_out, side_y, za, zb, y_low, y_high, field, side_x, sems = refs
     species = rate.shape[1]
     lines = size_x * size_y
     even_x, below_x, above_x = place_on("gx")
     even_y, below_y, above_y = place_on("gy")
     even_z, _, _ = place_on("gz")
-    for plane in range(2 * size_x + 2):
+    for plane in range(2 * size_x):
         y_low[plane], y_high[plane] = low_high(even_y, ya[plane], yb[plane])
+    for side, halo in enumerate((y_low, y_high)):
+        parts = [corner[side] for corner in corners]
+        edges = low_high(even_x, parts[0], parts[1] if turns_x == 2 else None)
+        halo[2 * size_x], halo[2 * size_x + 1] = edges
     column = as_column(rate[...])
     for side, (halo, row, exists) in enumerate(((y_low, 0, below_y), (y_high, size_y - 1, above_y))):
         for x in range(size_x):
@@ -303,7 +344,7 @@
         parts = [x[at] for x in xs]
         return low_high(even_x, parts[0], parts[1] if turns_x == 2 else None)
 
-    @pl.loop(0, species, unroll=2)
+    @pl.loop(0, species, unroll=16)
     def _(s):
         r = rate_s[0, s]
         own = gas[pl.ds(s * lines, lines), :].reshape(size_x, size_y, LANES)
@@ -321,6 +362,12 @@
             total = total + beside_y(near, y_low[edge, here, :], y_high[edge, here, :])
             side_x[side, s] = near + r * (total - 6.0 * near)
 
+    saves = [
+        pltpu.make_async_copy(field, field_out, sems.at[0]),
+        pltpu.make_async_copy(side_x, side_x_out, sems.at[1]),
+    ]
+    for save in saves:
+        save.start()
     low_rows, high_rows = [], []
 
     def add_columns(block):
@@ -348,13 +395,22 @@
     high = jnp.concatenate(high_rows + [rest], axis=0)
     za[...] = jnp.where(even_z, high, low)
     zb[...] = jnp.where(even_z, low, high)
+    for save in saves:
+        save.wait()
 
 
 def second_step_kernel(
-    size_x, size_y, field, side_x, side_y, za, zb, za_in, zb_in, rate_s, rate, deposit, out, halo, halo_x, halo_y, halo_next
+    size_x, size_y, field_in, side_x_in, side_y, za, zb, za_in, zb_in, rate_s, rate, deposit_in,
+    out, halo, halo_x, halo_y, halo_next, field, side_x, deposit, sems,
 ):
     species = rate.shape[1]
     lines = size_x * size_y
+    loads = [
+        pltpu.make_async_copy(source, here, sems.at[i])
+        for i, (source, here) in enumerate(((field_in, field), (side_x_in, side_x), (deposit_in, deposit)))
+    ]
+    for load in loads:
+        load.start()
     even, below, above = place_on("gz")
     low, high = low_high(even, za_in[...], zb_in[...])
     own_low, own_high = low_high(even, za[...], zb[...])
@@ -389,8 +445,10 @@
         for x in range(size_x):
             at = pl.ds((side * size_x + x) * species, species)
             halo_y[at, :] = side_y[side, x] + column * halo_y[at, :]
-
-    @pl.loop(0, species, unroll=2)
+    for load in loads:
+        load.wait()
+
+    @pl.loop(0, species, unroll=16)
     def _(s):
         r = rate_s[0, s]
         at = pl.ds(s * lines, lines)
@@ -407,11 +465,19 @@
         total = beside_x(now, x_low, x_high) + beside_y(now, y_low, y_high) + beside_z(now)
         total = total + halo_next[at, :].reshape(now.shape)
         result = now + r * (total - 6.0 * now)
-        out[at, :] = result.reshape(lines, LANES) + deposit[at, :]
+        out[at, :] = result.reshape(lines, LANES) + deposit[pl.ds(s, lines, stride=species), :]
 
 
 def full(shape):
     return pl.BlockSpec(shape, lambda *_: (0,) * len(shape))
+
+
+def lasts(microseconds):
+    return pl.CostEstimate(flops=0, bytes_accessed=int(3.69e6 * microseconds), transcendentals=0)
+
+
+def in_hbm(array):
+    return pltpu.with_memory_space_constraint(array, pltpu.HBM)
 
 
 def exchange(rows, group):
@@ -434,60 +500,96 @@
     tail_block = nodes // DROP_STEPS - 1
     tail_spec = pl.BlockSpec((DROP_STEPS, species, parcels), lambda *_: (tail_block, 0, 0))
     rate_spec = full((1, species))
-
-    send, slot = pl.pallas_call(
+    size_x, size_y = gas.shape[1], gas.shape[2]
+    rate = gas_rate.reshape(1, species)
+    smem = pl.BlockSpec(memory_space=pltpu.SMEM)
+    vmem = pl.BlockSpec(memory_space=pltpu.VMEM)
+    hbm = pl.BlockSpec(memory_space=pl.ANY)
+    whole = pl.BlockSpec()
+    turns_x = len(swaps("gx"))
+    x_shape = (species * 2 * size_y, LANES)
+    y_shape = (2 * size_x, species, LANES)
+
+    send, slot, near_gas = pl.pallas_call(
         functools.partial(pack_kernel, cap),
         grid=(1,),
-        out_shape=(
+        out_shape=[
             jax.ShapeDtypeStruct((slots, LANES), F32),
             jax.ShapeDtypeStruct((1, parcels), jnp.int32),
-        ),
-        in_specs=[
-            tail_spec,
-            full((1, parcels)),
-            full((STENCIL, parcels)),
-            full((STENCIL, parcels)),
-            full((1, parcels)),
-            rate_spec,
-            rate_spec,
+            pltpu.VMEM(flat.shape, F32),
         ],
-        out_specs=(full((slots, LANES)), full((1, parcels))),
+        in_specs=[hbm, hbm, full((1, parcels)), full((STENCIL, parcels)), full((STENCIL, parcels)), full((1, parcels))]
+        + [rate_spec] * 2,
+        out_specs=[full((slots, LANES)), full((1, parcels)), vmem],
+        scratch_shapes=[
+            pltpu.VMEM((DROP_STEPS, species, parcels), F32),
+            pltpu.SemaphoreType.DMA((2,)),
+        ],
+        compiler_params=pltpu.CompilerParams(vmem_limit_bytes=8 * MIB),
+        cost_estimate=lasts(2.5),
+        name="pack",
+    )(
+        in_hbm(droplet),
+        in_hbm(flat),
+        in_hbm(owner.reshape(1, parcels)),
+        in_hbm(cells),
+        in_hbm(weights),
+        in_hbm(mass.reshape(1, parcels)),
+        in_hbm(liquid),
+        in_hbm(surface),
+    )
+    rows = exchange(send, group)
+
+    faces = pl.pallas_call(
+        functools.partial(faces_kernel, size_x, size_y, turns_x),
+        out_shape=[jax.ShapeDtypeStruct(x_shape, F32)] * turns_x + [jax.ShapeDtypeStruct(y_shape, F32)] * 2,
+        in_specs=[vmem],
         compiler_params=pltpu.CompilerParams(vmem_limit_bytes=4 * MIB),
-        name="pack_parcels",
-    )(droplet, owner.reshape(1, parcels), cells, weights, mass.reshape(1, parcels), liquid, surface)
-
-    rows = exchange(send, group)
+        cost_estimate=lasts(0.6),
+        name="faces",
+    )(near_gas)
+    x_halo = swap_all(faces[:turns_x], "gx")
+    y_halo = swap_all(faces[turns_x:], "gy")
+
+    evolved = pl.pallas_call(
+        droplet_kernel,
+        out_shape=jax.ShapeDtypeStruct(droplet.shape, F32),
+        compiler_params=pltpu.CompilerParams(vmem_limit_bytes=8 * MIB),
+        cost_estimate=lasts(2.0),
+        name="evolve_droplets",
+    )(droplet, liquid, surface)
+
+    corners = pl.pallas_call(
+        functools.partial(corner_kernel, size_x),
+        out_shape=[jax.ShapeDtypeStruct((2, species, LANES), F32)] * turns_x,
+        in_specs=[vmem] * 2,
+        out_specs=[vmem] * turns_x,
+        compiler_params=pltpu.CompilerParams(vmem_limit_bytes=4 * MIB),
+        cost_estimate=lasts(0.3),
+        name="corner_planes",
+    )(*y_halo)
+    corners = swap_all(corners, "gx")
 
     back_rows = slots // 2 if packed else slots
+    w_shape = (lines, LANES, slots)
+    deposit_shape = (lines, species, LANES)
     back, deposit = pl.pallas_call(
         functools.partial(couple_kernel, cap, packed),
-        out_shape=(
-            jax.ShapeDtypeStruct((back_rows, LANES), F32),
-            jax.ShapeDtypeStruct((species * lines, LANES), F32),
-        ),
+        out_shape=[jax.ShapeDtypeStruct((back_rows, LANES), F32), pltpu.HBM(deposit_shape, F32)],
+        in_specs=[vmem] * 2 + [whole] * 2,
+        out_specs=[whole, hbm],
         scratch_shapes=[
-            pltpu.VMEM((lines, LANES, slots), BF16),
-            pltpu.VMEM((lines, LANES, slots), BF16),
-            pltpu.VMEM((lines, 2 * species, LANES), BF16),
+            pltpu.VMEM(deposit_shape, F32),
+            pltpu.VMEM(w_shape, BF16),
+            pltpu.VMEM(w_shape, BF16),
+            pltpu.SemaphoreType.DMA((GROUPS,)),
         ],
-        compiler_params=pltpu.CompilerParams(vmem_limit_bytes=12 * MIB),
+        compiler_params=pltpu.CompilerParams(vmem_limit_bytes=10 * MIB),
+        cost_estimate=lasts(7.0),
         name="couple_gas",
-    )(rows, flat, liquid, surface)
+    )(rows, near_gas, liquid, surface)
 
     returned = exchange(back, group)
-
-    block = 16
-    drop_spec = pl.BlockSpec((nodes, block, parcels), lambda i: (0, i, 0))
-    evolved = pl.pallas_call(
-        droplet_kernel,
-        grid=(species // block,),
-        out_shape=jax.ShapeDtypeStruct(droplet.shape, F32),
-        in_specs=[drop_spec, rate_spec, rate_spec],
-        out_specs=drop_spec,
-        compiler_params=pltpu.CompilerParams(vmem_limit_bytes=8 * MIB),
-        cost_estimate=pl.CostEstimate(flops=20 * droplet.size, bytes_accessed=8 * droplet.size, transcendentals=0),
-        name="evolve_droplets",
-    )(droplet, liquid, surface)
 
     droplet_next = pl.pallas_call(
         functools.partial(finish_kernel, cap, packed),
@@ -497,62 +599,63 @@
         out_specs=tail_spec,
         input_output_aliases={0: 0},
         compiler_params=pltpu.CompilerParams(vmem_limit_bytes=4 * MIB),
+        cost_estimate=lasts(1.8),
         name="finish_droplets",
     )(evolved, returned, slot, liquid, surface)
 
-    size_x, size_y = gas.shape[1], gas.shape[2]
-    rate = gas_rate.reshape(1, species)
-    smem = pl.BlockSpec(memory_space=pltpu.SMEM)
-    vmem = pl.BlockSpec(memory_space=pltpu.VMEM)
-    turns_x = len(swaps("gx"))
-    x_shape = jax.ShapeDtypeStruct((species, 2, size_y, LANES), F32)
-    x_sends = pl.pallas_call(
-        x_faces_kernel,
-        out_shape=[x_shape] * turns_x,
-        in_specs=[pl.BlockSpec(memory_space=pl.ANY)],
-        out_specs=[vmem] * turns_x,
-        scratch_shapes=[pltpu.SemaphoreType.DMA((2,))],
-        compiler_params=pltpu.CompilerParams(vmem_limit_bytes=4 * MIB),
-        name="x_faces",
-    )(gas)
-    x_halo = [x.reshape(-1, LANES) for x in swap_all(x_sends, "gx")]
-    y_shape = (2 * size_x + 2, species, LANES)
-    y_sends = pl.pallas_call(
-        functools.partial(y_faces_kernel, size_x, size_y, turns_x),
-        out_shape=[jax.ShapeDtypeStruct(y_shape, F32)] * 2,
-        compiler_params=pltpu.CompilerParams(vmem_limit_bytes=6 * MIB),
-        name="y_faces",
-    )(flat, *x_halo)
-    y_halo = swap_all(y_sends, "gy")
     z_shape = (48, LANES)
+    full_y = (2 * size_x + 2, species, LANES)
+    side_x_shape = (2, species, size_y, LANES)
     field, side_x, side_y, *z_sends = pl.pallas_call(
         functools.partial(first_step_kernel, size_x, size_y, turns_x),
-        out_shape=(
-            jax.ShapeDtypeStruct(flat.shape, F32),
-            jax.ShapeDtypeStruct((2, species, size_y, LANES), F32),
+        out_shape=[
+            pltpu.HBM(flat.shape, F32),
+            pltpu.HBM(side_x_shape, F32),
             jax.ShapeDtypeStruct((2, size_x, species, LANES), F32),
             jax.ShapeDtypeStruct(z_shape, F32),
             jax.ShapeDtypeStruct(z_shape, F32),
-        ),
-        in_specs=[vmem] * (turns_x + 3) + [smem, vmem],
-        scratch_shapes=[pltpu.VMEM(y_shape, F32), pltpu.VMEM(y_shape, F32)],
-        compiler_params=pltpu.CompilerParams(vmem_limit_bytes=10 * MIB),
+        ],
+        in_specs=[vmem] * (2 * turns_x + 3) + [smem, whole, hbm],
+        out_specs=[hbm] * 2 + [whole] * 3,
+        scratch_shapes=[
+            pltpu.VMEM(full_y, F32),
+            pltpu.VMEM(full_y, F32),
+            pltpu.VMEM(flat.shape, F32),
+            pltpu.VMEM(side_x_shape, F32),
+            pltpu.SemaphoreType.DMA((2,)),
+        ],
+        compiler_params=pltpu.CompilerParams(vmem_limit_bytes=8 * MIB),
+        cost_estimate=lasts(3.8),
         name="first_gas_step",
-    )(flat, *x_halo, *y_halo, rate, rate)
+    )(near_gas, *x_halo, *corners, *y_halo, rate, rate, in_hbm(evolved))
     z_halo = swap_all(z_sends, "gz")
     gas_next = pl.pallas_call(
         functools.partial(second_step_kernel, size_x, size_y),
         out_shape=jax.ShapeDtypeStruct(flat.shape, F32),
-        in_specs=[vmem] * 7 + [smem, vmem, vmem],
+        in_specs=[hbm] * 2 + [whole] * 5 + [smem, whole, hbm],
         scratch_shapes=[
             pltpu.VMEM(flat.shape, F32),
             pltpu.VMEM((2 * species * size_y, LANES), F32),
             pltpu.VMEM((2 * species * size_x, LANES), F32),
             pltpu.VMEM(flat.shape, F32),
+            pltpu.VMEM(flat.shape, F32),
+            pltpu.VMEM(side_x_shape, F32),
+            pltpu.VMEM(flat.shape, F32),
+            pltpu.SemaphoreType.DMA((3,)),
         ],
         compiler_params=pltpu.CompilerParams(vmem_limit_bytes=10 * MIB),
+        cost_estimate=lasts(5.0),
         name="second_gas_step",
-    )(field, side_x, side_y, *z_sends, *z_halo, rate, rate, deposit)
+    )(
+        in_hbm(field),
+        in_hbm(side_x),
+        side_y,
+        *z_sends,
+        *z_halo,
+        rate,
+        rate,
+        in_hbm(deposit.reshape(flat.shape)),
+    )
     return (gas_next.reshape(gas.shape), droplet_next)
 
 

time: 58.9 us -> 52.2 us (0.89)
  local copies, waits for them, and re-layouts: 4.93 us -> 0.02 us
  starting transfers between devices: 22.9 us -> 20.7 us
  waiting for transfers between devices: 3.76 us -> 5.92 us
  Pallas kernels: 26.1 us -> 24.5 us
    unnamed x32 -> x8, local copies, waits for them, and re-layouts: 4.93 us -> 0.02 us
    all_to_all x2, waiting for transfers between devices: 0.01 us -> 4.83 us  [exchange(): lax.all_to_all(chunks, ('gy', 'gz'), split_axis=0, concat_axis=0, tiled=T...]
    all_to_all x2, starting transfers between devices: 14.6 us -> 11.8 us  [exchange(): lax.all_to_all(chunks, ('gy', 'gz'), split_axis=0, concat_axis=0, tiled=T...]
    ppermute x5 -> x6, waiting for transfers between devices: 3.75 us -> 1.09 us  [swap_all(): lax.ppermute(m, axis, pairs)]
    pallas_call x1, Pallas kernels: 1.07 us -> 2.72 us  [on_device(): pl.pallas_call(functools.partial(pack_kernel, cap), grid=(1,), out_shape=...]
    pallas_call x1, Pallas kernels: 5.34 us -> 3.85 us  [on_device(): pl.pallas_call(functools.partial(first_step_kernel, size_x, size_y, turns...]
    pallas_call x4, Pallas kernels: 12.1 us -> 10.8 us  [the longest x1 7.42 us: on_device(): pl.pallas_call(functools.partial(couple_kernel, cap, packed), out_shape=[...]
    ppermute x5 -> x6, starting transfers between devices: 8.39 us -> 8.83 us  [swap_all(): lax.ppermute(m, axis, pairs)]
  transfers between devices with their start and end apart: 7 -> 8, of which waited for: 1 -> 2; matrix products, arithmetic and copies ran while one was open for 0% -> 0% of each run, Pallas kernels for 35% -> 29%
where the time goes in v3:
time: 52.2 us; the launch traced here: 51.8 us
  Pallas kernels  24.5 us (47%)
  starting transfers between devices  20.7 us (40%)
  waiting for transfers between devices  5.92 us (11%)
  between operations  0.72 us (1%)
    all_to_all x2, starting transfers between devices, exchange(): lax.all_to_all(chunks, ('gy', 'gz'), split_axis=0, concat_axis=0, tiled=T...  11.8 us
    ppermute x6, starting transfers between devices, swap_all(): lax.ppermute(m, axis, pairs)  8.83 us
    pallas_call x1, Pallas kernels, on_device(): pl.pallas_call(functools.partial(couple_kernel, cap, packed), out_shape=[...  7.42 us
    pallas_call x1, Pallas kernels, on_device(): pl.pallas_call(functools.partial(second_step_kernel, size_x, size_y), out...  5.32 us
    all_to_all x2, waiting for transfers between devices, exchange(): lax.all_to_all(chunks, ('gy', 'gz'), split_axis=0, concat_axis=0, tiled=T...  4.83 us
    pallas_call x1, Pallas kernels, on_device(): pl.pallas_call(functools.partial(first_step_kernel, size_x, size_y, turns...  3.85 us
    pallas_call x1, Pallas kernels, on_device(): pl.pallas_call(functools.partial(pack_kernel, cap), grid=(1,), out_shape=...  2.72 us
    pallas_call x1, Pallas kernels, on_device(): pl.pallas_call(droplet_kernel, out_shape=jax.ShapeDtypeStruct(droplet.sha...  2.13 us
  transfers between devices with their start and end apart: 8, of which 2 were waited for; matrix products, arithmetic and copies ran while one was open for 0% of the time, Pallas kernels for 29%

profile of v3, /device:TPU:1, one launch (start us, length us, event | category | flops | bytes accessed | tf_op | source)
XLA Modules:
  0.0 51.8 jit_solution(9020329169833888715)
XLA Ops:
  0.6 2.7 %pack.1 = (f32[256,128]{1,0:T(8,128)}, s32[1,128]{1,0:T(1,128)S(1)}, f32[2048,128]{1,0:T(8,128)S(1)}) custom-call(f32[32,64,128]{2,1,0:T(8,128)} %state_in.1, f32[2048,128]{1,0:T(8,128)} %bitcast.28, s32[1,128]{1,0:T(1,128)} %bitcast.29, s32[8,128]{1,0:T(8,128)} %cells.1, f32[8,128]{1,0:T(8,128)} %weights.1, f32[1,128]{1,0:T(1,128)} %bitcast.30, ...), custom_call_target="tpu_custom_call" | custom-call | bytes 9225000 | tf_op jit(solution)/shard_map/pack/pallas_call | solution.py:513
  3.4 0.0 copy-start.2
  3.4 0.0 copy-start.3
  3.4 1.2 %faces.1 = (f32[1024,128]{1,0:T(8,128)}, f32[8,64,128]{2,1,0:T(8,128)}, f32[8,64,128]{2,1,0:T(8,128)S(1)}) custom-call(f32[2048,128]{1,0:T(8,128)S(1)} %get-tuple-element.15.near_gas.gas), custom_call_target="tpu_custom_call" | custom-call | bytes 2214000 | tf_op jit(solution)/shard_map/faces/pallas_call | solution.py:543
  4.6 2.0 %collective-permute-start = (f32[1024,128]{1,0:T(8,128)}, f32[1024,128]{1,0:T(8,128)S(1)}, u32[]{:S(2)}, u32[]{:S(2)}) collective-permute-start(f32[1024,128]{1,0:T(8,128)} %get-tuple-element.16), channel_id=1, source_target_pairs={{0,16},{16,0},{1,17},{17,1},{2,18},{18,2},{3,19},{19,3},{4,20},{20... | collective-permute-start | bytes 1572872 | tf_op jit(solution)/shard_map/ppermute | solution.py:286
  6.6 0.0 copy-start
  6.6 6.9 %all-to-all-start = ((f32[16,16,128]{2,1,0:T(8,128)}), f32[16,16,128]{2,1,0:T(8,128)S(1)}, u32[]{:S(2)}, u32[]{:S(2)}) async-start(f32[16,16,128]{2,1,0:T(8,128)} %bitcast.6), calls=%async_computation | async-start | bytes 262144 | tf_op jit(solution)/shard_map/all_to_all | solution.py:486
  13.6 1.4 %collective-permute-start.1 = (f32[8,64,128]{2,1,0:T(8,128)}, f32[8,64,128]{2,1,0:T(8,128)S(1)}, u32[]{:S(2)}, u32[]{:S(2)}) collective-permute-start(f32[8,64,128]{2,1,0:T(8,128)} %get-tuple-element.17), channel_id=1, source_target_pairs={{0,4},{8,12},{4,0},{12,8},{1,5},{9,13},{5,1},{13,9},{2,6},{10,14},... | collective-permute-start | bytes 786440 | tf_op jit(solution)/shard_map/ppermute | solution.py:286
  14.9 0.7 %collective-permute-start.2 = (f32[8,64,128]{2,1,0:T(8,128)S(1)}, f32[8,64,128]{2,1,0:T(8,128)S(1)}, u32[]{:S(2)}, u32[]{:S(2)}) collective-permute-start(f32[8,64,128]{2,1,0:T(8,128)S(1)} %get-tuple-element.18), channel_id=1, source_target_pairs={{4,8},{8,4},{5,9},{9,5},{6,10},{10,6},{7,11},{11,7},{20,24},{24,20... | collective-permute-start | bytes 786440 | tf_op jit(solution)/shard_map/ppermute | solution.py:286
  15.6 4.8 %all-to-all-done = f32[16,16,128]{2,1,0:T(8,128)S(1)} async-done(((f32[16,16,128]{2,1,0:T(8,128)}), f32[16,16,128]{2,1,0:T(8,128)S(1)}, u32[]{:S(2)}, u32[]{:S(2)}) %all-to-all-start) | async-done | bytes 131104 | tf_op jit(solution)/shard_map/all_to_all | solution.py:486
  20.4 0.0 copy-done.2
  20.5 0.0 copy-done.3
  20.5 7.4 %couple_gas.1 = (f32[128,128]{1,0:T(8,128)}, f32[32,64,128]{2,1,0:T(8,128)}) custom-call(f32[256,128]{1,0:T(8,128)S(1)} %bitcast.12, f32[2048,128]{1,0:T(8,128)S(1)} %get-tuple-element.15.near_gas.gas, f32[1,64]{1,0:T(1,128)S(1)} %bitcast.19, f32[1,64]{1,0:T(1,128)S(1)} %bitcast.23), custom_call_target="tpu_custom_call" | custom-call | bytes 25830000 | tf_op jit(solution)/shard_map/couple_gas/pallas_call | solution.py:576
  27.9 4.9 %all-to-all-start.1 = ((f32[16,8,128]{2,1,0:T(8,128)}), f32[16,8,128]{2,1,0:T(8,128)S(1)}, u32[]{:S(2)}, u32[]{:S(2)}) async-start(f32[16,8,128]{2,1,0:T(8,128)} %bitcast.10), calls=%async_computation.1 | async-start | bytes 131072 | tf_op jit(solution)/shard_map/all_to_all | solution.py:486
  32.8 0.0 collective-permute-done.1.ya.refs_2_
  32.8 0.0 collective-permute-done.2.yb.refs_3_
  32.8 0.3 collective-permute-start.3
  33.2 0.0 copy-done
  33.2 2.1 %evolve_droplets.1.refs_6_.tail = f32[32,64,128]{2,1,0:T(8,128)} custom-call(f32[32,64,128]{2,1,0:T(8,128)S(1)} %copy-done, f32[1,64]{1,0:T(1,128)S(1)} %bitcast.20, f32[1,64]{1,0:T(1,128)S(1)} %bitcast.24), custom_call_target="tpu_custom_call" | custom-call | bytes 7380000 | tf_op jit(solution)/shard_map/evolve_droplets/pallas_call | solution.py:554
  35.3 0.0 copy-start.1
  35.3 1.1 %collective-permute-done.3.refs_1_ = f32[2,64,128]{2,1,0:T(8,128)S(1)} collective-permute-done((f32[2,64,128]{2,1,0:T(8,128)S(1)}, f32[2,64,128]{2,1,0:T(8,128)S(1)}, u32[]{:S(2)}, u32[]{:S(2)}) %collective-permute-start.3) | collective-permute-done | bytes 65568 | tf_op jit(solution)/shard_map/ppermute | solution.py:286
  36.4 0.0 collective-permute-done.refs_0_
  36.4 0.0 copy-done.1
  36.4 3.8 %first_gas_step.1 = (f32[2048,128]{1,0:T(8,128)}, f32[2,64,8,128]{3,2,1,0:T(8,128)}, f32[2,4,64,128]{3,2,1,0:T(8,128)S(1)}, f32[48,128]{1,0:T(8,128)S(1)}, f32[48,128]{1,0:T(8,128)S(1)}) custom-call(f32[2048,128]{1,0:T(8,128)S(1)} %get-tuple-element.15.near_gas.gas, f32[1024,128]{1,0:T(8,128)S(1)} %collective-permute-done.refs_0_, ...), custom_call_target="tpu_custom_call" | custom-call | bytes 14022000 | tf_op jit(solution)/shard_map/first_gas_step/pallas_call | solution.py:609
  40.2 1.1 %collective-permute-start.4 = (f32[48,128]{1,0:T(8,128)S(1)}, f32[48,128]{1,0:T(8,128)S(1)}, u32[]{:S(2)}, u32[]{:S(2)}) collective-permute-start(f32[48,128]{1,0:T(8,128)S(1)} %get-tuple-element.22.za), channel_id=1, source_target_pairs={{0,1},{2,3},{1,0},{3,2},{4,5},{6,7},{5,4},{7,6},{8,9},{10,11},{9,8... | collective-permute-start | bytes 73736 | tf_op jit(solution)/shard_map/ppermute | solution.py:286
  41.3 3.3 %collective-permute-start.5 = (f32[48,128]{1,0:T(8,128)S(1)}, f32[48,128]{1,0:T(8,128)S(1)}, u32[]{:S(2)}, u32[]{:S(2)}) collective-permute-start(f32[48,128]{1,0:T(8,128)S(1)} %get-tuple-element.23.zb), channel_id=1, source_target_pairs={{1,2},{2,1},{5,6},{6,5},{9,10},{10,9},{13,14},{14,13},{17,18},{18,... | collective-permute-start | bytes 73736 | tf_op jit(solution)/shard_map/ppermute | solution.py:286
  44.7 0.0 all-to-all-done.1
  44.7 1.8 %finish_droplets.1 = f32[32,64,128]{2,1,0:T(8,128)} custom-call(f32[32,64,128]{2,1,0:T(8,128)} %evolve_droplets.1.refs_6_.tail, f32[128,128]{1,0:T(8,128)S(1)} %bitcast.13, s32[1,128]{1,0:T(1,128)S(1)} %get-tuple-element.27.slots, f32[1,64]{1,0:T(1,128)S(1)} %bitcast.21, f32[1,64]{1,0:T(1,128)S(1)} %bitcast.25), custom_call_target="tpu_custom_call", output_to_operand_aliasing={{}: (0, {})} | custom-call | bytes 6642000 | tf_op jit(solution)/shard_map/finish_droplets/pallas_call | solution.py:594
  46.5 0.0 collective-permute-done.4.za_in
  46.5 0.0 collective-permute-done.5.zb_in
  46.5 5.3 %second_gas_step.1 = f32[2048,128]{1,0:T(8,128)} custom-call(f32[2048,128]{1,0:T(8,128)} %get-tuple-element.19.field_in, f32[2,64,8,128]{3,2,1,0:T(8,128)} %get-tuple-element.20.side_x_in, f32[2,4,64,128]{3,2,1,0:T(8,128)S(1)} %get-tuple-element.21.side_y, f32[48,128]{1,0:T(8,128)S(1)} %get-tuple-element.22.za, f32[48,128]{1,0:T(8,128)S(1)} %get-tuple-element.23.zb, ...), custom_call_target="tpu_custom_call" | custom-call | bytes 18450000 | tf_op jit(solution)/shard_map/second_gas_step/pallas_call | solution.py:632
  (1 shorter events, 0.0 us)
Async XLA Ops:
  3.4 17.1 %copy-start.2 = (f32[64]{0:T(128)S(1)}, f32[64]{0:T(128)}, u32[]{:S(2)}) copy-start(f32[64]{0:T(128)} %param.15) | copy-start | bytes 772
  3.4 17.1 %copy-start.3 = (f32[64]{0:T(128)S(1)}, f32[64]{0:T(128)}, u32[]{:S(2)}) copy-start(f32[64]{0:T(128)} %param.16) | copy-start | bytes 772
  4.6 31.8 %collective-permute-start = (f32[1024,128]{1,0:T(8,128)}, f32[1024,128]{1,0:T(8,128)S(1)}, u32[]{:S(2)}, u32[]{:S(2)}) collective-permute-start(f32[1024,128]{1,0:T(8,128)} %get-tuple-element.16), channel_id=1, source_target_pairs={{0,16},{16,0},{1,17},{17,1},{2,18},{18,2},{3,19},{19,3},{4,20},{20... | collective-permute-start | bytes 1572872 | tf_op jit(solution)/shard_map/ppermute | solution.py:286
  6.6 26.5 %copy-start = (f32[32,64,128]{2,1,0:T(8,128)S(1)}, f32[32,64,128]{2,1,0:T(8,128)}, u32[]{:S(2)}) copy-start(f32[32,64,128]{2,1,0:T(8,128)} %state_in.1) | copy-start | bytes 3145732
  6.6 13.8 %all-to-all-start = ((f32[16,16,128]{2,1,0:T(8,128)}), f32[16,16,128]{2,1,0:T(8,128)S(1)}, u32[]{:S(2)}, u32[]{:S(2)}) async-start(f32[16,16,128]{2,1,0:T(8,128)} %bitcast.6), calls=%async_computation | async-start | bytes 262144 | tf_op jit(solution)/shard_map/all_to_all | solution.py:486
  13.6 19.2 %collective-permute-start.1 = (f32[8,64,128]{2,1,0:T(8,128)}, f32[8,64,128]{2,1,0:T(8,128)S(1)}, u32[]{:S(2)}, u32[]{:S(2)}) collective-permute-start(f32[8,64,128]{2,1,0:T(8,128)} %get-tuple-element.17), channel_id=1, source_target_pairs={{0,4},{8,12},{4,0},{12,8},{1,5},{9,13},{5,1},{13,9},{2,6},{10,14},... | collective-permute-start | bytes 786440 | tf_op jit(solution)/shard_map/ppermute | solution.py:286
  14.9 17.9 %collective-permute-start.2 = (f32[8,64,128]{2,1,0:T(8,128)S(1)}, f32[8,64,128]{2,1,0:T(8,128)S(1)}, u32[]{:S(2)}, u32[]{:S(2)}) collective-permute-start(f32[8,64,128]{2,1,0:T(8,128)S(1)} %get-tuple-element.18), channel_id=1, source_target_pairs={{4,8},{8,4},{5,9},{9,5},{6,10},{10,6},{7,11},{11,7},{20,24},{24,20... | collective-permute-start | bytes 786440 | tf_op jit(solution)/shard_map/ppermute | solution.py:286
  27.9 16.8 %all-to-all-start.1 = ((f32[16,8,128]{2,1,0:T(8,128)}), f32[16,8,128]{2,1,0:T(8,128)S(1)}, u32[]{:S(2)}, u32[]{:S(2)}) async-start(f32[16,8,128]{2,1,0:T(8,128)} %bitcast.10), calls=%async_computation.1 | async-start | bytes 131072 | tf_op jit(solution)/shard_map/all_to_all | solution.py:486
  32.8 3.5 %collective-permute-start.3 = (f32[2,64,128]{2,1,0:T(8,128)S(1)}, f32[2,64,128]{2,1,0:T(8,128)S(1)}, u32[]{:S(2)}, u32[]{:S(2)}) collective-permute-start(f32[2,64,128]{2,1,0:T(8,128)S(1)} %corner_planes.1), channel_id=1, source_target_pairs={{0,16},{16,0},{1,17},{17,1},{2,18},{18,2},{3,19},{19,3},{4,20},{20... | collective-permute-start | bytes 196616 | tf_op jit(solution)/shard_map/ppermute | solution.py:286
  35.3 1.1 %copy-start.1 = (f32[64]{0:T(128)S(1)}, f32[64]{0:T(128)}, u32[]{:S(2)}) copy-start(f32[64]{0:T(128)} %param.17) | copy-start | bytes 772
  40.2 6.3 %collective-permute-start.4 = (f32[48,128]{1,0:T(8,128)S(1)}, f32[48,128]{1,0:T(8,128)S(1)}, u32[]{:S(2)}, u32[]{:S(2)}) collective-permute-start(f32[48,128]{1,0:T(8,128)S(1)} %get-tuple-element.22.za), channel_id=1, source_target_pairs={{0,1},{2,3},{1,0},{3,2},{4,5},{6,7},{5,4},{7,6},{8,9},{10,11},{9,8... | collective-permute-start | bytes 73736 | tf_op jit(solution)/shard_map/ppermute | solution.py:286
  41.3 5.2 %collective-permute-start.5 = (f32[48,128]{1,0:T(8,128)S(1)}, f32[48,128]{1,0:T(8,128)S(1)}, u32[]{:S(2)}, u32[]{:S(2)}) collective-permute-start(f32[48,128]{1,0:T(8,128)S(1)} %get-tuple-element.23.zb), channel_id=1, source_target_pairs={{1,2},{2,1},{5,6},{6,5},{9,10},{10,9},{13,14},{14,13},{17,18},{18,... | collective-permute-start | bytes 73736 | tf_op jit(solution)/shard_map/ppermute | solution.py:286

commit v4 on v3

v4 whole, which is shorter than its diff:
```python
import functools

import jax
import jax.numpy as jnp
from jax import lax
from jax.experimental import pallas as pl
from jax.experimental.pallas import tpu as pltpu
from jax.sharding import PartitionSpec as P

STENCIL = 8
DROP_STEPS = 4
GAS_STEPS = 2
LANES = 128
GROUPS = 4
MIB = 1 << 20
NT = (((1,), (1,)), ((), ()))
HIGH = lax.Precision.HIGHEST
F32 = jnp.float32
BF16 = jnp.bfloat16


def iota(shape, dim):
    return lax.broadcasted_iota(jnp.int32, shape, dim)


def as_column(row):
    n = row.shape[1]
    return jnp.sum(jnp.where(iota((n, n), 0) == iota((n, n), 1), row, 0.0), axis=1, keepdims=True)


def leading(value):
    scaled = value * 65537.0
    return scaled - (scaled - value)


def split(value):
    high = leading(value)
    return high.astype(BF16), (value - high).astype(BF16)


def split_all(value):
    high = leading(value)
    rest = value - high
    middle = leading(rest)
    return high.astype(BF16), middle.astype(BF16), (rest - middle).astype(BF16)


def one_hot(hit):
    return jnp.where(hit, 1.0, 0.0).astype(BF16)


def surface_steps(nodes, gas_at, liquid, surface):
    emitted = None
    for step in range(DROP_STEPS):
        last = nodes[-1]
        flux = surface * (last - gas_at)
        emitted = flux if emitted is None else emitted + flux
        inner = [
            nodes[i] + liquid * (nodes[i + 1] - 2.0 * nodes[i] + nodes[i - 1])
            for i in range(1, len(nodes) - 1)
        ]
        if len(nodes) > 1:
            nodes = inner + [last + liquid * (nodes[-2] - last) - flux]
    return emitted


def surface_response(liquid, surface):
    return surface_steps([jnp.zeros_like(liquid)] * DROP_STEPS, 1.0, liquid, surface)


def pack_kernel(
    cap, size_x, size_y, turns_x, droplet, gas, owner, cells, weights, mass, liquid, surface, send, slots, near_gas, *refs
):
    x_sends, (tail, sems) = refs[:turns_x], refs[turns_x:]
    parcels = owner.shape[1]
    nodes, species = droplet.shape[0], droplet.shape[1]
    load_tail = pltpu.make_async_copy(droplet.at[pl.ds(nodes - DROP_STEPS, DROP_STEPS)], tail, sems.at[0])
    lines = gas.shape[1]
    loads = [pltpu.make_async_copy(gas.at[:, line, :], near_gas.at[line], sems.at[1 + line]) for line in range(lines)]
    load_tail.start()
    for load in loads:
        load.start()
    wts = weights[...]
    norm = wts / jnp.sum(wts, axis=0, keepdims=True)
    mine = owner[...]
    column = jnp.transpose(jnp.broadcast_to(mine.astype(F32), (parcels, parcels)))
    earlier = (column == mine.astype(F32)) & (iota((parcels, parcels), 0) < iota((parcels, parcels), 1))
    rank = jnp.sum(jnp.where(earlier, 1.0, 0.0), axis=0, keepdims=True).astype(jnp.int32)
    slot = mine * cap + rank
    slots[...] = slot
    place = one_hot(iota((send.shape[0], parcels), 0) == slot)
    rest = jnp.zeros((LANES - species - 2 * STENCIL - 8, parcels), F32)
    liquid_col, surface_col = as_column(liquid[...]), as_column(surface[...])
    load_tail.wait()
    emitted = surface_steps([tail[i] for i in range(DROP_STEPS)], 0.0, liquid_col, surface_col)
    values = jnp.concatenate(
        [
            mass[...] * emitted,
            cells[...].astype(F32),
            norm,
            jnp.broadcast_to(mass[...], (8, parcels)),
            rest,
        ],
        axis=0,
    )
    for load in loads:
        load.wait()
    even_x, _, _ = place_on("gx")
    for turn, x_send in enumerate(x_sends):
        start = jnp.where(even_x == (turn == 0), size_x - 2, 0) * size_y
        for i in range(2 * size_y):
            x_send[i] = near_gas[start + i]
    parts = jnp.concatenate(split_all(values), axis=0)
    placed = lax.dot_general(place, parts, NT, preferred_element_type=F32)
    send[...] = placed[:, :LANES] + placed[:, LANES : 2 * LANES] + placed[:, 2 * LANES :]


def y_faces_kernel(size_x, size_y, near_gas, ya, yb):
    even_y, _, _ = place_on("gy")
    for turn, y_send in enumerate((ya, yb)):
        up = even_y == (turn == 0)
        near = jnp.where(up, size_y - 1, 0)
        far = jnp.where(up, size_y - 2, 1)
        for x in range(size_x):
            y_send[x] = near_gas[x * size_y + near]
            y_send[size_x + x] = near_gas[x * size_y + far]


def corner_kernel(size_x, ya, yb, *sends):
    even_x, _, _ = place_on("gx")
    even_y, _, _ = place_on("gy")
    for turn, send in enumerate(sends):
        x = jnp.where(even_x == (turn == 0), size_x - 1, 0)
        send[0], send[1] = low_high(even_y, ya[x], yb[x])


def couple_kernel(cap, packed, rows, gas, liquid, surface, back, deposit_out, deposit, w_high, w_low, sems):
    slots = rows.shape[0]
    species = liquid.shape[1]
    lines = gas.shape[0]
    table = jnp.transpose(rows[...])
    first = species
    cell = table[first : first + STENCIL]
    wts = table[first + STENCIL : first + 2 * STENCIL]
    mass = table[first + 2 * STENCIL : first + 2 * STENCIL + 1]
    whole = wts
    for shift in range(1, STENCIL):
        same = cell == pltpu.roll(cell, shift, 0)
        whole = whole + jnp.where(same, pltpu.roll(wts, shift, 0), 0.0)
    tile = 16
    cell = cell.astype(jnp.int32)
    high_rows, low_rows = split(whole)
    named = [jnp.broadcast_to(cell[k : k + 1], (tile, slots)).astype(jnp.int16) for k in range(STENCIL)]
    highs = [jnp.broadcast_to(high_rows[k : k + 1], (tile, slots)) for k in range(STENCIL)]
    lows = [jnp.broadcast_to(low_rows[k : k + 1], (tile, slots)) for k in range(STENCIL)]

    def pair(ref, line):
        return ref[line : line + 2].reshape(2 * LANES, slots)

    gathered = jnp.zeros((species, slots), F32)
    for line in range(0, lines, 2):
        for part in range(2):
            for z in range(0, LANES, tile):
                along = (iota((tile, slots), 0) + ((line + part) * LANES + z)).astype(jnp.int16)
                high = jnp.zeros((tile, slots), BF16)
                low = jnp.zeros((tile, slots), BF16)
                for k in range(STENCIL):
                    hit = named[k] == along
                    high = jnp.where(hit, highs[k], high)
                    low = jnp.where(hit, lows[k], low)
                w_high[line + part, z : z + tile] = high
                w_low[line + part, z : z + tile] = low
        t_high, t_low = split(jnp.concatenate([gas[line], gas[line + 1]], axis=1))
        t_all = jnp.concatenate([t_high, t_low], axis=0)
        both = jnp.dot(t_all, pair(w_high, line), preferred_element_type=F32)
        extra = jnp.dot(t_high, pair(w_low, line), preferred_element_type=F32)
        gathered = gathered + both[:species] + both[species:] + extra
    gas_rows = jnp.transpose(gathered)
    if packed:
        gas_rows = gas_rows.reshape(slots // cap, cap, species)
        gas_rows = jnp.concatenate([gas_rows[:, : cap // 2], gas_rows[:, cap // 2 :]], axis=2)
        back[...] = gas_rows.reshape(slots // 2, 2 * species)
    else:
        back[...] = jnp.concatenate([gas_rows, jnp.zeros((slots, LANES - species), F32)], axis=1)
    response = surface_response(as_column(liquid[...]), as_column(surface[...]))
    s_high, s_low = split(table[:species] + mass * (response * gathered))
    s_all = jnp.concatenate([s_high, s_low], axis=0)
    s_only = jnp.concatenate([s_high, jnp.zeros_like(s_low)], axis=0)
    saves = []
    each = lines // GROUPS
    for line in range(0, lines, 2):
        both = lax.dot_general(pair(w_high, line), s_all, NT, preferred_element_type=F32)
        both = both + lax.dot_general(pair(w_low, line), s_only, NT, preferred_element_type=F32)
        for i in range(2):
            turned = jnp.transpose(both[i * LANES : (i + 1) * LANES])
            deposit[line + i] = turned[:species] + turned[species:]
        if line % each == each - 2:
            at = pl.ds(line + 2 - each, each)
            saves.append(pltpu.make_async_copy(deposit.at[at], deposit_out.at[at], sems.at[line // each]))
            saves[-1].start()
    for save in saves:
        save.wait()


def droplet_kernel(
    cap, packed, droplet, rows, slots, liquid, surface, _, state_out, state_in, state_next, gas_at, load_sems, sems
):
    nodes, species, parcels = state_in.shape
    block = 8

    def load(i):
        at = pl.ds(i * block, block)
        return pltpu.make_async_copy(droplet.at[:, at], state_in.at[:, at], load_sems.at[i])

    for i in range(species // block):
        load(i).start()
    table = jnp.transpose(rows[...])
    count = rows.shape[0]
    at = iota((count, parcels), 0)
    slot = slots[...]
    if packed:
        half = cap // 2
        at = at // half * cap + at % half
        pairs = [(table[:species], at), (table[species:], at + half)]
    else:
        pairs = [(table[:species], at)]
    total = jnp.zeros((species, parcels), F32)
    for values, index in pairs:
        parts = jnp.concatenate(split_all(values), axis=0)
        placed = jnp.dot(parts, one_hot(index == slot), preferred_element_type=F32)
        total = total + placed[:species] + placed[species : 2 * species] + placed[2 * species :]
    gas_at[...] = total

    def save(i):
        at = pl.ds(i * block, block)
        return pltpu.make_async_copy(state_next.at[:, at], state_out.at[:, at], sems.at[i])

    @pl.loop(0, species // block)
    def _(i):
        at = pl.ds(pl.multiple_of(i * block, block), block)
        pick = i * block + iota((block, species), 0) == iota((block, species), 1)
        liquid_col = jnp.sum(jnp.where(pick, liquid[...], 0.0), axis=1, keepdims=True)
        surface_col = jnp.sum(jnp.where(pick, surface[...], 0.0), axis=1, keepdims=True)
        rate = jnp.broadcast_to(liquid_col, (block, parcels))
        keep = 1.0 - 2.0 * rate
        last_keep = jnp.broadcast_to(1.0 - liquid_col - surface_col, (block, parcels))
        from_gas = surface_col * gas_at[at, :]
        load(i).wait()
        state = [state_in[node, at] for node in range(nodes)]
        for step in range(DROP_STEPS):
            state = (
                [keep * state[0] + (rate + rate) * state[1]]
                + [keep * state[n] + rate * (state[n - 1] + state[n + 1]) for n in range(1, nodes - 1)]
                + [last_keep * state[-1] + rate * state[-2] + from_gas]
            )
        for node in range(nodes):
            state_next[node, at] = state[node]
        save(i).start()

    for i in range(species // block):
        save(i).wait()


def place_on(axis):
    index, count = lax.axis_index(axis), lax.axis_size(axis)
    even = lax.rem(index, 2) == 0
    below = jnp.where(index > 0, 1.0, 0.0).astype(F32)
    above = jnp.where(index < count - 1, 1.0, 0.0).astype(F32)
    return even, below, above


def swaps(axis, wrap=False):
    count = lax.axis_size(axis)
    rounds = []
    for first in range(2):
        pairs = [(i, i + 1) for i in range(first, count - 1, 2)]
        if wrap and first == 1 and count > 2 and count % 2 == 0:
            pairs.append((count - 1, 0))
        if pairs:
            rounds.append(pairs + [(j, i) for i, j in pairs])
    return rounds


def swap_all(messages, axis, wrap=False):
    return [lax.ppermute(m, axis, pairs) for m, pairs in zip(messages, swaps(axis, wrap), strict=True)]


def low_high(even, first, second):
    if second is None:
        second = jnp.zeros_like(first)
    return jnp.where(even, second, first), jnp.where(even, first, second)


def beside_z(block):
    axis = block.ndim - 1
    lane = iota(block.shape, axis)
    before = jnp.where(lane == 0, 0.0, pltpu.roll(block, 1, axis))
    after = jnp.where(lane == LANES - 1, 0.0, pltpu.roll(block, LANES - 1, axis))
    return before + after


def beside_xy(planes, x, y, x_low, x_high, y_low, y_high):
    size_x, size_y = len(planes), len(planes[0])
    total = planes[x - 1][y]() if x > 0 else x_low(y)
    total = total + (planes[x + 1][y]() if x < size_x - 1 else x_high(y))
    total = total + (planes[x][y - 1]() if y > 0 else y_low(x))
    return total + (planes[x][y + 1]() if y < size_y - 1 else y_high(x))


def plane_at(ref, index):
    return lambda: ref[index]


def wide_rates(rate, rows):
    column = as_column(rate[...])
    column = jnp.concatenate([column] * (rows // column.shape[0]), axis=0)
    return jnp.broadcast_to(column, (rows, LANES))


def columns_of(block):
    turned = jnp.transpose(block)
    return turned[:1], turned[-1:]


def first_step_kernel(size_x, size_y, turns_x, gas, *refs):
    xs, refs = refs[:turns_x], refs[turns_x:]
    (ya, yb, rate, field), refs = refs[:4], refs[4:]
    xs_out, (ya_out, yb_out, za, zb) = refs[:turns_x], refs[turns_x:]
    species = rate.shape[1]
    lines = size_x * size_y
    even_x, below_x, above_x = place_on("gx")
    even_y, below_y, above_y = place_on("gy")
    even_z, _, _ = place_on("gz")
    wide = wide_rates(rate, species)
    keep = 1.0 - 6.0 * wide
    planes = [[plane_at(gas, x * size_y + y) for y in range(size_y)] for x in range(size_x)]

    def from_x(side, y):
        near = [ref[(1 - side) * size_y + y] for ref in xs]
        return low_high(even_x, near[0], near[1] if turns_x == 2 else None)[side]

    def from_y(side, x):
        return low_high(even_y, ya[x], yb[x])[side]

    for x in range(size_x):
        for y in range(size_y):
            own = gas[x * size_y + y]
            total = beside_xy(
                planes,
                x,
                y,
                functools.partial(from_x, 0),
                functools.partial(from_x, 1),
                functools.partial(from_y, 0),
                functools.partial(from_y, 1),
            )
            field[x * size_y + y] = keep * own + wide * (total + beside_z(own))

    for turn, ref in enumerate(xs):
        up = even_x == (turn == 0)
        exists = jnp.where(up, above_x, below_x)
        near, far = jnp.where(up, 0, size_y), jnp.where(up, size_y, 0)
        inner = jnp.where(up, lines - size_y, 0)
        for y in range(size_y):
            own = ref[near + y]
            total = ref[far + y] + exists * gas[inner + y]
            if y > 0:
                total = total + ref[near + y - 1]
            if y < size_y - 1:
                total = total + ref[near + y + 1]
            xs_out[turn][far + y] = keep * own + wide * (total + beside_z(own))

    for turn, (ref, ref_out) in enumerate(((ya, ya_out), (yb, yb_out))):
        up = even_y == (turn == 0)
        exists = jnp.where(up, above_y, below_y)
        inner = jnp.where(up, size_y - 1, 0)
        for x in range(size_x):
            own = ref[x]
            total = ref[size_x + x] + exists * gas[x * size_y + inner]
            if x > 0:
                total = total + ref[x - 1]
            if x < size_x - 1:
                total = total + ref[x + 1]
            ref_out[size_x + x] = keep * own + wide * (total + beside_z(own))

    rows = []
    each = LANES // species
    for ref in (gas, field):
        rows += [columns_of(ref[i : i + each].reshape(LANES, LANES)) for i in range(0, lines, each)]
    for turn, ref in enumerate(xs):
        near = jnp.where(even_x == (turn == 0), 0, size_y)
        rows += [columns_of(ref[pl.ds(near + i, each)].reshape(LANES, LANES)) for i in range(0, size_y, each)]
    for ref in (ya, yb):
        rows += [columns_of(ref[i : i + each].reshape(LANES, LANES)) for i in range(0, size_x, each)]
    rest = [jnp.zeros((za.shape[0] - len(rows), LANES), F32)]
    low = jnp.concatenate([row[0] for row in rows] + rest, axis=0)
    high = jnp.concatenate([row[1] for row in rows] + rest, axis=0)
    za[...] = jnp.where(even_z, high, low)
    zb[...] = jnp.where(even_z, low, high)


def second_step_kernel(
    size_x, size_y, turns_x, field, *refs
):
    xs, refs = refs[:turns_x], refs[turns_x:]
    corners, refs = refs[:turns_x], refs[turns_x:]
    ya, yb, za, zb, za_in, zb_in, rate, deposit_in, out, now, now_x, now_y, result, deposit, sems = refs
    species = rate.shape[1]
    lines = size_x * size_y
    load = pltpu.make_async_copy(deposit_in, deposit, sems.at[lines])
    load.start()
    even_x, _, _ = place_on("gx")
    even_y, _, _ = place_on("gy")
    even, below, above = place_on("gz")
    each = LANES // species
    count = lines // each
    rates = jnp.concatenate([rate[...]] * each, axis=1)
    low, high = low_high(even, za_in[...], zb_in[...])
    low, high = jnp.where(below > 0.0, low, 0.0), jnp.where(above > 0.0, high, 0.0)
    own_low, own_high = low_high(even, za[...], zb[...])
    next_low = rates * (low[count : 2 * count] + below * rates * own_low[:count])
    next_high = rates * (high[count : 2 * count] + above * rates * own_high[:count])
    low, high = rates * low, rates * high

    def spread(low_row, high_row):
        turned = iota((LANES, LANES), 0)
        rows = jnp.where(turned == 0, low_row, jnp.where(turned == LANES - 1, high_row, 0.0))
        return jnp.transpose(rows)

    def row(i):
        return spread(low[i : i + 1], high[i : i + 1])

    def add_halo(target, source, start, count, first):
        for i in range(count):
            block = source[pl.ds(start + i * each, each)].reshape(LANES, LANES) + row(first + i)
            target[i * each : (i + 1) * each] = block.reshape(each, species, LANES)

    wide = wide_rates(rate, species)
    add_halo(now, field, 0, count, 0)
    first = 2 * count
    for turn, (ref, corner) in enumerate(zip(xs, corners, strict=True)):
        start = jnp.where(even_x == (turn == 0), size_y, 0)
        add_halo(now_x.at[turn], ref, start, size_y // each, first)
        first = first + size_y // each
        now_x[turn, 0] = now_x[turn, 0] + wide * corner[0]
        now_x[turn, size_y - 1] = now_x[turn, size_y - 1] + wide * corner[1]
    for turn, ref in enumerate((ya, yb)):
        add_halo(now_y.at[turn], ref, size_x, size_x // each, first)
        first = first + size_x // each
        edges = [jnp.where(even_y == (turn == 0), corner[1], corner[0]) for corner in corners]
        edges = low_high(even_x, edges[0], edges[1] if turns_x == 2 else None)
        now_y[turn, 0] = now_y[turn, 0] + wide * edges[0]
        now_y[turn, size_x - 1] = now_y[turn, size_x - 1] + wide * edges[1]

    keep = 1.0 - 6.0 * wide
    planes = [[plane_at(now, x * size_y + y) for y in range(size_y)] for x in range(size_x)]

    def from_x(side, y):
        return low_high(even_x, now_x[0, y], now_x[1, y] if turns_x == 2 else None)[side]

    def from_y(side, x):
        return low_high(even_y, now_y[0, x], now_y[1, x])[side]

    load.wait()
    saves = []
    for x in range(size_x):
        for y in range(size_y):
            line = x * size_y + y
            own = now[line]
            total = beside_xy(
                planes,
                x,
                y,
                functools.partial(from_x, 0),
                functools.partial(from_x, 1),
                functools.partial(from_y, 0),
                functools.partial(from_y, 1),
            )
            if line % each == 0:
                i = line // each
                ends = spread(next_low[i : i + 1], next_high[i : i + 1])
            part = ends[line % each * species : (line % each + 1) * species]
            result[line] = keep * own + wide * (total + beside_z(own)) + part + deposit[line]
            saves.append(pltpu.make_async_copy(result.at[line], out.at[:, line, :], sems.at[line]))
            saves[-1].start()
    for save in saves:
        save.wait()


def full(shape):
    return pl.BlockSpec(shape, lambda *_: (0,) * len(shape))


def lasts(microseconds):
    return pl.CostEstimate(flops=0, bytes_accessed=int(3.69e6 * microseconds), transcendentals=0)


def in_hbm(array):
    return pltpu.with_memory_space_constraint(array, pltpu.HBM)


def in_vmem(array):
    return pltpu.with_memory_space_constraint(array, pltpu.VMEM)


def exchange(rows, group):
    width = rows.shape[1]
    chunks = rows.reshape(group, -1, width)
    chunks = lax.all_to_all(chunks, ("gy", "gz"), split_axis=0, concat_axis=0, tiled=True)
    return chunks.reshape(-1, width)


def on_device(gas, droplet, owner, cells, weights, mass, liquid_rate, surface_rate, gas_rate):
    group = lax.axis_size("gy") * lax.axis_size("gz")
    nodes, species, parcels = droplet.shape
    cap = 2 * parcels // group
    slots = group * cap
    packed = cap % 16 == 0
    lines = gas.shape[1] * gas.shape[2]
    flat = gas.reshape(species, lines, LANES)
    planes = (lines, species, LANES)
    liquid = liquid_rate.reshape(1, species)
    surface = surface_rate.reshape(1, species)
    rate_spec = full((1, species))
    size_x, size_y = gas.shape[1], gas.shape[2]
    rate = gas_rate.reshape(1, species)
    vmem = pl.BlockSpec(memory_space=pltpu.VMEM)
    hbm = pl.BlockSpec(memory_space=pl.ANY)
    whole = pl.BlockSpec()
    turns_x = len(swaps("gx"))
    x_shape = (2 * size_y, species, LANES)
    y_shape = (2 * size_x, species, LANES)

    send, slot, near_gas, *x_faces = pl.pallas_call(
        functools.partial(pack_kernel, cap, size_x, size_y, turns_x),
        grid=(1,),
        out_shape=[
            pltpu.VMEM((slots, LANES), F32),
            jax.ShapeDtypeStruct((1, parcels), jnp.int32),
            pltpu.VMEM(planes, F32),
        ]
        + [pltpu.VMEM(x_shape, F32)] * turns_x,
        in_specs=[hbm, hbm, full((1, parcels)), full((STENCIL, parcels)), full((STENCIL, parcels)), full((1, parcels))]
        + [rate_spec] * 2,
        out_specs=[vmem, full((1, parcels)), vmem] + [vmem] * turns_x,
        scratch_shapes=[
            pltpu.VMEM((DROP_STEPS, species, parcels), F32),
            pltpu.SemaphoreType.DMA((1 + lines,)),
        ],
        compiler_params=pltpu.CompilerParams(vmem_limit_bytes=8 * MIB),
        cost_estimate=lasts(2.5),
        name="pack",
    )(
        in_hbm(droplet),
        in_hbm(flat),
        in_hbm(owner.reshape(1, parcels)),
        in_hbm(cells),
        in_hbm(weights),
        in_hbm(mass.reshape(1, parcels)),
        in_hbm(liquid),
        in_hbm(surface),
    )
    rows = exchange(send, group)

    x_halo = swap_all(x_faces, "gx")
    y_faces = pl.pallas_call(
        functools.partial(y_faces_kernel, size_x, size_y),
        out_shape=[pltpu.VMEM(y_shape, F32)] * 2,
        in_specs=[vmem],
        out_specs=[vmem] * 2,
        compiler_params=pltpu.CompilerParams(vmem_limit_bytes=4 * MIB),
        cost_estimate=lasts(0.6),
        name="y_faces",
    )(near_gas)
    y_halo = swap_all(y_faces, "gy")

    corners = pl.pallas_call(
        functools.partial(corner_kernel, size_x),
        out_shape=[jax.ShapeDtypeStruct((2, species, LANES), F32)] * turns_x,
        in_specs=[vmem] * 2,
        out_specs=[vmem] * turns_x,
        compiler_params=pltpu.CompilerParams(vmem_limit_bytes=4 * MIB),
        cost_estimate=lasts(0.3),
        name="corner_planes",
    )(*y_halo)
    corners = swap_all(corners, "gx")

    back_rows = slots // 2 if packed else slots
    w_shape = (lines, LANES, slots)
    back, deposit = pl.pallas_call(
        functools.partial(couple_kernel, cap, packed),
        out_shape=[pltpu.VMEM((back_rows, LANES), F32), pltpu.HBM(planes, F32)],
        in_specs=[vmem] * 2 + [whole] * 2,
        out_specs=[vmem, hbm],
        scratch_shapes=[
            pltpu.VMEM(planes, F32),
            pltpu.VMEM(w_shape, BF16),
            pltpu.VMEM(w_shape, BF16),
            pltpu.SemaphoreType.DMA((GROUPS,)),
        ],
        compiler_params=pltpu.CompilerParams(vmem_limit_bytes=10 * MIB),
        cost_estimate=lasts(7.0),
        name="couple_gas",
    )(rows, near_gas, liquid, surface)

    returned = exchange(back, group)

    z_shape = (48, LANES)
    halos = [in_vmem(halo) for halo in x_halo + y_halo]
    field, *stepped = pl.pallas_call(
        functools.partial(first_step_kernel, size_x, size_y, turns_x),
        out_shape=[pltpu.VMEM(planes, F32)]
        + [pltpu.VMEM(x_shape, F32)] * turns_x
        + [pltpu.VMEM(y_shape, F32)] * 2
        + [jax.ShapeDtypeStruct(z_shape, F32)] * 2,
        in_specs=[vmem] * (turns_x + 3) + [whole],
        out_specs=[vmem] * (turns_x + 3) + [whole] * 2,
        input_output_aliases={1 + i: 1 + i for i in range(turns_x + 2)},
        compiler_params=pltpu.CompilerParams(vmem_limit_bytes=8 * MIB),
        cost_estimate=lasts(1.6),
        name="first_gas_step",
    )(near_gas, *halos, rate)
    halos, z_sends = stepped[:-2], stepped[-2:]
    z_halo = swap_all(z_sends, "gz", wrap=True)
    gas_next = pl.pallas_call(
        functools.partial(second_step_kernel, size_x, size_y, turns_x),
        out_shape=jax.ShapeDtypeStruct(flat.shape, F32),
        in_specs=[vmem] * (2 * turns_x + 3) + [whole] * 5 + [hbm],
        out_specs=hbm,
        scratch_shapes=[
            pltpu.VMEM(planes, F32),
            pltpu.VMEM((turns_x, size_y, species, LANES), F32),
            pltpu.VMEM((2, size_x, species, LANES), F32),
            pltpu.VMEM(planes, F32),
            pltpu.VMEM(planes, F32),
            pltpu.SemaphoreType.DMA((lines + 1,)),
        ],
        compiler_params=pltpu.CompilerParams(vmem_limit_bytes=10 * MIB),
        cost_estimate=lasts(4.0),
        name="second_gas_step",
    )(field, *halos[:turns_x], *corners, *halos[turns_x:], *z_sends, *z_halo, rate, in_hbm(deposit))
    droplet_next = pl.pallas_call(
        functools.partial(droplet_kernel, cap, packed),
        out_shape=jax.ShapeDtypeStruct(droplet.shape, F32),
        in_specs=[hbm] + [whole] * 4 + [hbm],
        out_specs=hbm,
        scratch_shapes=[
            pltpu.VMEM(droplet.shape, F32),
            pltpu.VMEM(droplet.shape, F32),
            pltpu.VMEM((species, parcels), F32),
            pltpu.SemaphoreType.DMA((species // 8,)),
            pltpu.SemaphoreType.DMA((species // 8,)),
        ],
        compiler_params=pltpu.CompilerParams(vmem_limit_bytes=8 * MIB),
        cost_estimate=lasts(2.5),
        name="droplets",
    )(in_hbm(droplet), returned, slot, liquid, surface, in_hbm(gas_next))
    return (gas_next.reshape(gas.shape), droplet_next)


def solution(mesh):
    return jax.shard_map(
        on_device,
        mesh=mesh,
        in_specs=(
            P(None, "gx", "gy", "gz"),
            P(None, None, ("gx", "gy", "gz")),
            P(("gx", "gy", "gz"), None),
            P(None, ("gx", "gy", "gz")),
            P(None, ("gx", "gy", "gz")),
            P(("gx", "gy", "gz")),
            P(),
            P(),
            P(),
        ),
        out_specs=(P(None, "gx", "gy", "gz"), P(None, None, ("gx", "gy", "gz"))),
        check_vma=False,
    )
```

time: 52.2 us -> 43.8 us (0.84)
  Pallas kernels: 24.5 us -> 17.5 us
  starting transfers between devices: 20.7 us -> 18.3 us
  waiting for transfers between devices: 5.92 us -> 6.61 us
    pallas_call x5 -> x4, Pallas kernels: 13.2 us -> 9.7 us  [the longest x1 3.54 us: on_device(): pl.pallas_call(functools.partial(second_step_kernel, size_x, size_y, turn...]
    ppermute x6, starting transfers between devices: 8.83 us -> 6.54 us  [swap_all(): lax.ppermute(m, axis, pairs)]
    pallas_call x1, Pallas kernels: 3.85 us -> 1.76 us  [on_device(): pl.pallas_call(functools.partial(first_step_kernel, size_x, size_y, turns...]
    pallas_call x1, Pallas kernels: 7.42 us -> 5.96 us  [on_device(): pl.pallas_call(functools.partial(couple_kernel, cap, packed), out_shape=[...]
    ppermute x6, waiting for transfers between devices: 1.09 us -> 2.02 us  [swap_all(): lax.ppermute(m, axis, pairs)]
  transfers between devices with their start and end apart: 8 -> 8, of which waited for: 2 -> 2; matrix products, arithmetic and copies ran while one was open for 0% -> 0% of each run, Pallas kernels for 29% -> 26%
where the time goes in v4:
time: 43.8 us; the launch traced here: 43.4 us
  starting transfers between devices  18.3 us (42%)
  Pallas kernels  17.5 us (40%)
  waiting for transfers between devices  6.61 us (15%)
  between operations  0.72 us (2%)
    all_to_all x2, starting transfers between devices, exchange(): lax.all_to_all(chunks, ('gy', 'gz'), split_axis=0, concat_axis=0, tiled=T...  11.7 us
    ppermute x6, starting transfers between devices, swap_all(): lax.ppermute(m, axis, pairs)  6.54 us
    pallas_call x1, Pallas kernels, on_device(): pl.pallas_call(functools.partial(couple_kernel, cap, packed), out_shape=[...  5.96 us
    all_to_all x2, waiting for transfers between devices, exchange(): lax.all_to_all(chunks, ('gy', 'gz'), split_axis=0, concat_axis=0, tiled=T...  4.59 us
    pallas_call x1, Pallas kernels, on_device(): pl.pallas_call(functools.partial(second_step_kernel, size_x, size_y, turn...  3.54 us
    pallas_call x1, Pallas kernels, on_device(): pl.pallas_call(functools.partial(pack_kernel, cap, size_x, size_y, turns_...  3.25 us
    pallas_call x1, Pallas kernels, on_device(): pl.pallas_call(functools.partial(droplet_kernel, cap, packed), out_shape=...  2.88 us
    ppermute x6, waiting for transfers between devices, swap_all(): lax.ppermute(m, axis, pairs)  2.02 us
  transfers between devices with their start and end apart: 8, of which 2 were waited for; matrix products, arithmetic and copies ran while one was open for 0% of the time, Pallas kernels for 26%

profile of v4, /device:TPU:1, one launch (start us, length us, event | category | flops | bytes accessed | tf_op | source)
XLA Modules:
  0.0 43.4 jit_solution(7857915177662736355)
XLA Ops:
  0.6 3.3 %pack.1 = (f32[256,128]{1,0:T(8,128)}, s32[1,128]{1,0:T(1,128)S(1)}, f32[32,64,128]{2,1,0:T(8,128)S(1)}, f32[16,64,128]{2,1,0:T(8,128)S(1)}) custom-call(f32[32,64,128]{2,1,0:T(8,128)} %droplet.3, f32[64,32,128]{2,1,0:T(8,128)} %bitcast.22, s32[1,128]{1,0:T(1,128)} %bitcast.23, s32[8,128]{1,0:T(8,128)} %cells.1, f32[8,128]{1,0:T(8,128)} %weights.1, ...), custom_call_target="tpu_custom_call" | custom-call | bytes 9225000 | tf_op jit(solution)/shard_map/pack/pallas_call | solution.py:534
  3.9 2.1 %collective-permute-start = (f32[16,64,128]{2,1,0:T(8,128)S(1)}, f32[16,64,128]{2,1,0:T(8,128)S(1)}, u32[]{:S(2)}, u32[]{:S(2)}) collective-permute-start(f32[16,64,128]{2,1,0:T(8,128)S(1)} %get-tuple-element.17), channel_id=1, source_target_pairs={{0,16},{16,0},{1,17},{17,1},{2,18},{18,2},{3,19},{19,3},{4,20},{20... | collective-permute-start | bytes 1572872 | tf_op jit(solution)/shard_map/ppermute | solution.py:285
  6.0 6.8 %all-to-all-start = ((f32[16,16,128]{2,1,0:T(8,128)}), f32[16,16,128]{2,1,0:T(8,128)S(1)}, u32[]{:S(2)}, u32[]{:S(2)}) async-start(f32[16,16,128]{2,1,0:T(8,128)} %bitcast.6), calls=%async_computation | async-start | bytes 262144 | tf_op jit(solution)/shard_map/all_to_all | solution.py:509
  12.8 1.5 %collective-permute-start.1 = (f32[8,64,128]{2,1,0:T(8,128)S(1)}, f32[8,64,128]{2,1,0:T(8,128)S(1)}, u32[]{:S(2)}, u32[]{:S(2)}) collective-permute-start(f32[8,64,128]{2,1,0:T(8,128)S(1)} %get-tuple-element.18), channel_id=1, source_target_pairs={{0,4},{8,12},{4,0},{12,8},{1,5},{9,13},{5,1},{13,9},{2,6},{10,14},... | collective-permute-start | bytes 786440 | tf_op jit(solution)/shard_map/ppermute | solution.py:285
  14.3 0.0 copy-start
  14.3 0.0 copy-start.1
  14.3 0.8 %collective-permute-start.2 = (f32[8,64,128]{2,1,0:T(8,128)S(1)}, f32[8,64,128]{2,1,0:T(8,128)S(1)}, u32[]{:S(2)}, u32[]{:S(2)}) collective-permute-start(f32[8,64,128]{2,1,0:T(8,128)S(1)} %get-tuple-element.19), channel_id=1, source_target_pairs={{4,8},{8,4},{5,9},{9,5},{6,10},{10,6},{7,11},{11,7},{20,24},{24,20... | collective-permute-start | bytes 786440 | tf_op jit(solution)/shard_map/ppermute | solution.py:285
  15.1 4.6 %all-to-all-done = f32[16,16,128]{2,1,0:T(8,128)S(1)} async-done(((f32[16,16,128]{2,1,0:T(8,128)}), f32[16,16,128]{2,1,0:T(8,128)S(1)}, u32[]{:S(2)}, u32[]{:S(2)}) %all-to-all-start) | async-done | bytes 131104 | tf_op jit(solution)/shard_map/all_to_all | solution.py:509
  19.7 0.0 copy-done
  19.7 0.0 copy-done.1
  19.7 6.0 %couple_gas.1 = (f32[128,128]{1,0:T(8,128)}, f32[32,64,128]{2,1,0:T(8,128)}) custom-call(f32[256,128]{1,0:T(8,128)S(1)} %bitcast.11, f32[32,64,128]{2,1,0:T(8,128)S(1)} %get-tuple-element.16.near_gas.gas, f32[1,64]{1,0:T(1,128)S(1)} %bitcast.14, f32[1,64]{1,0:T(1,128)S(1)} %bitcast.17), custom_call_target="tpu_custom_call" | custom-call | bytes 25830000 | tf_op jit(solution)/shard_map/couple_gas/pallas_call | solution.py:590
  25.7 4.9 %all-to-all-start.1 = ((f32[16,8,128]{2,1,0:T(8,128)}), f32[16,8,128]{2,1,0:T(8,128)S(1)}, u32[]{:S(2)}, u32[]{:S(2)}) async-start(f32[16,8,128]{2,1,0:T(8,128)} %bitcast.9), calls=%async_computation.1 | async-start | bytes 131072 | tf_op jit(solution)/shard_map/all_to_all | solution.py:509
  30.6 0.0 collective-permute-done.1.refs_1_.ya
  30.6 0.0 collective-permute-done.2.refs_2_.yb
  30.6 0.0 copy-start.2
  30.6 0.3 collective-permute-start.3
  31.0 0.0 collective-permute-done.refs_0_
  31.0 0.3 copy-done.2
  31.3 1.8 %first_gas_step.1 = (f32[32,64,128]{2,1,0:T(8,128)S(1)}, f32[16,64,128]{2,1,0:T(8,128)S(1)}, f32[8,64,128]{2,1,0:T(8,128)S(1)}, f32[8,64,128]{2,1,0:T(8,128)S(1)...) custom-call(f32[32,64,128]{2,1,0:T(8,128)S(1)} %get-tuple-element.16.n, ...), custom_call_target="tpu_custom_call", output_to_operand_aliasing={{1}: (1, {}), {2}: (2, {}), {3}: (3, {})} | custom-call | bytes 5904000 | tf_op jit(solution)/shard_map/first_gas_step/pallas_call | solution.py:610
  33.1 0.3 collective-permute-start.4
  33.3 1.6 %collective-permute-start.5 = (f32[48,128]{1,0:T(8,128)S(1)}, f32[48,128]{1,0:T(8,128)S(1)}, u32[]{:S(2)}, u32[]{:S(2)}) collective-permute-start(f32[48,128]{1,0:T(8,128)S(1)} %get-tuple-element.25.refs_5_), channel_id=1, source_target_pairs={{1,2},{3,0},{2,1},{0,3},{5,6},{7,4},{6,5},{4,7},{9,10},{11,8},{10,... | collective-permute-start | bytes 73736 | tf_op jit(solution)/shard_map/ppermute | solution.py:285
  34.9 0.0 collective-permute-done.3.refs_1_
  34.9 0.0 collective-permute-done.4.refs_6_
  34.9 2.0 %collective-permute-done.5.refs_7_ = f32[48,128]{1,0:T(8,128)S(1)} collective-permute-done((f32[48,128]{1,0:T(8,128)S(1)}, f32[48,128]{1,0:T(8,128)S(1)}, u32[]{:S(2)}, u32[]{:S(2)}) %collective-permute-start.5) | collective-permute-done | bytes 24608 | tf_op jit(solution)/shard_map/ppermute | solution.py:285
  36.9 3.5 %second_gas_step.1._ = f32[64,32,128]{2,1,0:T(8,128)} custom-call(f32[32,64,128]{2,1,0:T(8,128)S(1)} %get-tuple-element.20.field, f32[16,64,128]{2,1,0:T(8,128)S(1)} %get-tuple-element.21.refs_0_, f32[2,64,128]{2,1,0:T(8,128)S(1)} %collective-permute-done.3.refs_1_, f32[8,64,128]{2,1,0:T(8,128)S(1)} %get-tuple-element.22.refs_2_, ...), custom_call_target="tpu_custom_call" | custom-call | bytes 14760000 | tf_op jit(solution)/shard_map/second_gas_step/pallas_call | solution.py:625
  40.5 0.0 all-to-all-done.1
  40.5 2.9 %droplets.1 = f32[32,64,128]{2,1,0:T(8,128)} custom-call(f32[32,64,128]{2,1,0:T(8,128)} %droplet.3, f32[128,128]{1,0:T(8,128)S(1)} %bitcast.12, s32[1,128]{1,0:T(1,128)S(1)} %get-tuple-element.29.slots, f32[1,64]{1,0:T(1,128)S(1)} %bitcast.15, f32[1,64]{1,0:T(1,128)S(1)} %bitcast.18, f32[64,32,128]{2,1,0:T(8,128)} %second_gas_step.1._), custom_call_target="tpu_custom_call" | custom-call | bytes 9225000 | tf_op jit(solution)/shard_map/droplets/pallas_call | solution.py:642
  (2 shorter events, 0.1 us)
Async XLA Ops:
  3.9 27.1 %collective-permute-start = (f32[16,64,128]{2,1,0:T(8,128)S(1)}, f32[16,64,128]{2,1,0:T(8,128)S(1)}, u32[]{:S(2)}, u32[]{:S(2)}) collective-permute-start(f32[16,64,128]{2,1,0:T(8,128)S(1)} %get-tuple-element.17), channel_id=1, source_target_pairs={{0,16},{16,0},{1,17},{17,1},{2,18},{18,2},{3,19},{19,3},{4,20},{20... | collective-permute-start | bytes 1572872 | tf_op jit(solution)/shard_map/ppermute | solution.py:285
  6.0 13.7 %all-to-all-start = ((f32[16,16,128]{2,1,0:T(8,128)}), f32[16,16,128]{2,1,0:T(8,128)S(1)}, u32[]{:S(2)}, u32[]{:S(2)}) async-start(f32[16,16,128]{2,1,0:T(8,128)} %bitcast.6), calls=%async_computation | async-start | bytes 262144 | tf_op jit(solution)/shard_map/all_to_all | solution.py:509
  12.8 17.8 %collective-permute-start.1 = (f32[8,64,128]{2,1,0:T(8,128)S(1)}, f32[8,64,128]{2,1,0:T(8,128)S(1)}, u32[]{:S(2)}, u32[]{:S(2)}) collective-permute-start(f32[8,64,128]{2,1,0:T(8,128)S(1)} %get-tuple-element.18), channel_id=1, source_target_pairs={{0,4},{8,12},{4,0},{12,8},{1,5},{9,13},{5,1},{13,9},{2,6},{10,14},... | collective-permute-start | bytes 786440 | tf_op jit(solution)/shard_map/ppermute | solution.py:285
  14.3 5.4 %copy-start = (f32[64]{0:T(128)S(1)}, f32[64]{0:T(128)}, u32[]{:S(2)}) copy-start(f32[64]{0:T(128)} %param.15) | copy-start | bytes 772
  14.3 5.4 %copy-start.1 = (f32[64]{0:T(128)S(1)}, f32[64]{0:T(128)}, u32[]{:S(2)}) copy-start(f32[64]{0:T(128)} %param.16) | copy-start | bytes 772
  14.3 16.3 %collective-permute-start.2 = (f32[8,64,128]{2,1,0:T(8,128)S(1)}, f32[8,64,128]{2,1,0:T(8,128)S(1)}, u32[]{:S(2)}, u32[]{:S(2)}) collective-permute-start(f32[8,64,128]{2,1,0:T(8,128)S(1)} %get-tuple-element.19), channel_id=1, source_target_pairs={{4,8},{8,4},{5,9},{9,5},{6,10},{10,6},{7,11},{11,7},{20,24},{24,20... | collective-permute-start | bytes 786440 | tf_op jit(solution)/shard_map/ppermute | solution.py:285
  25.7 14.8 %all-to-all-start.1 = ((f32[16,8,128]{2,1,0:T(8,128)}), f32[16,8,128]{2,1,0:T(8,128)S(1)}, u32[]{:S(2)}, u32[]{:S(2)}) async-start(f32[16,8,128]{2,1,0:T(8,128)} %bitcast.9), calls=%async_computation.1 | async-start | bytes 131072 | tf_op jit(solution)/shard_map/all_to_all | solution.py:509
  30.6 0.7 %copy-start.2 = (f32[64]{0:T(128)S(1)}, f32[64]{0:T(128)}, u32[]{:S(2)}) copy-start(f32[64]{0:T(128)} %param.17) | copy-start | bytes 772
  30.6 4.3 %collective-permute-start.3 = (f32[2,64,128]{2,1,0:T(8,128)S(1)}, f32[2,64,128]{2,1,0:T(8,128)S(1)}, u32[]{:S(2)}, u32[]{:S(2)}) collective-permute-start(f32[2,64,128]{2,1,0:T(8,128)S(1)} %corner_planes.1), channel_id=1, source_target_pairs={{0,16},{16,0},{1,17},{17,1},{2,18},{18,2},{3,19},{19,3},{4,20},{20... | collective-permute-start | bytes 196616 | tf_op jit(solution)/shard_map/ppermute | solution.py:285
  33.1 1.9 %collective-permute-start.4 = (f32[48,128]{1,0:T(8,128)S(1)}, f32[48,128]{1,0:T(8,128)S(1)}, u32[]{:S(2)}, u32[]{:S(2)}) collective-permute-start(f32[48,128]{1,0:T(8,128)S(1)} %get-tuple-element.24.refs_4_), channel_id=1, source_target_pairs={{0,1},{2,3},{1,0},{3,2},{4,5},{6,7},{5,4},{7,6},{8,9},{10,11},{9,8... | collective-permute-start | bytes 73736 | tf_op jit(solution)/shard_map/ppermute | solution.py:285
  33.3 3.6 %collective-permute-start.5 = (f32[48,128]{1,0:T(8,128)S(1)}, f32[48,128]{1,0:T(8,128)S(1)}, u32[]{:S(2)}, u32[]{:S(2)}) collective-permute-start(f32[48,128]{1,0:T(8,128)S(1)} %get-tuple-element.25.refs_5_), channel_id=1, source_target_pairs={{1,2},{3,0},{2,1},{0,3},{5,6},{7,4},{6,5},{4,7},{9,10},{11,8},{10,... | collective-permute-start | bytes 73736 | tf_op jit(solution)/shard_map/ppermute | solution.py:285

commit v5 on v4

--- a/solution.py
+++ b/solution.py
@@ -68,18 +68,22 @@
     return surface_steps([jnp.zeros_like(liquid)] * DROP_STEPS, 1.0, liquid, surface)
 
 
-def pack_kernel(
-    cap, size_x, size_y, turns_x, droplet, gas, owner, cells, weights, mass, liquid, surface, send, slots, near_gas, *refs
-):
-    x_sends, (tail, sems) = refs[:turns_x], refs[turns_x:]
+def pack_kernel(cap, size_x, size_y, turns_x, droplet, gas, *refs):
+    sources, (send, slots, near_gas), refs = refs[:6], refs[6:9], refs[9:]
+    x_sends, refs = refs[:turns_x], refs[turns_x:]
+    (owner, cells, weights, mass, liquid, surface), (tail, sems) = refs[:6], refs[6:]
     parcels = owner.shape[1]
     nodes, species = droplet.shape[0], droplet.shape[1]
-    load_tail = pltpu.make_async_copy(droplet.at[pl.ds(nodes - DROP_STEPS, DROP_STEPS)], tail, sems.at[0])
     lines = gas.shape[1]
-    loads = [pltpu.make_async_copy(gas.at[:, line, :], near_gas.at[line], sems.at[1 + line]) for line in range(lines)]
-    load_tail.start()
+    pairs = list(zip(sources, refs[:6], strict=True))
+    pairs.append((droplet.at[pl.ds(nodes - DROP_STEPS, DROP_STEPS)], tail))
+    small = len(pairs)
+    pairs += [(gas.at[:, line, :], near_gas.at[line]) for line in range(lines)]
+    loads = [pltpu.make_async_copy(source, here, sems.at[i]) for i, (source, here) in enumerate(pairs)]
     for load in loads:
         load.start()
+    for load in loads[: small - 1]:
+        load.wait()
     wts = weights[...]
     norm = wts / jnp.sum(wts, axis=0, keepdims=True)
     mine = owner[...]
@@ -91,7 +95,7 @@
     place = one_hot(iota((send.shape[0], parcels), 0) == slot)
     rest = jnp.zeros((LANES - species - 2 * STENCIL - 8, parcels), F32)
     liquid_col, surface_col = as_column(liquid[...]), as_column(surface[...])
-    load_tail.wait()
+    loads[small - 1].wait()
     emitted = surface_steps([tail[i] for i in range(DROP_STEPS)], 0.0, liquid_col, surface_col)
     values = jnp.concatenate(
         [
@@ -103,7 +107,7 @@
         ],
         axis=0,
     )
-    for load in loads:
+    for load in loads[small:]:
         load.wait()
     even_x, _, _ = place_on("gx")
     for turn, x_send in enumerate(x_sends):
@@ -203,17 +207,11 @@
 
 
 def droplet_kernel(
-    cap, packed, droplet, rows, slots, liquid, surface, _, state_out, state_in, state_next, gas_at, load_sems, sems
+    cap, packed, state_in, rows, slots, liquid, surface, _, state_out, state_next, gas_at, sems
 ):
     nodes, species, parcels = state_in.shape
     block = 8
 
-    def load(i):
-        at = pl.ds(i * block, block)
-        return pltpu.make_async_copy(droplet.at[:, at], state_in.at[:, at], load_sems.at[i])
-
-    for i in range(species // block):
-        load(i).start()
     table = jnp.transpose(rows[...])
     count = rows.shape[0]
     at = iota((count, parcels), 0)
@@ -235,7 +233,7 @@
         at = pl.ds(i * block, block)
         return pltpu.make_async_copy(state_next.at[:, at], state_out.at[:, at], sems.at[i])
 
-    @pl.loop(0, species // block)
+    @pl.loop(0, species // block, unroll=4)
     def _(i):
         at = pl.ds(pl.multiple_of(i * block, block), block)
         pick = i * block + iota((block, species), 0) == iota((block, species), 1)
@@ -245,7 +243,6 @@
         keep = 1.0 - 2.0 * rate
         last_keep = jnp.broadcast_to(1.0 - liquid_col - surface_col, (block, parcels))
         from_gas = surface_col * gas_at[at, :]
-        load(i).wait()
         state = [state_in[node, at] for node in range(nodes)]
         for step in range(DROP_STEPS):
             state = (
@@ -404,11 +401,9 @@
 ):
     xs, refs = refs[:turns_x], refs[turns_x:]
     corners, refs = refs[:turns_x], refs[turns_x:]
-    ya, yb, za, zb, za_in, zb_in, rate, deposit_in, out, now, now_x, now_y, result, deposit, sems = refs
+    ya, yb, za, zb, za_in, zb_in, rate, deposit, out, now, now_x, now_y, result, sems = refs
     species = rate.shape[1]
     lines = size_x * size_y
-    load = pltpu.make_async_copy(deposit_in, deposit, sems.at[lines])
-    load.start()
     even_x, _, _ = place_on("gx")
     even_y, _, _ = place_on("gy")
     even, below, above = place_on("gz")
@@ -461,7 +456,6 @@
     def from_y(side, x):
         return low_high(even_y, now_y[0, x], now_y[1, x])[side]
 
-    load.wait()
     saves = []
     for x in range(size_x):
         for y in range(size_y):
@@ -533,19 +527,23 @@
 
     send, slot, near_gas, *x_faces = pl.pallas_call(
         functools.partial(pack_kernel, cap, size_x, size_y, turns_x),
-        grid=(1,),
         out_shape=[
             pltpu.VMEM((slots, LANES), F32),
-            jax.ShapeDtypeStruct((1, parcels), jnp.int32),
+            pltpu.VMEM((1, parcels), jnp.int32),
             pltpu.VMEM(planes, F32),
         ]
         + [pltpu.VMEM(x_shape, F32)] * turns_x,
-        in_specs=[hbm, hbm, full((1, parcels)), full((STENCIL, parcels)), full((STENCIL, parcels)), full((1, parcels))]
-        + [rate_spec] * 2,
-        out_specs=[vmem, full((1, parcels)), vmem] + [vmem] * turns_x,
+        in_specs=[hbm] * 8,
+        out_specs=[vmem] * (3 + turns_x),
         scratch_shapes=[
+            pltpu.VMEM((1, parcels), jnp.int32),
+            pltpu.VMEM((STENCIL, parcels), jnp.int32),
+            pltpu.VMEM((STENCIL, parcels), F32),
+            pltpu.VMEM((1, parcels), F32),
+            pltpu.VMEM((1, species), F32),
+            pltpu.VMEM((1, species), F32),
             pltpu.VMEM((DROP_STEPS, species, parcels), F32),
-            pltpu.SemaphoreType.DMA((1 + lines,)),
+            pltpu.SemaphoreType.DMA((7 + lines,)),
         ],
         compiler_params=pltpu.CompilerParams(vmem_limit_bytes=8 * MIB),
         cost_estimate=lasts(2.5),
@@ -562,7 +560,6 @@
     )
     rows = exchange(send, group)
 
-    x_halo = swap_all(x_faces, "gx")
     y_faces = pl.pallas_call(
         functools.partial(y_faces_kernel, size_x, size_y),
         out_shape=[pltpu.VMEM(y_shape, F32)] * 2,
@@ -573,6 +570,7 @@
         name="y_faces",
     )(near_gas)
     y_halo = swap_all(y_faces, "gy")
+    x_halo = swap_all(x_faces, "gx")
 
     corners = pl.pallas_call(
         functools.partial(corner_kernel, size_x),
@@ -625,36 +623,33 @@
     gas_next = pl.pallas_call(
         functools.partial(second_step_kernel, size_x, size_y, turns_x),
         out_shape=jax.ShapeDtypeStruct(flat.shape, F32),
-        in_specs=[vmem] * (2 * turns_x + 3) + [whole] * 5 + [hbm],
+        in_specs=[vmem] * (2 * turns_x + 3) + [whole] * 5 + [vmem],
         out_specs=hbm,
         scratch_shapes=[
             pltpu.VMEM(planes, F32),
             pltpu.VMEM((turns_x, size_y, species, LANES), F32),
             pltpu.VMEM((2, size_x, species, LANES), F32),
             pltpu.VMEM(planes, F32),
-            pltpu.VMEM(planes, F32),
-            pltpu.SemaphoreType.DMA((lines + 1,)),
+            pltpu.SemaphoreType.DMA((lines,)),
         ],
         compiler_params=pltpu.CompilerParams(vmem_limit_bytes=10 * MIB),
         cost_estimate=lasts(4.0),
         name="second_gas_step",
-    )(field, *halos[:turns_x], *corners, *halos[turns_x:], *z_sends, *z_halo, rate, in_hbm(deposit))
+    )(field, *halos[:turns_x], *corners, *halos[turns_x:], *z_sends, *z_halo, rate, in_vmem(deposit))
     droplet_next = pl.pallas_call(
         functools.partial(droplet_kernel, cap, packed),
         out_shape=jax.ShapeDtypeStruct(droplet.shape, F32),
-        in_specs=[hbm] + [whole] * 4 + [hbm],
+        in_specs=[whole] * 5 + [hbm],
         out_specs=hbm,
         scratch_shapes=[
             pltpu.VMEM(droplet.shape, F32),
-            pltpu.VMEM(droplet.shape, F32),
             pltpu.VMEM((species, parcels), F32),
-            pltpu.SemaphoreType.DMA((species // 8,)),
             pltpu.SemaphoreType.DMA((species // 8,)),
         ],
         compiler_params=pltpu.CompilerParams(vmem_limit_bytes=8 * MIB),
         cost_estimate=lasts(2.5),
         name="droplets",
-    )(in_hbm(droplet), returned, slot, liquid, surface, in_hbm(gas_next))
+    )(droplet, returned, slot, liquid, surface, in_hbm(gas_next))
     return (gas_next.reshape(gas.shape), droplet_next)
 
 

time: 43.8 us -> 40.9 us (0.934)
  Pallas kernels: 17.5 us -> 14.6 us
    pallas_call x1, Pallas kernels: 2.88 us -> 1.68 us  [on_device(): pl.pallas_call(functools.partial(droplet_kernel, cap, packed), out_shape=...]
    pallas_call x1, Pallas kernels: 3.54 us -> 2.44 us  [on_device(): pl.pallas_call(functools.partial(second_step_kernel, size_x, size_y, turn...]
    pallas_call x1, Pallas kernels: 3.25 us -> 2.66 us  [on_device(): pl.pallas_call(functools.partial(pack_kernel, cap, size_x, size_y, turns_...]
  transfers between devices with their start and end apart: 8 -> 8, of which waited for: 2 -> 2; matrix products, arithmetic and copies ran while one was open for 0% -> 0% of each run, Pallas kernels for 26% -> 25%
where the time goes in v5:
time: 40.9 us; the launch traced here: 40.5 us
  starting transfers between devices  18.3 us (45%)
  Pallas kernels  14.6 us (36%)
  waiting for transfers between devices  6.61 us (16%)
  between operations  0.73 us (2%)
    all_to_all x2, starting transfers between devices, exchange(): lax.all_to_all(chunks, ('gy', 'gz'), split_axis=0, concat_axis=0, tiled=T...  11.7 us
    ppermute x6, starting transfers between devices, swap_all(): lax.ppermute(m, axis, pairs)  6.54 us
    pallas_call x1, Pallas kernels, on_device(): pl.pallas_call(functools.partial(couple_kernel, cap, packed), out_shape=[...  5.97 us
    all_to_all x2, waiting for transfers between devices, exchange(): lax.all_to_all(chunks, ('gy', 'gz'), split_axis=0, concat_axis=0, tiled=T...  4.59 us
    pallas_call x1, Pallas kernels, on_device(): pl.pallas_call(functools.partial(pack_kernel, cap, size_x, size_y, turns_...  2.66 us
    pallas_call x1, Pallas kernels, on_device(): pl.pallas_call(functools.partial(second_step_kernel, size_x, size_y, turn...  2.44 us
    ppermute x6, waiting for transfers between devices, swap_all(): lax.ppermute(m, axis, pairs)  2.02 us
    pallas_call x1, Pallas kernels, on_device(): pl.pallas_call(functools.partial(first_step_kernel, size_x, size_y, turns...  1.76 us
  transfers between devices with their start and end apart: 8, of which 2 were waited for; matrix products, arithmetic and copies ran while one was open for 0% of the time, Pallas kernels for 25%

profile of v5, /device:TPU:1, one launch (start us, length us, event | category | flops | bytes accessed | tf_op | source)
XLA Modules:
  0.0 40.5 jit_solution(15327390843607714462)
XLA Ops:
  0.6 2.7 %pack.1 = (f32[256,128]{1,0:T(8,128)}, s32[1,128]{1,0:T(1,128)S(1)}, f32[32,64,128]{2,1,0:T(8,128)S(1)}, f32[16,64,128]{2,1,0:T(8,128)S(1)}) custom-call(f32[32,64,128]{2,1,0:T(8,128)} %state_in.1, f32[64,32,128]{2,1,0:T(8,128)} %bitcast.22, s32[1,128]{1,0:T(1,128)} %bitcast.23, s32[8,128]{1,0:T(8,128)} %refs_1_.1, f32[8,128]{1,0:T(8,128)} %refs_2_.1, ...), custom_call_target="tpu_custom_call" | custom-call | bytes 9225000 | tf_op jit(solution)/shard_map/pack/pallas_call | solution.py:528
  3.3 2.1 %collective-permute-start = (f32[16,64,128]{2,1,0:T(8,128)S(1)}, f32[16,64,128]{2,1,0:T(8,128)S(1)}, u32[]{:S(2)}, u32[]{:S(2)}) collective-permute-start(f32[16,64,128]{2,1,0:T(8,128)S(1)} %get-tuple-element.17), channel_id=1, source_target_pairs={{0,16},{16,0},{1,17},{17,1},{2,18},{18,2},{3,19},{19,3},{4,20},{20... | collective-permute-start | bytes 1572872 | tf_op jit(solution)/shard_map/ppermute | solution.py:282
  5.4 6.8 %all-to-all-start = ((f32[16,16,128]{2,1,0:T(8,128)}), f32[16,16,128]{2,1,0:T(8,128)S(1)}, u32[]{:S(2)}, u32[]{:S(2)}) async-start(f32[16,16,128]{2,1,0:T(8,128)} %bitcast.6), calls=%async_computation | async-start | bytes 262144 | tf_op jit(solution)/shard_map/all_to_all | solution.py:503
  12.2 1.5 %collective-permute-start.1 = (f32[8,64,128]{2,1,0:T(8,128)S(1)}, f32[8,64,128]{2,1,0:T(8,128)S(1)}, u32[]{:S(2)}, u32[]{:S(2)}) collective-permute-start(f32[8,64,128]{2,1,0:T(8,128)S(1)} %get-tuple-element.18), channel_id=1, source_target_pairs={{0,4},{8,12},{4,0},{12,8},{1,5},{9,13},{5,1},{13,9},{2,6},{10,14},... | collective-permute-start | bytes 786440 | tf_op jit(solution)/shard_map/ppermute | solution.py:282
  13.7 0.0 copy-start.2
  13.7 0.0 copy-start.3
  13.7 0.8 %collective-permute-start.2 = (f32[8,64,128]{2,1,0:T(8,128)S(1)}, f32[8,64,128]{2,1,0:T(8,128)S(1)}, u32[]{:S(2)}, u32[]{:S(2)}) collective-permute-start(f32[8,64,128]{2,1,0:T(8,128)S(1)} %get-tuple-element.19), channel_id=1, source_target_pairs={{4,8},{8,4},{5,9},{9,5},{6,10},{10,6},{7,11},{11,7},{20,24},{24,20... | collective-permute-start | bytes 786440 | tf_op jit(solution)/shard_map/ppermute | solution.py:282
  14.5 4.6 %all-to-all-done = f32[16,16,128]{2,1,0:T(8,128)S(1)} async-done(((f32[16,16,128]{2,1,0:T(8,128)}), f32[16,16,128]{2,1,0:T(8,128)S(1)}, u32[]{:S(2)}, u32[]{:S(2)}) %all-to-all-start) | async-done | bytes 131104 | tf_op jit(solution)/shard_map/all_to_all | solution.py:503
  19.1 0.0 copy-done.2
  19.1 0.0 copy-done.3
  19.1 6.0 %couple_gas.1 = (f32[128,128]{1,0:T(8,128)}, f32[32,64,128]{2,1,0:T(8,128)}) custom-call(f32[256,128]{1,0:T(8,128)S(1)} %bitcast.11, f32[32,64,128]{2,1,0:T(8,128)S(1)} %get-tuple-element.16.near_gas.gas, f32[1,64]{1,0:T(1,128)S(1)} %bitcast.14, f32[1,64]{1,0:T(1,128)S(1)} %bitcast.17), custom_call_target="tpu_custom_call" | custom-call | bytes 25830000 | tf_op jit(solution)/shard_map/couple_gas/pallas_call | solution.py:588
  25.1 4.9 %all-to-all-start.1 = ((f32[16,8,128]{2,1,0:T(8,128)}), f32[16,8,128]{2,1,0:T(8,128)S(1)}, u32[]{:S(2)}, u32[]{:S(2)}) async-start(f32[16,8,128]{2,1,0:T(8,128)} %bitcast.9), calls=%async_computation.1 | async-start | bytes 131072 | tf_op jit(solution)/shard_map/all_to_all | solution.py:503
  30.0 0.0 collective-permute-done.1.refs_1_.ya
  30.0 0.0 collective-permute-done.2.refs_2_.yb
  30.0 0.0 copy-start.4
  30.1 0.3 collective-permute-start.3
  30.4 0.0 collective-permute-done.refs_0_
  30.4 0.3 copy-done.4
  30.7 0.0 copy-start.1
  30.7 1.8 %first_gas_step.1 = (f32[32,64,128]{2,1,0:T(8,128)S(1)}, f32[16,64,128]{2,1,0:T(8,128)S(1)}, f32[8,64,128]{2,1,0:T(8,128)S(1)}, f32[8,64,128]{2,1,0:T(8,128)S(1)...) custom-call(f32[32,64,128]{2,1,0:T(8,128)S(1)} %get-tuple-element.16.n, ...), custom_call_target="tpu_custom_call", output_to_operand_aliasing={{1}: (1, {}), {2}: (2, {}), {3}: (3, {})} | custom-call | bytes 5904000 | tf_op jit(solution)/shard_map/first_gas_step/pallas_call | solution.py:608
  32.5 0.3 collective-permute-start.4
  32.8 1.6 %collective-permute-start.5 = (f32[48,128]{1,0:T(8,128)S(1)}, f32[48,128]{1,0:T(8,128)S(1)}, u32[]{:S(2)}, u32[]{:S(2)}) collective-permute-start(f32[48,128]{1,0:T(8,128)S(1)} %get-tuple-element.25.refs_5_), channel_id=1, source_target_pairs={{1,2},{3,0},{2,1},{0,3},{5,6},{7,4},{6,5},{4,7},{9,10},{11,8},{10,... | collective-permute-start | bytes 73736 | tf_op jit(solution)/shard_map/ppermute | solution.py:282
  34.3 0.0 collective-permute-done.3.refs_1_
  34.3 0.0 collective-permute-done.4.refs_6_
  34.3 2.0 %collective-permute-done.5.refs_7_ = f32[48,128]{1,0:T(8,128)S(1)} collective-permute-done((f32[48,128]{1,0:T(8,128)S(1)}, f32[48,128]{1,0:T(8,128)S(1)}, u32[]{:S(2)}, u32[]{:S(2)}) %collective-permute-start.5) | collective-permute-done | bytes 24608 | tf_op jit(solution)/shard_map/ppermute | solution.py:282
  36.4 0.0 copy-done.1
  36.4 0.0 copy-start
  36.4 2.4 %second_gas_step.1._ = f32[64,32,128]{2,1,0:T(8,128)} custom-call(f32[32,64,128]{2,1,0:T(8,128)S(1)} %get-tuple-element.20.field, f32[16,64,128]{2,1,0:T(8,128)S(1)} %get-tuple-element.21.refs_0_, f32[2,64,128]{2,1,0:T(8,128)S(1)} %collective-permute-done.3.refs_1_, f32[8,64,128]{2,1,0:T(8,128)S(1)} %get-tuple-element.22.refs_2_, ...), custom_call_target="tpu_custom_call" | custom-call | bytes 14760000 | tf_op jit(solution)/shard_map/second_gas_step/pallas_call | solution.py:623
  38.8 0.0 all-to-all-done.1
  38.8 0.0 copy-done
  38.8 1.7 %droplets.1 = f32[32,64,128]{2,1,0:T(8,128)} custom-call(f32[32,64,128]{2,1,0:T(8,128)S(1)} %copy-done, f32[128,128]{1,0:T(8,128)S(1)} %bitcast.12, s32[1,128]{1,0:T(1,128)S(1)} %get-tuple-element.29.slots, f32[1,64]{1,0:T(1,128)S(1)} %bitcast.15, f32[1,64]{1,0:T(1,128)S(1)} %bitcast.18, f32[64,32,128]{2,1,0:T(8,128)} %second_gas_step.1._), custom_call_target="tpu_custom_call" | custom-call | bytes 9225000 | tf_op jit(solution)/shard_map/droplets/pallas_call | solution.py:639
  (2 shorter events, 0.1 us)
Async XLA Ops:
  3.3 27.1 %collective-permute-start = (f32[16,64,128]{2,1,0:T(8,128)S(1)}, f32[16,64,128]{2,1,0:T(8,128)S(1)}, u32[]{:S(2)}, u32[]{:S(2)}) collective-permute-start(f32[16,64,128]{2,1,0:T(8,128)S(1)} %get-tuple-element.17), channel_id=1, source_target_pairs={{0,16},{16,0},{1,17},{17,1},{2,18},{18,2},{3,19},{19,3},{4,20},{20... | collective-permute-start | bytes 1572872 | tf_op jit(solution)/shard_map/ppermute | solution.py:282
  5.4 13.7 %all-to-all-start = ((f32[16,16,128]{2,1,0:T(8,128)}), f32[16,16,128]{2,1,0:T(8,128)S(1)}, u32[]{:S(2)}, u32[]{:S(2)}) async-start(f32[16,16,128]{2,1,0:T(8,128)} %bitcast.6), calls=%async_computation | async-start | bytes 262144 | tf_op jit(solution)/shard_map/all_to_all | solution.py:503
  12.2 17.8 %collective-permute-start.1 = (f32[8,64,128]{2,1,0:T(8,128)S(1)}, f32[8,64,128]{2,1,0:T(8,128)S(1)}, u32[]{:S(2)}, u32[]{:S(2)}) collective-permute-start(f32[8,64,128]{2,1,0:T(8,128)S(1)} %get-tuple-element.18), channel_id=1, source_target_pairs={{0,4},{8,12},{4,0},{12,8},{1,5},{9,13},{5,1},{13,9},{2,6},{10,14},... | collective-permute-start | bytes 786440 | tf_op jit(solution)/shard_map/ppermute | solution.py:282
  13.7 5.4 %copy-start.2 = (f32[64]{0:T(128)S(1)}, f32[64]{0:T(128)}, u32[]{:S(2)}) copy-start(f32[64]{0:T(128)} %param.15) | copy-start | bytes 772
  13.7 5.4 %copy-start.3 = (f32[64]{0:T(128)S(1)}, f32[64]{0:T(128)}, u32[]{:S(2)}) copy-start(f32[64]{0:T(128)} %param.16) | copy-start | bytes 772
  13.7 16.3 %collective-permute-start.2 = (f32[8,64,128]{2,1,0:T(8,128)S(1)}, f32[8,64,128]{2,1,0:T(8,128)S(1)}, u32[]{:S(2)}, u32[]{:S(2)}) collective-permute-start(f32[8,64,128]{2,1,0:T(8,128)S(1)} %get-tuple-element.19), channel_id=1, source_target_pairs={{4,8},{8,4},{5,9},{9,5},{6,10},{10,6},{7,11},{11,7},{20,24},{24,20... | collective-permute-start | bytes 786440 | tf_op jit(solution)/shard_map/ppermute | solution.py:282
  25.1 13.7 %all-to-all-start.1 = ((f32[16,8,128]{2,1,0:T(8,128)}), f32[16,8,128]{2,1,0:T(8,128)S(1)}, u32[]{:S(2)}, u32[]{:S(2)}) async-start(f32[16,8,128]{2,1,0:T(8,128)} %bitcast.9), calls=%async_computation.1 | async-start | bytes 131072 | tf_op jit(solution)/shard_map/all_to_all | solution.py:503
  30.0 0.7 %copy-start.4 = (f32[64]{0:T(128)S(1)}, f32[64]{0:T(128)}, u32[]{:S(2)}) copy-start(f32[64]{0:T(128)} %param.17) | copy-start | bytes 772
  30.1 4.3 %collective-permute-start.3 = (f32[2,64,128]{2,1,0:T(8,128)S(1)}, f32[2,64,128]{2,1,0:T(8,128)S(1)}, u32[]{:S(2)}, u32[]{:S(2)}) collective-permute-start(f32[2,64,128]{2,1,0:T(8,128)S(1)} %corner_planes.1), channel_id=1, source_target_pairs={{0,16},{16,0},{1,17},{17,1},{2,18},{18,2},{3,19},{19,3},{4,20},{20... | collective-permute-start | bytes 196616 | tf_op jit(solution)/shard_map/ppermute | solution.py:282
  30.7 5.7 %copy-start.1 = (f32[32,64,128]{2,1,0:T(8,128)S(1)}, f32[32,64,128]{2,1,0:T(8,128)}, u32[]{:S(2)}) copy-start(f32[32,64,128]{2,1,0:T(8,128)} %get-tuple-element.27.refs_9_) | copy-start | bytes 3145732
  32.5 1.9 %collective-permute-start.4 = (f32[48,128]{1,0:T(8,128)S(1)}, f32[48,128]{1,0:T(8,128)S(1)}, u32[]{:S(2)}, u32[]{:S(2)}) collective-permute-start(f32[48,128]{1,0:T(8,128)S(1)} %get-tuple-element.24.refs_4_), channel_id=1, source_target_pairs={{0,1},{2,3},{1,0},{3,2},{4,5},{6,7},{5,4},{7,6},{8,9},{10,11},{9,8... | collective-permute-start | bytes 73736 | tf_op jit(solution)/shard_map/ppermute | solution.py:282
  32.8 3.6 %collective-permute-start.5 = (f32[48,128]{1,0:T(8,128)S(1)}, f32[48,128]{1,0:T(8,128)S(1)}, u32[]{:S(2)}, u32[]{:S(2)}) collective-permute-start(f32[48,128]{1,0:T(8,128)S(1)} %get-tuple-element.25.refs_5_), channel_id=1, source_target_pairs={{1,2},{3,0},{2,1},{0,3},{5,6},{7,4},{6,5},{4,7},{9,10},{11,8},{10,... | collective-permute-start | bytes 73736 | tf_op jit(solution)/shard_map/ppermute | solution.py:282
  36.4 2.5 %copy-start = (f32[32,64,128]{2,1,0:T(8,128)S(1)}, f32[32,64,128]{2,1,0:T(8,128)}, u32[]{:S(2)}) copy-start(f32[32,64,128]{2,1,0:T(8,128)} %state_in.1) | copy-start | bytes 3145732

commit v6 on v5

--- a/solution.py
+++ b/solution.py
@@ -11,7 +11,6 @@
 DROP_STEPS = 4
 GAS_STEPS = 2
 LANES = 128
-GROUPS = 4
 MIB = 1 << 20
 NT = (((1,), (1,)), ((), ()))
 HIGH = lax.Precision.HIGHEST
@@ -70,7 +69,7 @@
 
 def pack_kernel(cap, size_x, size_y, turns_x, droplet, gas, *refs):
     sources, (send, slots, near_gas), refs = refs[:6], refs[6:9], refs[9:]
-    x_sends, refs = refs[:turns_x], refs[turns_x:]
+    x_sends, refs = refs[: 2 * turns_x], refs[2 * turns_x :]
     (owner, cells, weights, mass, liquid, surface), (tail, sems) = refs[:6], refs[6:]
     parcels = owner.shape[1]
     nodes, species = droplet.shape[0], droplet.shape[1]
@@ -110,10 +109,13 @@
     for load in loads[small:]:
         load.wait()
     even_x, _, _ = place_on("gx")
-    for turn, x_send in enumerate(x_sends):
-        start = jnp.where(even_x == (turn == 0), size_x - 2, 0) * size_y
-        for i in range(2 * size_y):
-            x_send[i] = near_gas[start + i]
+    for turn in range(turns_x):
+        up = even_x == (turn == 0)
+        near = jnp.where(up, size_x - 1, 0) * size_y
+        far = jnp.where(up, size_x - 2, 1) * size_y
+        for y in range(size_y):
+            x_sends[turn][y] = near_gas[near + y]
+            x_sends[turns_x + turn][y] = near_gas[far + y]
     parts = jnp.concatenate(split_all(values), axis=0)
     placed = lax.dot_general(place, parts, NT, preferred_element_type=F32)
     send[...] = placed[:, :LANES] + placed[:, LANES : 2 * LANES] + placed[:, 2 * LANES :]
@@ -138,7 +140,7 @@
         send[0], send[1] = low_high(even_y, ya[x], yb[x])
 
 
-def couple_kernel(cap, packed, rows, gas, liquid, surface, back, deposit_out, deposit, w_high, w_low, sems):
+def couple_kernel(cap, packed, rows, gas, liquid, surface, back, deposit, w_high, w_low):
     slots = rows.shape[0]
     species = liquid.shape[1]
     lines = gas.shape[0]
@@ -190,20 +192,12 @@
     s_high, s_low = split(table[:species] + mass * (response * gathered))
     s_all = jnp.concatenate([s_high, s_low], axis=0)
     s_only = jnp.concatenate([s_high, jnp.zeros_like(s_low)], axis=0)
-    saves = []
-    each = lines // GROUPS
     for line in range(0, lines, 2):
         both = lax.dot_general(pair(w_high, line), s_all, NT, preferred_element_type=F32)
         both = both + lax.dot_general(pair(w_low, line), s_only, NT, preferred_element_type=F32)
         for i in range(2):
             turned = jnp.transpose(both[i * LANES : (i + 1) * LANES])
             deposit[line + i] = turned[:species] + turned[species:]
-        if line % each == each - 2:
-            at = pl.ds(line + 2 - each, each)
-            saves.append(pltpu.make_async_copy(deposit.at[at], deposit_out.at[at], sems.at[line // each]))
-            saves[-1].start()
-    for save in saves:
-        save.wait()
 
 
 def droplet_kernel(
@@ -321,6 +315,7 @@
 
 def first_step_kernel(size_x, size_y, turns_x, gas, *refs):
     xs, refs = refs[:turns_x], refs[turns_x:]
+    xs_far, refs = refs[:turns_x], refs[turns_x:]
     (ya, yb, rate, field), refs = refs[:4], refs[4:]
     xs_out, (ya_out, yb_out, za, zb) = refs[:turns_x], refs[turns_x:]
     species = rate.shape[1]
@@ -333,7 +328,7 @@
     planes = [[plane_at(gas, x * size_y + y) for y in range(size_y)] for x in range(size_x)]
 
     def from_x(side, y):
-        near = [ref[(1 - side) * size_y + y] for ref in xs]
+        near = [ref[y] for ref in xs]
         return low_high(even_x, near[0], near[1] if turns_x == 2 else None)[side]
 
     def from_y(side, x):
@@ -356,16 +351,15 @@
     for turn, ref in enumerate(xs):
         up = even_x == (turn == 0)
         exists = jnp.where(up, above_x, below_x)
-        near, far = jnp.where(up, 0, size_y), jnp.where(up, size_y, 0)
         inner = jnp.where(up, lines - size_y, 0)
         for y in range(size_y):
-            own = ref[near + y]
-            total = ref[far + y] + exists * gas[inner + y]
+            own = ref[y]
+            total = xs_far[turn][y] + exists * gas[inner + y]
             if y > 0:
-                total = total + ref[near + y - 1]
+                total = total + ref[y - 1]
             if y < size_y - 1:
-                total = total + ref[near + y + 1]
-            xs_out[turn][far + y] = keep * own + wide * (total + beside_z(own))
+                total = total + ref[y + 1]
+            xs_out[turn][y] = keep * own + wide * (total + beside_z(own))
 
     for turn, (ref, ref_out) in enumerate(((ya, ya_out), (yb, yb_out))):
         up = even_y == (turn == 0)
@@ -384,9 +378,8 @@
     each = LANES // species
     for ref in (gas, field):
         rows += [columns_of(ref[i : i + each].reshape(LANES, LANES)) for i in range(0, lines, each)]
-    for turn, ref in enumerate(xs):
-        near = jnp.where(even_x == (turn == 0), 0, size_y)
-        rows += [columns_of(ref[pl.ds(near + i, each)].reshape(LANES, LANES)) for i in range(0, size_y, each)]
+    for ref in xs:
+        rows += [columns_of(ref[i : i + each].reshape(LANES, LANES)) for i in range(0, size_y, each)]
     for ref in (ya, yb):
         rows += [columns_of(ref[i : i + each].reshape(LANES, LANES)) for i in range(0, size_x, each)]
     rest = [jnp.zeros((za.shape[0] - len(rows), LANES), F32)]
@@ -434,8 +427,7 @@
     add_halo(now, field, 0, count, 0)
     first = 2 * count
     for turn, (ref, corner) in enumerate(zip(xs, corners, strict=True)):
-        start = jnp.where(even_x == (turn == 0), size_y, 0)
-        add_halo(now_x.at[turn], ref, start, size_y // each, first)
+        add_halo(now_x.at[turn], ref, 0, size_y // each, first)
         first = first + size_y // each
         now_x[turn, 0] = now_x[turn, 0] + wide * corner[0]
         now_x[turn, size_y - 1] = now_x[turn, size_y - 1] + wide * corner[1]
@@ -522,7 +514,7 @@
     hbm = pl.BlockSpec(memory_space=pl.ANY)
     whole = pl.BlockSpec()
     turns_x = len(swaps("gx"))
-    x_shape = (2 * size_y, species, LANES)
+    x_shape = (size_y, species, LANES)
     y_shape = (2 * size_x, species, LANES)
 
     send, slot, near_gas, *x_faces = pl.pallas_call(
@@ -532,9 +524,9 @@
             pltpu.VMEM((1, parcels), jnp.int32),
             pltpu.VMEM(planes, F32),
         ]
-        + [pltpu.VMEM(x_shape, F32)] * turns_x,
+        + [pltpu.VMEM(x_shape, F32)] * (2 * turns_x),
         in_specs=[hbm] * 8,
-        out_specs=[vmem] * (3 + turns_x),
+        out_specs=[vmem] * (3 + 2 * turns_x),
         scratch_shapes=[
             pltpu.VMEM((1, parcels), jnp.int32),
             pltpu.VMEM((STENCIL, parcels), jnp.int32),
@@ -570,7 +562,8 @@
         name="y_faces",
     )(near_gas)
     y_halo = swap_all(y_faces, "gy")
-    x_halo = swap_all(x_faces, "gx")
+    x_near = swap_all(x_faces[:turns_x], "gx")
+    x_far = swap_all(x_faces[turns_x:], "gx")
 
     corners = pl.pallas_call(
         functools.partial(corner_kernel, size_x),
@@ -587,14 +580,12 @@
     w_shape = (lines, LANES, slots)
     back, deposit = pl.pallas_call(
         functools.partial(couple_kernel, cap, packed),
-        out_shape=[pltpu.VMEM((back_rows, LANES), F32), pltpu.HBM(planes, F32)],
+        out_shape=[pltpu.VMEM((back_rows, LANES), F32), pltpu.VMEM(planes, F32)],
         in_specs=[vmem] * 2 + [whole] * 2,
-        out_specs=[vmem, hbm],
+        out_specs=[vmem, vmem],
         scratch_shapes=[
-            pltpu.VMEM(planes, F32),
             pltpu.VMEM(w_shape, BF16),
             pltpu.VMEM(w_shape, BF16),
-            pltpu.SemaphoreType.DMA((GROUPS,)),
         ],
         compiler_params=pltpu.CompilerParams(vmem_limit_bytes=10 * MIB),
         cost_estimate=lasts(7.0),
@@ -604,16 +595,16 @@
     returned = exchange(back, group)
 
     z_shape = (48, LANES)
-    halos = [in_vmem(halo) for halo in x_halo + y_halo]
+    halos = [in_vmem(halo) for halo in x_near + x_far + y_halo]
     field, *stepped = pl.pallas_call(
         functools.partial(first_step_kernel, size_x, size_y, turns_x),
         out_shape=[pltpu.VMEM(planes, F32)]
         + [pltpu.VMEM(x_shape, F32)] * turns_x
         + [pltpu.VMEM(y_shape, F32)] * 2
         + [jax.ShapeDtypeStruct(z_shape, F32)] * 2,
-        in_specs=[vmem] * (turns_x + 3) + [whole],
+        in_specs=[vmem] * (2 * turns_x + 3) + [whole],
         out_specs=[vmem] * (turns_x + 3) + [whole] * 2,
-        input_output_aliases={1 + i: 1 + i for i in range(turns_x + 2)},
+        input_output_aliases={1 + turns_x + i: 1 + i for i in range(turns_x + 2)},
         compiler_params=pltpu.CompilerParams(vmem_limit_bytes=8 * MIB),
         cost_estimate=lasts(1.6),
         name="first_gas_step",

time: 40.9 us -> 39.2 us (0.958)
  the two profiles are of different devices: /device:TPU:1 before, /device:TPU:11 now
where the time goes in v6:
time: 39.2 us; the launch traced here: 38.8 us
  starting transfers between devices  21.2 us (54%)
  Pallas kernels  13.9 us (35%)
  waiting for transfers between devices  2.92 us (7%)
  between operations  0.73 us (2%)
    all_to_all x2, starting transfers between devices, exchange(): lax.all_to_all(chunks, ('gy', 'gz'), split_axis=0, concat_axis=0, tiled=T...  12 us
    ppermute x7, starting transfers between devices, swap_all(): lax.ppermute(m, axis, pairs)  9.27 us
    pallas_call x1, Pallas kernels, on_device(): pl.pallas_call(functools.partial(couple_kernel, cap, packed), out_shape=[...  4.59 us
    ppermute x7, waiting for transfers between devices, swap_all(): lax.ppermute(m, axis, pairs)  2.92 us
    pallas_call x1, Pallas kernels, on_device(): pl.pallas_call(functools.partial(pack_kernel, cap, size_x, size_y, turns_...  2.69 us
    pallas_call x1, Pallas kernels, on_device(): pl.pallas_call(functools.partial(second_step_kernel, size_x, size_y, turn...  2.39 us
    pallas_call x1, Pallas kernels, on_device(): pl.pallas_call(functools.partial(first_step_kernel, size_x, size_y, turns...  1.71 us
    pallas_call x1, Pallas kernels, on_device(): pl.pallas_call(functools.partial(droplet_kernel, cap, packed), out_shape=...  1.68 us
  transfers between devices with their start and end apart: 9, of which 2 were waited for; matrix products, arithmetic and copies ran while one was open for 0% of the time, Pallas kernels for 25%

profile of v6, /device:TPU:11, one launch (start us, length us, event | category | flops | bytes accessed | tf_op | source)
XLA Modules:
  0.0 38.8 jit_solution(11994455007483746280)
XLA Ops:
  0.6 2.7 %pack.1 = (f32[256,128]{1,0:T(8,128)}, s32[1,128]{1,0:T(1,128)S(1)}, f32[32,64,128]{2,1,0:T(8,128)S(1)}, f32[8,64,128]{2,1,0:T(8,128)}, f32[8,64,128]{2,1,0:T(8,128)S(1)}) custom-call(f32[32,64,128]{2,1,0:T(8,128)} %state_in.1, f32[64,32,128]{2,1,0:T(8,128)} %bitcast.22, s32[1,128]{1,0:T(1,128)} %bitcast.23, s32[8,128]{1,0:T(8,128)} %refs_1_.1, ...), custom_call_target="tpu_custom_call" | custom-call | bytes 9225000 | tf_op jit(solution)/shard_map/pack/pallas_call | solution.py:520
  3.3 6.6 %all-to-all-start = ((f32[16,16,128]{2,1,0:T(8,128)}), f32[16,16,128]{2,1,0:T(8,128)S(1)}, u32[]{:S(2)}, u32[]{:S(2)}) async-start(f32[16,16,128]{2,1,0:T(8,128)} %bitcast.6), calls=%async_computation | async-start | bytes 262144 | tf_op jit(solution)/shard_map/all_to_all | solution.py:495
  10.0 0.8 %y_faces.1 = (f32[8,64,128]{2,1,0:T(8,128)}, f32[8,64,128]{2,1,0:T(8,128)}) custom-call(f32[32,64,128]{2,1,0:T(8,128)S(1)} %get-tuple-element.17.near_gas.gas), custom_call_target="tpu_custom_call" | custom-call | bytes 2214000 | tf_op jit(solution)/shard_map/y_faces/pallas_call | solution.py:555
  10.8 0.1 collective-permute-start.2
  10.9 4.2 %collective-permute-start.3 = (f32[8,64,128]{2,1,0:T(8,128)}, f32[8,64,128]{2,1,0:T(8,128)S(1)}, u32[]{:S(2)}, u32[]{:S(2)}) collective-permute-start(f32[8,64,128]{2,1,0:T(8,128)} %get-tuple-element.21), channel_id=1, source_target_pairs={{4,8},{8,4},{5,9},{9,5},{6,10},{10,6},{7,11},{11,7},{20,24},{24,20... | collective-permute-start | bytes 786440 | tf_op jit(solution)/shard_map/ppermute | solution.py:276
  15.1 0.3 collective-permute-start
  15.4 0.0 copy-start.1
  15.4 0.0 copy-start.2
  15.4 1.2 %collective-permute-start.1 = (f32[8,64,128]{2,1,0:T(8,128)S(1)}, f32[8,64,128]{2,1,0:T(8,128)S(1)}, u32[]{:S(2)}, u32[]{:S(2)}) collective-permute-start(f32[8,64,128]{2,1,0:T(8,128)S(1)} %get-tuple-element.19), channel_id=1, source_target_pairs={{0,16},{16,0},{1,17},{17,1},{2,18},{18,2},{3,19},{19,3},{4,20},{20... | collective-permute-start | bytes 786440 | tf_op jit(solution)/shard_map/ppermute | solution.py:276
  16.6 0.0 all-to-all-done
  16.6 0.0 copy-done.1
  16.6 0.0 copy-done.2
  16.6 4.6 %couple_gas.1 = (f32[128,128]{1,0:T(8,128)}, f32[32,64,128]{2,1,0:T(8,128)S(1)}) custom-call(f32[256,128]{1,0:T(8,128)S(1)} %bitcast.11, f32[32,64,128]{2,1,0:T(8,128)S(1)} %get-tuple-element.17.near_gas.gas, f32[1,64]{1,0:T(1,128)S(1)} %bitcast.14, f32[1,64]{1,0:T(1,128)S(1)} %bitcast.17), custom_call_target="tpu_custom_call" | custom-call | bytes 25830000 | tf_op jit(solution)/shard_map/couple_gas/pallas_call | solution.py:581
  21.2 5.4 %all-to-all-start.1 = ((f32[16,8,128]{2,1,0:T(8,128)}), f32[16,8,128]{2,1,0:T(8,128)S(1)}, u32[]{:S(2)}, u32[]{:S(2)}) async-start(f32[16,8,128]{2,1,0:T(8,128)} %bitcast.9), calls=%async_computation.1 | async-start | bytes 131072 | tf_op jit(solution)/shard_map/all_to_all | solution.py:495
  26.6 0.0 collective-permute-done.2.refs_2_.ya
  26.6 0.0 collective-permute-done.3.refs_3_.yb
  26.6 0.0 copy-start.3
  26.6 0.4 %collective-permute-start.4 = (f32[2,64,128]{2,1,0:T(8,128)S(1)}, f32[2,64,128]{2,1,0:T(8,128)S(1)}, u32[]{:S(2)}, u32[]{:S(2)}) collective-permute-start(f32[2,64,128]{2,1,0:T(8,128)S(1)} %corner_planes.1), channel_id=1, source_target_pairs={{0,16},{16,0},{1,17},{17,1},{2,18},{18,2},{3,19},{19,3},{4,20},{20... | collective-permute-start | bytes 196616 | tf_op jit(solution)/shard_map/ppermute | solution.py:276
  27.1 0.0 collective-permute-done.refs_0_
  27.1 0.8 %collective-permute-done.1.refs_1_ = f32[8,64,128]{2,1,0:T(8,128)S(1)} collective-permute-done((f32[8,64,128]{2,1,0:T(8,128)S(1)}, f32[8,64,128]{2,1,0:T(8,128)S(1)}, u32[]{:S(2)}, u32[]{:S(2)}) %collective-permute-start.1) | collective-permute-done | bytes 262176 | tf_op jit(solution)/shard_map/ppermute | solution.py:276
  27.9 0.0 copy-done.3
  27.9 1.7 %first_gas_step.1 = (f32[32,64,128]{2,1,0:T(8,128)S(1)}, f32[8,64,128]{2,1,0:T(8,128)S(1)}, f32[8,64,128]{2,1,0:T(8,128)S(1)}, f32[8,64,128]{2,1,0:T(8,128)S(1)}...) custom-call(f32[32,64,128]{2,1,0:T(8,128)S(1)} %get-tuple-element.17.ne, ...), custom_call_target="tpu_custom_call", output_to_operand_aliasing={{1}: (2, {}), {2}: (3, {}), {3}: (4, {})} | custom-call | bytes 5904000 | tf_op jit(solution)/shard_map/first_gas_step/pallas_call | solution.py:599
  29.6 1.9 %collective-permute-start.5 = (f32[48,128]{1,0:T(8,128)S(1)}, f32[48,128]{1,0:T(8,128)S(1)}, u32[]{:S(2)}, u32[]{:S(2)}) collective-permute-start(f32[48,128]{1,0:T(8,128)S(1)} %get-tuple-element.26.refs_4_), channel_id=1, source_target_pairs={{0,1},{2,3},{1,0},{3,2},{4,5},{6,7},{5,4},{7,6},{8,9},{10,11},{9,8... | collective-permute-start | bytes 73736 | tf_op jit(solution)/shard_map/ppermute | solution.py:276
  31.5 1.1 %collective-permute-start.6 = (f32[48,128]{1,0:T(8,128)S(1)}, f32[48,128]{1,0:T(8,128)S(1)}, u32[]{:S(2)}, u32[]{:S(2)}) collective-permute-start(f32[48,128]{1,0:T(8,128)S(1)} %get-tuple-element.27.refs_5_), channel_id=1, source_target_pairs={{1,2},{3,0},{2,1},{0,3},{5,6},{7,4},{6,5},{4,7},{9,10},{11,8},{10,... | collective-permute-start | bytes 73736 | tf_op jit(solution)/shard_map/ppermute | solution.py:276
  32.6 0.0 collective-permute-done.5.refs_6_
  32.6 2.1 %collective-permute-done.6.refs_7_ = f32[48,128]{1,0:T(8,128)S(1)} collective-permute-done((f32[48,128]{1,0:T(8,128)S(1)}, f32[48,128]{1,0:T(8,128)S(1)}, u32[]{:S(2)}, u32[]{:S(2)}) %collective-permute-start.6) | collective-permute-done | bytes 24608 | tf_op jit(solution)/shard_map/ppermute | solution.py:276
  34.7 0.0 collective-permute-done.4.refs_1_
  34.7 0.0 copy-start
  34.7 2.4 %second_gas_step.1._ = f32[64,32,128]{2,1,0:T(8,128)} custom-call(f32[32,64,128]{2,1,0:T(8,128)S(1)} %get-tuple-element.22.field, f32[8,64,128]{2,1,0:T(8,128)S(1)} %get-tuple-element.23.refs_0_, f32[2,64,128]{2,1,0:T(8,128)S(1)} %collective-permute-done.4.refs_1_, f32[8,64,128]{2,1,0:T(8,128)S(1)} %get-tuple-element.24.refs_2_, ...), custom_call_target="tpu_custom_call" | custom-call | bytes 14760000 | tf_op jit(solution)/shard_map/second_gas_step/pallas_call | solution.py:614
  37.1 0.0 all-to-all-done.1
  37.1 0.0 copy-done
  37.2 1.7 %droplets.1 = f32[32,64,128]{2,1,0:T(8,128)} custom-call(f32[32,64,128]{2,1,0:T(8,128)S(1)} %copy-done, f32[128,128]{1,0:T(8,128)S(1)} %bitcast.12, s32[1,128]{1,0:T(1,128)S(1)} %get-tuple-element.31.slots, f32[1,64]{1,0:T(1,128)S(1)} %bitcast.15, f32[1,64]{1,0:T(1,128)S(1)} %bitcast.18, f32[64,32,128]{2,1,0:T(8,128)} %second_gas_step.1._), custom_call_target="tpu_custom_call" | custom-call | bytes 9225000 | tf_op jit(solution)/shard_map/droplets/pallas_call | solution.py:630
  (1 shorter events, 0.0 us)
Async XLA Ops:
  3.3 13.3 %all-to-all-start = ((f32[16,16,128]{2,1,0:T(8,128)}), f32[16,16,128]{2,1,0:T(8,128)S(1)}, u32[]{:S(2)}, u32[]{:S(2)}) async-start(f32[16,16,128]{2,1,0:T(8,128)} %bitcast.6), calls=%async_computation | async-start | bytes 262144 | tf_op jit(solution)/shard_map/all_to_all | solution.py:495
  10.8 15.8 %collective-permute-start.2 = (f32[8,64,128]{2,1,0:T(8,128)}, f32[8,64,128]{2,1,0:T(8,128)S(1)}, u32[]{:S(2)}, u32[]{:S(2)}) collective-permute-start(f32[8,64,128]{2,1,0:T(8,128)} %get-tuple-element.20), channel_id=1, source_target_pairs={{0,4},{8,12},{4,0},{12,8},{1,5},{9,13},{5,1},{13,9},{2,6},{10,14},... | collective-permute-start | bytes 786440 | tf_op jit(solution)/shard_map/ppermute | solution.py:276
  10.9 15.7 %collective-permute-start.3 = (f32[8,64,128]{2,1,0:T(8,128)}, f32[8,64,128]{2,1,0:T(8,128)S(1)}, u32[]{:S(2)}, u32[]{:S(2)}) collective-permute-start(f32[8,64,128]{2,1,0:T(8,128)} %get-tuple-element.21), channel_id=1, source_target_pairs={{4,8},{8,4},{5,9},{9,5},{6,10},{10,6},{7,11},{11,7},{20,24},{24,20... | collective-permute-start | bytes 786440 | tf_op jit(solution)/shard_map/ppermute | solution.py:276
  15.1 12.0 %collective-permute-start = (f32[8,64,128]{2,1,0:T(8,128)}, f32[8,64,128]{2,1,0:T(8,128)S(1)}, u32[]{:S(2)}, u32[]{:S(2)}) collective-permute-start(f32[8,64,128]{2,1,0:T(8,128)} %get-tuple-element.18), channel_id=1, source_target_pairs={{0,16},{16,0},{1,17},{17,1},{2,18},{18,2},{3,19},{19,3},{4,20},{20... | collective-permute-start | bytes 786440 | tf_op jit(solution)/shard_map/ppermute | solution.py:276
  15.4 1.2 %copy-start.1 = (f32[64]{0:T(128)S(1)}, f32[64]{0:T(128)}, u32[]{:S(2)}) copy-start(f32[64]{0:T(128)} %param.15) | copy-start | bytes 772
  15.4 1.2 %copy-start.2 = (f32[64]{0:T(128)S(1)}, f32[64]{0:T(128)}, u32[]{:S(2)}) copy-start(f32[64]{0:T(128)} %param.16) | copy-start | bytes 772
  15.4 12.5 %collective-permute-start.1 = (f32[8,64,128]{2,1,0:T(8,128)S(1)}, f32[8,64,128]{2,1,0:T(8,128)S(1)}, u32[]{:S(2)}, u32[]{:S(2)}) collective-permute-start(f32[8,64,128]{2,1,0:T(8,128)S(1)} %get-tuple-element.19), channel_id=1, source_target_pairs={{0,16},{16,0},{1,17},{17,1},{2,18},{18,2},{3,19},{19,3},{4,20},{20... | collective-permute-start | bytes 786440 | tf_op jit(solution)/shard_map/ppermute | solution.py:276
  21.2 15.9 %all-to-all-start.1 = ((f32[16,8,128]{2,1,0:T(8,128)}), f32[16,8,128]{2,1,0:T(8,128)S(1)}, u32[]{:S(2)}, u32[]{:S(2)}) async-start(f32[16,8,128]{2,1,0:T(8,128)} %bitcast.9), calls=%async_computation.1 | async-start | bytes 131072 | tf_op jit(solution)/shard_map/all_to_all | solution.py:495
  26.6 1.2 %copy-start.3 = (f32[64]{0:T(128)S(1)}, f32[64]{0:T(128)}, u32[]{:S(2)}) copy-start(f32[64]{0:T(128)} %param.17) | copy-start | bytes 772
  26.6 8.1 %collective-permute-start.4 = (f32[2,64,128]{2,1,0:T(8,128)S(1)}, f32[2,64,128]{2,1,0:T(8,128)S(1)}, u32[]{:S(2)}, u32[]{:S(2)}) collective-permute-start(f32[2,64,128]{2,1,0:T(8,128)S(1)} %corner_planes.1), channel_id=1, source_target_pairs={{0,16},{16,0},{1,17},{17,1},{2,18},{18,2},{3,19},{19,3},{4,20},{20... | collective-permute-start | bytes 196616 | tf_op jit(solution)/shard_map/ppermute | solution.py:276
  29.6 3.0 %collective-permute-start.5 = (f32[48,128]{1,0:T(8,128)S(1)}, f32[48,128]{1,0:T(8,128)S(1)}, u32[]{:S(2)}, u32[]{:S(2)}) collective-permute-start(f32[48,128]{1,0:T(8,128)S(1)} %get-tuple-element.26.refs_4_), channel_id=1, source_target_pairs={{0,1},{2,3},{1,0},{3,2},{4,5},{6,7},{5,4},{7,6},{8,9},{10,11},{9,8... | collective-permute-start | bytes 73736 | tf_op jit(solution)/shard_map/ppermute | solution.py:276
  31.5 3.3 %collective-permute-start.6 = (f32[48,128]{1,0:T(8,128)S(1)}, f32[48,128]{1,0:T(8,128)S(1)}, u32[]{:S(2)}, u32[]{:S(2)}) collective-permute-start(f32[48,128]{1,0:T(8,128)S(1)} %get-tuple-element.27.refs_5_), channel_id=1, source_target_pairs={{1,2},{3,0},{2,1},{0,3},{5,6},{7,4},{6,5},{4,7},{9,10},{11,8},{10,... | collective-permute-start | bytes 73736 | tf_op jit(solution)/shard_map/ppermute | solution.py:276
  34.7 2.4 %copy-start = (f32[32,64,128]{2,1,0:T(8,128)S(1)}, f32[32,64,128]{2,1,0:T(8,128)}, u32[]{:S(2)}) copy-start(f32[32,64,128]{2,1,0:T(8,128)} %state_in.1) | copy-start | bytes 3145732

commit v7 on v6

--- a/solution.py
+++ b/solution.py
@@ -134,10 +134,10 @@
 
 def corner_kernel(size_x, ya, yb, *sends):
     even_x, _, _ = place_on("gx")
-    even_y, _, _ = place_on("gy")
+    even_y, below_y, above_y = place_on("gy")
     for turn, send in enumerate(sends):
         x = jnp.where(even_x == (turn == 0), size_x - 1, 0)
-        send[0], send[1] = low_high(even_y, ya[x], yb[x])
+        send[0], send[1] = low_high(even_y, ya[x], second_round(even_y, below_y, above_y, yb[x]))
 
 
 def couple_kernel(cap, packed, rows, gas, liquid, surface, back, deposit, w_high, w_low):
@@ -260,20 +260,29 @@
     return even, below, above
 
 
-def swaps(axis, wrap=False):
+def swaps(axis, closed=False, spare=None):
     count = lax.axis_size(axis)
+    across = 1 if spare is None else lax.axis_size(spare)
     rounds = []
     for first in range(2):
-        pairs = [(i, i + 1) for i in range(first, count - 1, 2)]
-        if wrap and first == 1 and count > 2 and count % 2 == 0:
-            pairs.append((count - 1, 0))
+        pairs = [(i * across + j, (i + 1) * across + j) for i in range(first, count - 1, 2) for j in range(across)]
+        if closed and first == 1 and count > 2 and count % 2 == 0:
+            if spare is None:
+                pairs.append((count - 1, 0))
+            elif across % 2 == 0:
+                pairs += [(i * across + j, i * across + j + 1) for i in (0, count - 1) for j in range(0, across, 2)]
         if pairs:
             rounds.append(pairs + [(j, i) for i, j in pairs])
     return rounds
 
 
-def swap_all(messages, axis, wrap=False):
-    return [lax.ppermute(m, axis, pairs) for m, pairs in zip(messages, swaps(axis, wrap), strict=True)]
+def swap_all(messages, axis, closed=False, spare=None):
+    axes = axis if spare is None else (axis, spare)
+    return [lax.ppermute(m, axes, pairs) for m, pairs in zip(messages, swaps(axis, closed, spare), strict=True)]
+
+
+def second_round(even, below, above, block):
+    return jnp.where(jnp.where(even, below, above) > 0.0, block, 0.0)
 
 
 def low_high(even, first, second):
@@ -332,7 +341,7 @@
         return low_high(even_x, near[0], near[1] if turns_x == 2 else None)[side]
 
     def from_y(side, x):
-        return low_high(even_y, ya[x], yb[x])[side]
+        return low_high(even_y, ya[x], second_round(even_y, below_y, above_y, yb[x]))[side]
 
     for x in range(size_x):
         for y in range(size_y):
@@ -389,70 +398,26 @@
     zb[...] = jnp.where(even_z, low, high)
 
 
-def second_step_kernel(
-    size_x, size_y, turns_x, field, *refs
-):
-    xs, refs = refs[:turns_x], refs[turns_x:]
-    corners, refs = refs[:turns_x], refs[turns_x:]
-    ya, yb, za, zb, za_in, zb_in, rate, deposit, out, now, now_x, now_y, result, sems = refs
+def second_step_kernel(size_x, size_y, turns_x, field, *refs):
+    xs, (ya, yb, rate, deposit, out) = refs[:turns_x], refs[turns_x:]
     species = rate.shape[1]
-    lines = size_x * size_y
     even_x, _, _ = place_on("gx")
-    even_y, _, _ = place_on("gy")
-    even, below, above = place_on("gz")
-    each = LANES // species
-    count = lines // each
-    rates = jnp.concatenate([rate[...]] * each, axis=1)
-    low, high = low_high(even, za_in[...], zb_in[...])
-    low, high = jnp.where(below > 0.0, low, 0.0), jnp.where(above > 0.0, high, 0.0)
-    own_low, own_high = low_high(even, za[...], zb[...])
-    next_low = rates * (low[count : 2 * count] + below * rates * own_low[:count])
-    next_high = rates * (high[count : 2 * count] + above * rates * own_high[:count])
-    low, high = rates * low, rates * high
-
-    def spread(low_row, high_row):
-        turned = iota((LANES, LANES), 0)
-        rows = jnp.where(turned == 0, low_row, jnp.where(turned == LANES - 1, high_row, 0.0))
-        return jnp.transpose(rows)
-
-    def row(i):
-        return spread(low[i : i + 1], high[i : i + 1])
-
-    def add_halo(target, source, start, count, first):
-        for i in range(count):
-            block = source[pl.ds(start + i * each, each)].reshape(LANES, LANES) + row(first + i)
-            target[i * each : (i + 1) * each] = block.reshape(each, species, LANES)
-
+    even_y, below_y, above_y = place_on("gy")
     wide = wide_rates(rate, species)
-    add_halo(now, field, 0, count, 0)
-    first = 2 * count
-    for turn, (ref, corner) in enumerate(zip(xs, corners, strict=True)):
-        add_halo(now_x.at[turn], ref, 0, size_y // each, first)
-        first = first + size_y // each
-        now_x[turn, 0] = now_x[turn, 0] + wide * corner[0]
-        now_x[turn, size_y - 1] = now_x[turn, size_y - 1] + wide * corner[1]
-    for turn, ref in enumerate((ya, yb)):
-        add_halo(now_y.at[turn], ref, size_x, size_x // each, first)
-        first = first + size_x // each
-        edges = [jnp.where(even_y == (turn == 0), corner[1], corner[0]) for corner in corners]
-        edges = low_high(even_x, edges[0], edges[1] if turns_x == 2 else None)
-        now_y[turn, 0] = now_y[turn, 0] + wide * edges[0]
-        now_y[turn, size_x - 1] = now_y[turn, size_x - 1] + wide * edges[1]
-
     keep = 1.0 - 6.0 * wide
-    planes = [[plane_at(now, x * size_y + y) for y in range(size_y)] for x in range(size_x)]
+    planes = [[plane_at(field, x * size_y + y) for y in range(size_y)] for x in range(size_x)]
 
     def from_x(side, y):
-        return low_high(even_x, now_x[0, y], now_x[1, y] if turns_x == 2 else None)[side]
+        return low_high(even_x, xs[0][y], xs[1][y] if turns_x == 2 else None)[side]
 
     def from_y(side, x):
-        return low_high(even_y, now_y[0, x], now_y[1, x])[side]
-
-    saves = []
+        second = second_round(even_y, below_y, above_y, yb[size_x + x])
+        return low_high(even_y, ya[size_x + x], second)[side]
+
     for x in range(size_x):
         for y in range(size_y):
             line = x * size_y + y
-            own = now[line]
+            own = field[line]
             total = beside_xy(
                 planes,
                 x,
@@ -462,11 +427,76 @@
                 functools.partial(from_y, 0),
                 functools.partial(from_y, 1),
             )
-            if line % each == 0:
-                i = line // each
-                ends = spread(next_low[i : i + 1], next_high[i : i + 1])
-            part = ends[line % each * species : (line % each + 1) * species]
-            result[line] = keep * own + wide * (total + beside_z(own)) + part + deposit[line]
+            out[line] = keep * own + wide * (total + beside_z(own)) + deposit[line]
+
+
+def close_kernel(size_x, size_y, turns_x, partial, *refs):
+    corners, (za, zb, za_in, zb_in, rate, out, result, sems) = refs[:turns_x], refs[turns_x:]
+    species = rate.shape[1]
+    lines = size_x * size_y
+    each = LANES // species
+    count, rows_x, rows_y = lines // each, size_y // each, size_x // each
+    even_x, _, _ = place_on("gx")
+    even_y, below_y, above_y = place_on("gy")
+    even, below, above = place_on("gz")
+    rates = jnp.concatenate([rate[...]] * each, axis=1)
+    keep = 1.0 - 6.0 * rates
+    incoming = low_high(even, za_in[...], zb_in[...])
+    leaving = low_high(even, za[...], zb[...])
+    row, lane = iota((count, LANES), 0), iota((count, LANES), 1)
+    first_place = (lane < species) & (row % rows_x == 0)
+    last_place = (lane >= LANES - species) & (row % rows_x == rows_x - 1)
+    blank = jnp.zeros((rows_x - 1, LANES), F32)
+    outer, inner = [], []
+    for column, own, exists in zip(incoming, leaving, (below, above), strict=True):
+        column = rates * jnp.where(exists > 0.0, column, 0.0)
+        main, partly = column[:count], column[count : 2 * count]
+        at = 2 * count
+        sides = [column[at + i * rows_x : at + (i + 1) * rows_x] for i in range(turns_x)]
+        x_low, x_high = low_high(even_x, sides[0], sides[1] if turns_x == 2 else None)
+        at = at + turns_x * rows_x
+        sides = [column[at + i * rows_y : at + (i + 1) * rows_y] for i in range(2)]
+        y_low, y_high = low_high(even_y, sides[0], second_round(even_y, below_y, above_y, sides[1]))
+        low_rows, high_rows = [], []
+        for x in range(size_x):
+            i, part = x // each, x % each
+            low_row, high_row = y_low[i : i + 1], y_high[i : i + 1]
+            if part > 0:
+                low_row = pltpu.roll(low_row, LANES - part * species, 1)
+            if part < each - 1:
+                high_row = pltpu.roll(high_row, (each - 1 - part) * species, 1)
+            low_rows += [low_row, blank]
+            high_rows += [blank, high_row]
+        ahead = pltpu.roll(main, LANES - species, 1)
+        after = jnp.where(lane >= LANES - species, jnp.concatenate([ahead[1:], ahead[-1:]], axis=0), ahead)
+        after = jnp.where(last_place, jnp.concatenate(high_rows, axis=0), after)
+        behind = pltpu.roll(main, species, 1)
+        before = jnp.where(lane < species, jnp.concatenate([behind[:1], behind[:-1]], axis=0), behind)
+        before = jnp.where(first_place, jnp.concatenate(low_rows, axis=0), before)
+        total = before + after + jnp.concatenate([x_low, main[:-rows_x]], axis=0)
+        total = total + jnp.concatenate([main[rows_x:], x_high], axis=0)
+        outer.append(keep * main + rates * total + partly + exists * rates * rates * own[:count])
+        inner.append(rates * main)
+
+    wide = wide_rates(rate, species)
+    twice = 2.0 * wide * wide
+    edge = {}
+    for i, y in enumerate((0, size_y - 1)):
+        planes = low_high(even_x, corners[0][i], corners[1][i] if turns_x == 2 else None)
+        edge[y], edge[lines - size_y + y] = planes
+    turned = iota((LANES, LANES), 0)
+    saves = []
+    for i in range(count):
+        at = slice(i, i + 1)
+        block = jnp.where(turned == 0, outer[0][at], jnp.where(turned == 1, inner[0][at], 0.0))
+        block = jnp.where(turned == LANES - 2, inner[1][at], block)
+        block = jnp.transpose(jnp.where(turned == LANES - 1, outer[1][at], block))
+        for part in range(each):
+            line = i * each + part
+            total = partial[line] + block[part * species : (part + 1) * species]
+            if line in edge:
+                total = total + twice * edge[line]
+            result[line] = total
             saves.append(pltpu.make_async_copy(result.at[line], out.at[:, line, :], sems.at[line]))
             saves[-1].start()
     for save in saves:
@@ -561,7 +591,7 @@
         cost_estimate=lasts(0.6),
         name="y_faces",
     )(near_gas)
-    y_halo = swap_all(y_faces, "gy")
+    y_halo = swap_all(y_faces, "gy", closed=True, spare="gz")
     x_near = swap_all(x_faces[:turns_x], "gx")
     x_far = swap_all(x_faces[turns_x:], "gx")
 
@@ -610,23 +640,26 @@
         name="first_gas_step",
     )(near_gas, *halos, rate)
     halos, z_sends = stepped[:-2], stepped[-2:]
-    z_halo = swap_all(z_sends, "gz", wrap=True)
+    z_halo = swap_all(z_sends, "gz", closed=True)
+    partial = pl.pallas_call(
+        functools.partial(second_step_kernel, size_x, size_y, turns_x),
+        out_shape=pltpu.VMEM(planes, F32),
+        in_specs=[vmem] * (turns_x + 3) + [whole, vmem],
+        out_specs=vmem,
+        compiler_params=pltpu.CompilerParams(vmem_limit_bytes=4 * MIB),
+        cost_estimate=lasts(1.3),
+        name="second_gas_step",
+    )(field, *halos, rate, in_vmem(deposit))
     gas_next = pl.pallas_call(
-        functools.partial(second_step_kernel, size_x, size_y, turns_x),
+        functools.partial(close_kernel, size_x, size_y, turns_x),
         out_shape=jax.ShapeDtypeStruct(flat.shape, F32),
-        in_specs=[vmem] * (2 * turns_x + 3) + [whole] * 5 + [vmem],
+        in_specs=[vmem] * (1 + turns_x) + [whole] * 5,
         out_specs=hbm,
-        scratch_shapes=[
-            pltpu.VMEM(planes, F32),
-            pltpu.VMEM((turns_x, size_y, species, LANES), F32),
-            pltpu.VMEM((2, size_x, species, LANES), F32),
-            pltpu.VMEM(planes, F32),
-            pltpu.SemaphoreType.DMA((lines,)),
-        ],
-        compiler_params=pltpu.CompilerParams(vmem_limit_bytes=10 * MIB),
-        cost_estimate=lasts(4.0),
-        name="second_gas_step",
-    )(field, *halos[:turns_x], *corners, *halos[turns_x:], *z_sends, *z_halo, rate, in_vmem(deposit))
+        scratch_shapes=[pltpu.VMEM(planes, F32), pltpu.SemaphoreType.DMA((lines,))],
+        compiler_params=pltpu.CompilerParams(vmem_limit_bytes=6 * MIB),
+        cost_estimate=lasts(1.5),
+        name="close_gas_step",
+    )(in_vmem(partial), *corners, *z_sends, *z_halo, rate)
     droplet_next = pl.pallas_call(
         functools.partial(droplet_kernel, cap, packed),
         out_shape=jax.ShapeDtypeStruct(droplet.shape, F32),

time: 39.2 us -> 37.7 us (0.962)
  the two profiles are of different devices: /device:TPU:11 before, /device:TPU:1 now
where the time goes in v7:
time: 37.7 us; the launch traced here: 37.2 us
  starting transfers between devices  19.1 us (51%)
  Pallas kernels  13.7 us (36%)
  waiting for transfers between devices  3.63 us (10%)
  between operations  0.74 us (2%)
    all_to_all x2, starting transfers between devices, exchange(): lax.all_to_all(chunks, ('gy', 'gz'), split_axis=0, concat_axis=0, tiled=T...  12.3 us
    ppermute x7, starting transfers between devices, swap_all(): lax.ppermute(m, axes, pairs)  6.83 us
    pallas_call x1, Pallas kernels, on_device(): pl.pallas_call(functools.partial(couple_kernel, cap, packed), out_shape=[...  4.59 us
    pallas_call x1, Pallas kernels, on_device(): pl.pallas_call(functools.partial(pack_kernel, cap, size_x, size_y, turns_...  2.69 us
    all_to_all x2, waiting for transfers between devices, exchange(): lax.all_to_all(chunks, ('gy', 'gz'), split_axis=0, concat_axis=0, tiled=T...  2.56 us
    pallas_call x1, Pallas kernels, on_device(): pl.pallas_call(functools.partial(first_step_kernel, size_x, size_y, turns...  1.71 us
    pallas_call x1, Pallas kernels, on_device(): pl.pallas_call(functools.partial(droplet_kernel, cap, packed), out_shape=...  1.68 us
    pallas_call x1, Pallas kernels, on_device(): pl.pallas_call(functools.partial(close_kernel, size_x, size_y, turns_x),...  1.48 us
  transfers between devices with their start and end apart: 9, of which 2 were waited for; matrix products, arithmetic and copies ran while one was open for 0% of the time, Pallas kernels for 25%

profile of v7, /device:TPU:1, one launch (start us, length us, event | category | flops | bytes accessed | tf_op | source)
XLA Modules:
  0.0 37.2 jit_solution(353163481627298730)
XLA Ops:
  0.6 2.7 %pack.1 = (f32[256,128]{1,0:T(8,128)}, s32[1,128]{1,0:T(1,128)S(1)}, f32[32,64,128]{2,1,0:T(8,128)S(1)}, f32[8,64,128]{2,1,0:T(8,128)}, f32[8,64,128]{2,1,0:T(8,128)S(1)}) custom-call(f32[32,64,128]{2,1,0:T(8,128)} %state_in.1, f32[64,32,128]{2,1,0:T(8,128)} %bitcast.23, s32[1,128]{1,0:T(1,128)} %bitcast.24, s32[8,128]{1,0:T(8,128)} %refs_1_.1, ...), custom_call_target="tpu_custom_call" | custom-call | bytes 9225000 | tf_op jit(solution)/shard_map/pack/pallas_call | solution.py:550
  3.3 7.4 %all-to-all-start = ((f32[16,16,128]{2,1,0:T(8,128)}), f32[16,16,128]{2,1,0:T(8,128)S(1)}, u32[]{:S(2)}, u32[]{:S(2)}) async-start(f32[16,16,128]{2,1,0:T(8,128)} %bitcast.6), calls=%async_computation | async-start | bytes 262144 | tf_op jit(solution)/shard_map/all_to_all | solution.py:525
  10.7 0.8 %y_faces.1 = (f32[8,64,128]{2,1,0:T(8,128)}, f32[8,64,128]{2,1,0:T(8,128)}) custom-call(f32[32,64,128]{2,1,0:T(8,128)S(1)} %get-tuple-element.17.near_gas.gas), custom_call_target="tpu_custom_call" | custom-call | bytes 2214000 | tf_op jit(solution)/shard_map/y_faces/pallas_call | solution.py:585
  11.5 1.4 %collective-permute-start.2 = (f32[8,64,128]{2,1,0:T(8,128)}, f32[8,64,128]{2,1,0:T(8,128)S(1)}, u32[]{:S(2)}, u32[]{:S(2)}) collective-permute-start(f32[8,64,128]{2,1,0:T(8,128)} %get-tuple-element.20), channel_id=1, source_target_pairs={{0,4},{1,5},{2,6},{3,7},{8,12},{9,13},{10,14},{11,15},{4,0},{5,1},... | collective-permute-start | bytes 786440 | tf_op jit(solution)/shard_map/ppermute | solution.py:281
  12.9 0.6 %collective-permute-start.3 = (f32[8,64,128]{2,1,0:T(8,128)}, f32[8,64,128]{2,1,0:T(8,128)S(1)}, u32[]{:S(2)}, u32[]{:S(2)}) collective-permute-start(f32[8,64,128]{2,1,0:T(8,128)} %get-tuple-element.21), channel_id=1, source_target_pairs={{4,8},{5,9},{6,10},{7,11},{0,1},{2,3},{12,13},{14,15},{8,4},{9,5},... | collective-permute-start | bytes 786440 | tf_op jit(solution)/shard_map/ppermute | solution.py:281
  13.6 1.2 %collective-permute-start = (f32[8,64,128]{2,1,0:T(8,128)}, f32[8,64,128]{2,1,0:T(8,128)S(1)}, u32[]{:S(2)}, u32[]{:S(2)}) collective-permute-start(f32[8,64,128]{2,1,0:T(8,128)} %get-tuple-element.18), channel_id=1, source_target_pairs={{0,16},{16,0},{1,17},{17,1},{2,18},{18,2},{3,19},{19,3},{4,20},{20... | collective-permute-start | bytes 786440 | tf_op jit(solution)/shard_map/ppermute | solution.py:281
  14.8 0.0 copy-start.2
  14.8 0.0 copy-start.3
  14.8 0.3 collective-permute-start.1
  15.0 2.6 %all-to-all-done = f32[16,16,128]{2,1,0:T(8,128)S(1)} async-done(((f32[16,16,128]{2,1,0:T(8,128)}), f32[16,16,128]{2,1,0:T(8,128)S(1)}, u32[]{:S(2)}, u32[]{:S(2)}) %all-to-all-start) | async-done | bytes 131104 | tf_op jit(solution)/shard_map/all_to_all | solution.py:525
  17.6 0.0 copy-done.2
  17.6 0.0 copy-done.3
  17.6 4.6 %couple_gas.1 = (f32[128,128]{1,0:T(8,128)}, f32[32,64,128]{2,1,0:T(8,128)S(1)}) custom-call(f32[256,128]{1,0:T(8,128)S(1)} %bitcast.11, f32[32,64,128]{2,1,0:T(8,128)S(1)} %get-tuple-element.17.near_gas.gas, f32[1,64]{1,0:T(1,128)S(1)} %bitcast.17, f32[1,64]{1,0:T(1,128)S(1)} %bitcast.20), custom_call_target="tpu_custom_call" | custom-call | bytes 25830000 | tf_op jit(solution)/shard_map/couple_gas/pallas_call | solution.py:611
  22.2 4.9 %all-to-all-start.1 = ((f32[16,8,128]{2,1,0:T(8,128)}), f32[16,8,128]{2,1,0:T(8,128)S(1)}, u32[]{:S(2)}, u32[]{:S(2)}) async-start(f32[16,8,128]{2,1,0:T(8,128)} %bitcast.9), calls=%async_computation.1 | async-start | bytes 131072 | tf_op jit(solution)/shard_map/all_to_all | solution.py:525
  27.1 0.0 collective-permute-done.2.refs_2_.ya
  27.1 0.0 collective-permute-done.3.refs_3_.yb
  27.2 0.0 copy-start.1
  27.2 1.3 %collective-permute-start.4 = (f32[2,64,128]{2,1,0:T(8,128)S(1)}, f32[2,64,128]{2,1,0:T(8,128)S(1)}, u32[]{:S(2)}, u32[]{:S(2)}) collective-permute-start(f32[2,64,128]{2,1,0:T(8,128)S(1)} %corner_planes.1), channel_id=1, source_target_pairs={{0,16},{16,0},{1,17},{17,1},{2,18},{18,2},{3,19},{19,3},{4,20},{20... | collective-permute-start | bytes 196616 | tf_op jit(solution)/shard_map/ppermute | solution.py:281
  28.4 0.0 collective-permute-done.refs_0_
  28.4 0.0 collective-permute-done.1.refs_1_
  28.5 0.0 copy-done.1
  28.5 1.7 %first_gas_step.1 = (f32[32,64,128]{2,1,0:T(8,128)S(1)}, f32[8,64,128]{2,1,0:T(8,128)S(1)}, f32[8,64,128]{2,1,0:T(8,128)S(1)}, f32[8,64,128]{2,1,0:T(8,128)S(1)}...) custom-call(f32[32,64,128]{2,1,0:T(8,128)S(1)} %get-tuple-element.17.ne, ...), custom_call_target="tpu_custom_call", output_to_operand_aliasing={{1}: (2, {}), {2}: (3, {}), {3}: (4, {})} | custom-call | bytes 5904000 | tf_op jit(solution)/shard_map/first_gas_step/pallas_call | solution.py:629
  30.2 0.6 %collective-permute-start.5 = (f32[48,128]{1,0:T(8,128)S(1)}, f32[48,128]{1,0:T(8,128)S(1)}, u32[]{:S(2)}, u32[]{:S(2)}) collective-permute-start(f32[48,128]{1,0:T(8,128)S(1)} %get-tuple-element.28.refs_1_), channel_id=1, source_target_pairs={{0,1},{2,3},{1,0},{3,2},{4,5},{6,7},{5,4},{7,6},{8,9},{10,11},{9,8... | collective-permute-start | bytes 73736 | tf_op jit(solution)/shard_map/ppermute | solution.py:281
  30.7 1.5 %collective-permute-start.6 = (f32[48,128]{1,0:T(8,128)S(1)}, f32[48,128]{1,0:T(8,128)S(1)}, u32[]{:S(2)}, u32[]{:S(2)}) collective-permute-start(f32[48,128]{1,0:T(8,128)S(1)} %get-tuple-element.29.refs_2_), channel_id=1, source_target_pairs={{1,2},{3,0},{2,1},{0,3},{5,6},{7,4},{6,5},{4,7},{9,10},{11,8},{10,... | collective-permute-start | bytes 73736 | tf_op jit(solution)/shard_map/ppermute | solution.py:281
  32.2 0.7 %second_gas_step.1.partial = f32[32,64,128]{2,1,0:T(8,128)S(1)} custom-call(f32[32,64,128]{2,1,0:T(8,128)S(1)} %get-tuple-element.22.field, f32[8,64,128]{2,1,0:T(8,128)S(1)} %get-tuple-element.23.refs_0_, f32[8,64,128]{2,1,0:T(8,128)S(1)} %get-tuple-element.24.refs_1_, f32[8,64,128]{2,1,0:T(8,128)S(1)} %get-tuple-element.25.refs_2_, f32[1,64]{1,0:T(1,128)S(1)} %bitcast.14, ...), custom_call_target="tpu_custom_call" | custom-call | bytes 4797000 | tf_op jit(solution)/shard_map/second_gas_step/pallas_call | solution.py:644
  32.9 0.0 copy-start
  32.9 0.0 collective-permute-done.5.refs_3_
  33.0 1.1 %collective-permute-done.6.refs_4_ = f32[48,128]{1,0:T(8,128)S(1)} collective-permute-done((f32[48,128]{1,0:T(8,128)S(1)}, f32[48,128]{1,0:T(8,128)S(1)}, u32[]{:S(2)}, u32[]{:S(2)}) %collective-permute-start.6) | collective-permute-done | bytes 24608 | tf_op jit(solution)/shard_map/ppermute | solution.py:281
  34.0 0.0 collective-permute-done.4.refs_0_
  34.0 1.5 %close_gas_step.1._ = f32[64,32,128]{2,1,0:T(8,128)} custom-call(f32[32,64,128]{2,1,0:T(8,128)S(1)} %second_gas_step.1.partial, f32[2,64,128]{2,1,0:T(8,128)S(1)} %collective-permute-done.4.refs_0_, f32[48,128]{1,0:T(8,128)S(1)} %get-tuple-element.28.refs_1_, f32[48,128]{1,0:T(8,128)S(1)} %get-tuple-element.29.refs_2_, ...), custom_call_target="tpu_custom_call" | custom-call | bytes 5535000 | tf_op jit(solution)/shard_map/close_gas_step/pallas_call | solution.py:653
  35.5 0.0 all-to-all-done.1
  35.5 0.0 copy-done
  35.5 1.7 %droplets.1 = f32[32,64,128]{2,1,0:T(8,128)} custom-call(f32[32,64,128]{2,1,0:T(8,128)S(1)} %copy-done, f32[128,128]{1,0:T(8,128)S(1)} %bitcast.12, s32[1,128]{1,0:T(1,128)S(1)} %get-tuple-element.31.slots, f32[1,64]{1,0:T(1,128)S(1)} %bitcast.18, f32[1,64]{1,0:T(1,128)S(1)} %bitcast.21, f32[64,32,128]{2,1,0:T(8,128)} %close_gas_step.1._), custom_call_target="tpu_custom_call" | custom-call | bytes 9225000 | tf_op jit(solution)/shard_map/droplets/pallas_call | solution.py:663
  (1 shorter events, 0.0 us)
Async XLA Ops:
  3.3 14.3 %all-to-all-start = ((f32[16,16,128]{2,1,0:T(8,128)}), f32[16,16,128]{2,1,0:T(8,128)S(1)}, u32[]{:S(2)}, u32[]{:S(2)}) async-start(f32[16,16,128]{2,1,0:T(8,128)} %bitcast.6), calls=%async_computation | async-start | bytes 262144 | tf_op jit(solution)/shard_map/all_to_all | solution.py:525
  11.5 15.6 %collective-permute-start.2 = (f32[8,64,128]{2,1,0:T(8,128)}, f32[8,64,128]{2,1,0:T(8,128)S(1)}, u32[]{:S(2)}, u32[]{:S(2)}) collective-permute-start(f32[8,64,128]{2,1,0:T(8,128)} %get-tuple-element.20), channel_id=1, source_target_pairs={{0,4},{1,5},{2,6},{3,7},{8,12},{9,13},{10,14},{11,15},{4,0},{5,1},... | collective-permute-start | bytes 786440 | tf_op jit(solution)/shard_map/ppermute | solution.py:281
  12.9 14.2 %collective-permute-start.3 = (f32[8,64,128]{2,1,0:T(8,128)}, f32[8,64,128]{2,1,0:T(8,128)S(1)}, u32[]{:S(2)}, u32[]{:S(2)}) collective-permute-start(f32[8,64,128]{2,1,0:T(8,128)} %get-tuple-element.21), channel_id=1, source_target_pairs={{4,8},{5,9},{6,10},{7,11},{0,1},{2,3},{12,13},{14,15},{8,4},{9,5},... | collective-permute-start | bytes 786440 | tf_op jit(solution)/shard_map/ppermute | solution.py:281
  13.6 14.9 %collective-permute-start = (f32[8,64,128]{2,1,0:T(8,128)}, f32[8,64,128]{2,1,0:T(8,128)S(1)}, u32[]{:S(2)}, u32[]{:S(2)}) collective-permute-start(f32[8,64,128]{2,1,0:T(8,128)} %get-tuple-element.18), channel_id=1, source_target_pairs={{0,16},{16,0},{1,17},{17,1},{2,18},{18,2},{3,19},{19,3},{4,20},{20... | collective-permute-start | bytes 786440 | tf_op jit(solution)/shard_map/ppermute | solution.py:281
  14.8 2.8 %copy-start.2 = (f32[64]{0:T(128)S(1)}, f32[64]{0:T(128)}, u32[]{:S(2)}) copy-start(f32[64]{0:T(128)} %param.15) | copy-start | bytes 772
  14.8 2.8 %copy-start.3 = (f32[64]{0:T(128)S(1)}, f32[64]{0:T(128)}, u32[]{:S(2)}) copy-start(f32[64]{0:T(128)} %param.16) | copy-start | bytes 772
  14.8 13.7 %collective-permute-start.1 = (f32[8,64,128]{2,1,0:T(8,128)S(1)}, f32[8,64,128]{2,1,0:T(8,128)S(1)}, u32[]{:S(2)}, u32[]{:S(2)}) collective-permute-start(f32[8,64,128]{2,1,0:T(8,128)S(1)} %get-tuple-element.19), channel_id=1, source_target_pairs={{0,16},{16,0},{1,17},{17,1},{2,18},{18,2},{3,19},{19,3},{4,20},{20... | collective-permute-start | bytes 786440 | tf_op jit(solution)/shard_map/ppermute | solution.py:281
  22.2 13.3 %all-to-all-start.1 = ((f32[16,8,128]{2,1,0:T(8,128)}), f32[16,8,128]{2,1,0:T(8,128)S(1)}, u32[]{:S(2)}, u32[]{:S(2)}) async-start(f32[16,8,128]{2,1,0:T(8,128)} %bitcast.9), calls=%async_computation.1 | async-start | bytes 131072 | tf_op jit(solution)/shard_map/all_to_all | solution.py:525
  27.2 1.3 %copy-start.1 = (f32[64]{0:T(128)S(1)}, f32[64]{0:T(128)}, u32[]{:S(2)}) copy-start(f32[64]{0:T(128)} %param.17) | copy-start | bytes 772
  27.2 6.8 %collective-permute-start.4 = (f32[2,64,128]{2,1,0:T(8,128)S(1)}, f32[2,64,128]{2,1,0:T(8,128)S(1)}, u32[]{:S(2)}, u32[]{:S(2)}) collective-permute-start(f32[2,64,128]{2,1,0:T(8,128)S(1)} %corner_planes.1), channel_id=1, source_target_pairs={{0,16},{16,0},{1,17},{17,1},{2,18},{18,2},{3,19},{19,3},{4,20},{20... | collective-permute-start | bytes 196616 | tf_op jit(solution)/shard_map/ppermute | solution.py:281
  30.2 2.8 %collective-permute-start.5 = (f32[48,128]{1,0:T(8,128)S(1)}, f32[48,128]{1,0:T(8,128)S(1)}, u32[]{:S(2)}, u32[]{:S(2)}) collective-permute-start(f32[48,128]{1,0:T(8,128)S(1)} %get-tuple-element.28.refs_1_), channel_id=1, source_target_pairs={{0,1},{2,3},{1,0},{3,2},{4,5},{6,7},{5,4},{7,6},{8,9},{10,11},{9,8... | collective-permute-start | bytes 73736 | tf_op jit(solution)/shard_map/ppermute | solution.py:281
  30.7 3.3 %collective-permute-start.6 = (f32[48,128]{1,0:T(8,128)S(1)}, f32[48,128]{1,0:T(8,128)S(1)}, u32[]{:S(2)}, u32[]{:S(2)}) collective-permute-start(f32[48,128]{1,0:T(8,128)S(1)} %get-tuple-element.29.refs_2_), channel_id=1, source_target_pairs={{1,2},{3,0},{2,1},{0,3},{5,6},{7,4},{6,5},{4,7},{9,10},{11,8},{10,... | collective-permute-start | bytes 73736 | tf_op jit(solution)/shard_map/ppermute | solution.py:281
  32.9 2.6 %copy-start = (f32[32,64,128]{2,1,0:T(8,128)S(1)}, f32[32,64,128]{2,1,0:T(8,128)}, u32[]{:S(2)}) copy-start(f32[32,64,128]{2,1,0:T(8,128)} %state_in.1) | copy-start | bytes 3145732

commit v8 on v7

--- a/solution.py
+++ b/solution.py
@@ -317,46 +317,108 @@
     return jnp.broadcast_to(column, (rows, LANES))
 
 
-def columns_of(block):
-    turned = jnp.transpose(block)
-    return turned[:1], turned[-1:]
-
-
-def first_step_kernel(size_x, size_y, turns_x, gas, *refs):
+def beside_in_rows(size_x, size_y, main, x_low, x_high, y_low, y_high):
+    count = main.shape[0]
+    each = size_x * size_y // count
+    species = LANES // each
+    rows_x = size_y // each
+    row, lane = iota((count, LANES), 0), iota((count, LANES), 1)
+    first_place = (lane < species) & (row % rows_x == 0)
+    last_place = (lane >= LANES - species) & (row % rows_x == rows_x - 1)
+    blank = jnp.zeros((rows_x - 1, LANES), F32)
+    low_rows, high_rows = [], []
+    for x in range(size_x):
+        i, part = x // each, x % each
+        low_row, high_row = y_low[i : i + 1], y_high[i : i + 1]
+        if part > 0:
+            low_row = pltpu.roll(low_row, LANES - part * species, 1)
+        if part < each - 1:
+            high_row = pltpu.roll(high_row, (each - 1 - part) * species, 1)
+        low_rows += [low_row, blank]
+        high_rows += [blank, high_row]
+    ahead = pltpu.roll(main, LANES - species, 1)
+    after = jnp.where(lane >= LANES - species, jnp.concatenate([ahead[1:], ahead[-1:]], axis=0), ahead)
+    after = jnp.where(last_place, jnp.concatenate(high_rows, axis=0), after)
+    behind = pltpu.roll(main, species, 1)
+    before = jnp.where(lane < species, jnp.concatenate([behind[:1], behind[:-1]], axis=0), behind)
+    before = jnp.where(first_place, jnp.concatenate(low_rows, axis=0), before)
+    total = before + after + jnp.concatenate([x_low, main[:-rows_x]], axis=0)
+    return total + jnp.concatenate([main[rows_x:], x_high], axis=0)
+
+
+def z_message_kernel(size_x, size_y, turns_x, gas, *refs):
+    xs, (ya, yb, rate, za, zb) = refs[:turns_x], refs[turns_x:]
+    species = rate.shape[1]
+    lines = size_x * size_y
+    each = LANES // species
+    rates = jnp.concatenate([rate[...]] * each, axis=1)
+    keep = 1.0 - 6.0 * rates
+    even_x, _, _ = place_on("gx")
+    even_y, below_y, above_y = place_on("gy")
+    even_z, _, _ = place_on("gz")
+
+    def columns(ref):
+        turned = [jnp.transpose(ref[i : i + each].reshape(LANES, LANES)) for i in range(0, ref.shape[0], each)]
+        return [jnp.concatenate([t[z : z + 1] for t in turned], axis=0) for z in (0, 1, LANES - 1, LANES - 2)]
+
+    main = columns(gas)
+    x_sides = [columns(x) for x in xs]
+    y_sides = [columns(y.at[:size_x]) for y in (ya, yb)]
+    messages = []
+    for side in range(2):
+        own, inner = main[2 * side], main[2 * side + 1]
+        from_x = [columns_of_x[2 * side] for columns_of_x in x_sides]
+        from_y = [columns_of_y[2 * side] for columns_of_y in y_sides]
+        x_low, x_high = low_high(even_x, from_x[0], from_x[1] if turns_x == 2 else None)
+        y_low, y_high = low_high(even_y, from_y[0], second_round(even_y, below_y, above_y, from_y[1]))
+        total = inner + beside_in_rows(size_x, size_y, own, x_low, x_high, y_low, y_high)
+        parts = [own, keep * own + rates * total] + from_x + from_y
+        filled = sum(part.shape[0] for part in parts)
+        parts.append(jnp.zeros((za.shape[0] - filled, LANES), F32))
+        messages.append(jnp.concatenate(parts, axis=0))
+    low, high = messages
+    za[...] = jnp.where(even_z, high, low)
+    zb[...] = jnp.where(even_z, low, high)
+
+
+def steps_kernel(size_x, size_y, turns_x, gas, *refs):
     xs, refs = refs[:turns_x], refs[turns_x:]
     xs_far, refs = refs[:turns_x], refs[turns_x:]
-    (ya, yb, rate, field), refs = refs[:4], refs[4:]
-    xs_out, (ya_out, yb_out, za, zb) = refs[:turns_x], refs[turns_x:]
+    ya, yb, rate, deposit, out, field, side_x, side_y = refs
     species = rate.shape[1]
     lines = size_x * size_y
     even_x, below_x, above_x = place_on("gx")
     even_y, below_y, above_y = place_on("gy")
-    even_z, _, _ = place_on("gz")
     wide = wide_rates(rate, species)
     keep = 1.0 - 6.0 * wide
-    planes = [[plane_at(gas, x * size_y + y) for y in range(size_y)] for x in range(size_x)]
-
-    def from_x(side, y):
-        near = [ref[y] for ref in xs]
-        return low_high(even_x, near[0], near[1] if turns_x == 2 else None)[side]
-
-    def from_y(side, x):
-        return low_high(even_y, ya[x], second_round(even_y, below_y, above_y, yb[x]))[side]
-
-    for x in range(size_x):
-        for y in range(size_y):
-            own = gas[x * size_y + y]
-            total = beside_xy(
-                planes,
-                x,
-                y,
-                functools.partial(from_x, 0),
-                functools.partial(from_x, 1),
-                functools.partial(from_y, 0),
-                functools.partial(from_y, 1),
-            )
-            field[x * size_y + y] = keep * own + wide * (total + beside_z(own))
-
+
+    def step(source, x_halos, y_halos, store):
+        planes = [[plane_at(source, x * size_y + y) for y in range(size_y)] for x in range(size_x)]
+
+        def from_x(side, y):
+            return low_high(even_x, x_halos[0][y], x_halos[1][y] if turns_x == 2 else None)[side]
+
+        def from_y(side, x):
+            return low_high(even_y, y_halos[0][x], second_round(even_y, below_y, above_y, y_halos[1][x]))[side]
+
+        for x in range(size_x):
+            for y in range(size_y):
+                own = source[x * size_y + y]
+                total = beside_xy(
+                    planes,
+                    x,
+                    y,
+                    functools.partial(from_x, 0),
+                    functools.partial(from_x, 1),
+                    functools.partial(from_y, 0),
+                    functools.partial(from_y, 1),
+                )
+                store(x * size_y + y, keep * own + wide * (total + beside_z(own)))
+
+    def store_field(line, value):
+        field[line] = value
+
+    step(gas, xs, (ya, yb), store_field)
     for turn, ref in enumerate(xs):
         up = even_x == (turn == 0)
         exists = jnp.where(up, above_x, below_x)
@@ -368,9 +430,9 @@
                 total = total + ref[y - 1]
             if y < size_y - 1:
                 total = total + ref[y + 1]
-            xs_out[turn][y] = keep * own + wide * (total + beside_z(own))
-
-    for turn, (ref, ref_out) in enumerate(((ya, ya_out), (yb, yb_out))):
+            side_x[turn, y] = keep * own + wide * (total + beside_z(own))
+
+    for turn, ref in enumerate((ya, yb)):
         up = even_y == (turn == 0)
         exists = jnp.where(up, above_y, below_y)
         inner = jnp.where(up, size_y - 1, 0)
@@ -381,53 +443,12 @@
                 total = total + ref[x - 1]
             if x < size_x - 1:
                 total = total + ref[x + 1]
-            ref_out[size_x + x] = keep * own + wide * (total + beside_z(own))
-
-    rows = []
-    each = LANES // species
-    for ref in (gas, field):
-        rows += [columns_of(ref[i : i + each].reshape(LANES, LANES)) for i in range(0, lines, each)]
-    for ref in xs:
-        rows += [columns_of(ref[i : i + each].reshape(LANES, LANES)) for i in range(0, size_y, each)]
-    for ref in (ya, yb):
-        rows += [columns_of(ref[i : i + each].reshape(LANES, LANES)) for i in range(0, size_x, each)]
-    rest = [jnp.zeros((za.shape[0] - len(rows), LANES), F32)]
-    low = jnp.concatenate([row[0] for row in rows] + rest, axis=0)
-    high = jnp.concatenate([row[1] for row in rows] + rest, axis=0)
-    za[...] = jnp.where(even_z, high, low)
-    zb[...] = jnp.where(even_z, low, high)
-
-
-def second_step_kernel(size_x, size_y, turns_x, field, *refs):
-    xs, (ya, yb, rate, deposit, out) = refs[:turns_x], refs[turns_x:]
-    species = rate.shape[1]
-    even_x, _, _ = place_on("gx")
-    even_y, below_y, above_y = place_on("gy")
-    wide = wide_rates(rate, species)
-    keep = 1.0 - 6.0 * wide
-    planes = [[plane_at(field, x * size_y + y) for y in range(size_y)] for x in range(size_x)]
-
-    def from_x(side, y):
-        return low_high(even_x, xs[0][y], xs[1][y] if turns_x == 2 else None)[side]
-
-    def from_y(side, x):
-        second = second_round(even_y, below_y, above_y, yb[size_x + x])
-        return low_high(even_y, ya[size_x + x], second)[side]
-
-    for x in range(size_x):
-        for y in range(size_y):
-            line = x * size_y + y
-            own = field[line]
-            total = beside_xy(
-                planes,
-                x,
-                y,
-                functools.partial(from_x, 0),
-                functools.partial(from_x, 1),
-                functools.partial(from_y, 0),
-                functools.partial(from_y, 1),
-            )
-            out[line] = keep * own + wide * (total + beside_z(own)) + deposit[line]
+            side_y[turn, x] = keep * own + wide * (total + beside_z(own))
+
+    def store_result(line, value):
+        out[line] = value + deposit[line]
+
+    step(field, [side_x.at[turn] for turn in range(turns_x)], [side_y.at[turn] for turn in range(2)], store_result)
 
 
 def close_kernel(size_x, size_y, turns_x, partial, *refs):
@@ -443,10 +464,6 @@
     keep = 1.0 - 6.0 * rates
     incoming = low_high(even, za_in[...], zb_in[...])
     leaving = low_high(even, za[...], zb[...])
-    row, lane = iota((count, LANES), 0), iota((count, LANES), 1)
-    first_place = (lane < species) & (row % rows_x == 0)
-    last_place = (lane >= LANES - species) & (row % rows_x == rows_x - 1)
-    blank = jnp.zeros((rows_x - 1, LANES), F32)
     outer, inner = [], []
     for column, own, exists in zip(incoming, leaving, (below, above), strict=True):
         column = rates * jnp.where(exists > 0.0, column, 0.0)
@@ -457,24 +474,7 @@
         at = at + turns_x * rows_x
         sides = [column[at + i * rows_y : at + (i + 1) * rows_y] for i in range(2)]
         y_low, y_high = low_high(even_y, sides[0], second_round(even_y, below_y, above_y, sides[1]))
-        low_rows, high_rows = [], []
-        for x in range(size_x):
-            i, part = x // each, x % each
-            low_row, high_row = y_low[i : i + 1], y_high[i : i + 1]
-            if part > 0:
-                low_row = pltpu.roll(low_row, LANES - part * species, 1)
-            if part < each - 1:
-                high_row = pltpu.roll(high_row, (each - 1 - part) * species, 1)
-            low_rows += [low_row, blank]
-            high_rows += [blank, high_row]
-        ahead = pltpu.roll(main, LANES - species, 1)
-        after = jnp.where(lane >= LANES - species, jnp.concatenate([ahead[1:], ahead[-1:]], axis=0), ahead)
-        after = jnp.where(last_place, jnp.concatenate(high_rows, axis=0), after)
-        behind = pltpu.roll(main, species, 1)
-        before = jnp.where(lane < species, jnp.concatenate([behind[:1], behind[:-1]], axis=0), behind)
-        before = jnp.where(first_place, jnp.concatenate(low_rows, axis=0), before)
-        total = before + after + jnp.concatenate([x_low, main[:-rows_x]], axis=0)
-        total = total + jnp.concatenate([main[rows_x:], x_high], axis=0)
+        total = beside_in_rows(size_x, size_y, main, x_low, x_high, y_low, y_high)
         outer.append(keep * main + rates * total + partly + exists * rates * rates * own[:count])
         inner.append(rates * main)
 
@@ -625,31 +625,30 @@
     returned = exchange(back, group)
 
     z_shape = (48, LANES)
-    halos = [in_vmem(halo) for halo in x_near + x_far + y_halo]
-    field, *stepped = pl.pallas_call(
-        functools.partial(first_step_kernel, size_x, size_y, turns_x),
-        out_shape=[pltpu.VMEM(planes, F32)]
-        + [pltpu.VMEM(x_shape, F32)] * turns_x
-        + [pltpu.VMEM(y_shape, F32)] * 2
-        + [jax.ShapeDtypeStruct(z_shape, F32)] * 2,
-        in_specs=[vmem] * (2 * turns_x + 3) + [whole],
-        out_specs=[vmem] * (turns_x + 3) + [whole] * 2,
-        input_output_aliases={1 + turns_x + i: 1 + i for i in range(turns_x + 2)},
-        compiler_params=pltpu.CompilerParams(vmem_limit_bytes=8 * MIB),
-        cost_estimate=lasts(1.6),
-        name="first_gas_step",
-    )(near_gas, *halos, rate)
-    halos, z_sends = stepped[:-2], stepped[-2:]
+    x_near, x_far, y_halo = [[in_vmem(halo) for halo in halos] for halos in (x_near, x_far, y_halo)]
+    z_sends = pl.pallas_call(
+        functools.partial(z_message_kernel, size_x, size_y, turns_x),
+        out_shape=[jax.ShapeDtypeStruct(z_shape, F32)] * 2,
+        in_specs=[vmem] * (turns_x + 3) + [whole],
+        compiler_params=pltpu.CompilerParams(vmem_limit_bytes=4 * MIB),
+        cost_estimate=lasts(0.6),
+        name="z_message",
+    )(near_gas, *x_near, *y_halo, rate)
     z_halo = swap_all(z_sends, "gz", closed=True)
     partial = pl.pallas_call(
-        functools.partial(second_step_kernel, size_x, size_y, turns_x),
+        functools.partial(steps_kernel, size_x, size_y, turns_x),
         out_shape=pltpu.VMEM(planes, F32),
-        in_specs=[vmem] * (turns_x + 3) + [whole, vmem],
+        in_specs=[vmem] * (2 * turns_x + 3) + [whole, vmem],
         out_specs=vmem,
-        compiler_params=pltpu.CompilerParams(vmem_limit_bytes=4 * MIB),
-        cost_estimate=lasts(1.3),
-        name="second_gas_step",
-    )(field, *halos, rate, in_vmem(deposit))
+        scratch_shapes=[
+            pltpu.VMEM(planes, F32),
+            pltpu.VMEM((turns_x, size_y, species, LANES), F32),
+            pltpu.VMEM((2, size_x, species, LANES), F32),
+        ],
+        compiler_params=pltpu.CompilerParams(vmem_limit_bytes=6 * MIB),
+        cost_estimate=lasts(2.2),
+        name="gas_steps",
+    )(near_gas, *x_near, *x_far, *y_halo, rate, in_vmem(deposit))
     gas_next = pl.pallas_call(
         functools.partial(close_kernel, size_x, size_y, turns_x),
         out_shape=jax.ShapeDtypeStruct(flat.shape, F32),

time: 37.7 us -> 36.7 us (0.973)
  waiting for transfers between devices: 3.63 us -> 3 us
    ppermute x7, waiting for transfers between devices: 1.07 us -> 0.44 us  [swap_all(): lax.ppermute(m, axes, pairs)]
where the time goes in v8:
time: 36.7 us; the launch traced here: 36.4 us
  starting transfers between devices  19.1 us (52%)
  Pallas kernels  13.5 us (37%)
  waiting for transfers between devices  3 us (8%)
  between operations  0.73 us (2%)
    all_to_all x2, starting transfers between devices, exchange(): lax.all_to_all(chunks, ('gy', 'gz'), split_axis=0, concat_axis=0, tiled=T...  12.3 us
    ppermute x7, starting transfers between devices, swap_all(): lax.ppermute(m, axes, pairs)  6.83 us
    pallas_call x1, Pallas kernels, on_device(): pl.pallas_call(functools.partial(couple_kernel, cap, packed), out_shape=[...  4.59 us
    pallas_call x1, Pallas kernels, on_device(): pl.pallas_call(functools.partial(pack_kernel, cap, size_x, size_y, turns_...  2.69 us
    all_to_all x2, waiting for transfers between devices, exchange(): lax.all_to_all(chunks, ('gy', 'gz'), split_axis=0, concat_axis=0, tiled=T...  2.56 us
    pallas_call x1, Pallas kernels, on_device(): pl.pallas_call(functools.partial(droplet_kernel, cap, packed), out_shape=...  1.68 us
    pallas_call x1, Pallas kernels, on_device(): pl.pallas_call(functools.partial(steps_kernel, size_x, size_y, turns_x),...  1.66 us
    pallas_call x1, Pallas kernels, on_device(): pl.pallas_call(functools.partial(close_kernel, size_x, size_y, turns_x),...  1.48 us
  transfers between devices with their start and end apart: 9, of which 2 were waited for; matrix products, arithmetic and copies ran while one was open for 0% of the time, Pallas kernels for 25%

profile of v8, /device:TPU:1, one launch (start us, length us, event | category | flops | bytes accessed | tf_op | source)
XLA Modules:
  0.0 36.4 jit_solution(932455683293292084)
XLA Ops:
  0.6 2.7 %pack.1 = (f32[256,128]{1,0:T(8,128)}, s32[1,128]{1,0:T(1,128)S(1)}, f32[32,64,128]{2,1,0:T(8,128)S(1)}, f32[8,64,128]{2,1,0:T(8,128)}, f32[8,64,128]{2,1,0:T(8,128)S(1)}) custom-call(f32[32,64,128]{2,1,0:T(8,128)} %state_in.1, f32[64,32,128]{2,1,0:T(8,128)} %bitcast.23, s32[1,128]{1,0:T(1,128)} %bitcast.24, s32[8,128]{1,0:T(8,128)} %refs_1_.1, ...), custom_call_target="tpu_custom_call" | custom-call | bytes 9225000 | tf_op jit(solution)/shard_map/pack/pallas_call | solution.py:550
  3.3 7.4 %all-to-all-start = ((f32[16,16,128]{2,1,0:T(8,128)}), f32[16,16,128]{2,1,0:T(8,128)S(1)}, u32[]{:S(2)}, u32[]{:S(2)}) async-start(f32[16,16,128]{2,1,0:T(8,128)} %bitcast.6), calls=%async_computation | async-start | bytes 262144 | tf_op jit(solution)/shard_map/all_to_all | solution.py:525
  10.7 0.8 %y_faces.1 = (f32[8,64,128]{2,1,0:T(8,128)}, f32[8,64,128]{2,1,0:T(8,128)}) custom-call(f32[32,64,128]{2,1,0:T(8,128)S(1)} %get-tuple-element.13.near_gas.gas), custom_call_target="tpu_custom_call" | custom-call | bytes 2214000 | tf_op jit(solution)/shard_map/y_faces/pallas_call | solution.py:585
  11.5 1.4 %collective-permute-start.2 = (f32[8,64,128]{2,1,0:T(8,128)}, f32[8,64,128]{2,1,0:T(8,128)S(1)}, u32[]{:S(2)}, u32[]{:S(2)}) collective-permute-start(f32[8,64,128]{2,1,0:T(8,128)} %get-tuple-element.16), channel_id=1, source_target_pairs={{0,4},{1,5},{2,6},{3,7},{8,12},{9,13},{10,14},{11,15},{4,0},{5,1},... | collective-permute-start | bytes 786440 | tf_op jit(solution)/shard_map/ppermute | solution.py:281
  12.9 0.6 %collective-permute-start.3 = (f32[8,64,128]{2,1,0:T(8,128)}, f32[8,64,128]{2,1,0:T(8,128)S(1)}, u32[]{:S(2)}, u32[]{:S(2)}) collective-permute-start(f32[8,64,128]{2,1,0:T(8,128)} %get-tuple-element.17), channel_id=1, source_target_pairs={{4,8},{5,9},{6,10},{7,11},{0,1},{2,3},{12,13},{14,15},{8,4},{9,5},... | collective-permute-start | bytes 786440 | tf_op jit(solution)/shard_map/ppermute | solution.py:281
  13.6 1.2 %collective-permute-start = (f32[8,64,128]{2,1,0:T(8,128)}, f32[8,64,128]{2,1,0:T(8,128)S(1)}, u32[]{:S(2)}, u32[]{:S(2)}) collective-permute-start(f32[8,64,128]{2,1,0:T(8,128)} %get-tuple-element.14), channel_id=1, source_target_pairs={{0,16},{16,0},{1,17},{17,1},{2,18},{18,2},{3,19},{19,3},{4,20},{20... | collective-permute-start | bytes 786440 | tf_op jit(solution)/shard_map/ppermute | solution.py:281
  14.8 0.0 copy-start.1
  14.8 0.0 copy-start.2
  14.8 0.3 collective-permute-start.1
  15.0 2.6 %all-to-all-done = f32[16,16,128]{2,1,0:T(8,128)S(1)} async-done(((f32[16,16,128]{2,1,0:T(8,128)}), f32[16,16,128]{2,1,0:T(8,128)S(1)}, u32[]{:S(2)}, u32[]{:S(2)}) %all-to-all-start) | async-done | bytes 131104 | tf_op jit(solution)/shard_map/all_to_all | solution.py:525
  17.6 0.0 copy-done.1
  17.6 0.0 copy-done.2
  17.6 4.6 %couple_gas.1 = (f32[128,128]{1,0:T(8,128)}, f32[32,64,128]{2,1,0:T(8,128)S(1)}) custom-call(f32[256,128]{1,0:T(8,128)S(1)} %bitcast.11, f32[32,64,128]{2,1,0:T(8,128)S(1)} %get-tuple-element.13.near_gas.gas, f32[1,64]{1,0:T(1,128)S(1)} %bitcast.14, f32[1,64]{1,0:T(1,128)S(1)} %bitcast.17), custom_call_target="tpu_custom_call" | custom-call | bytes 25830000 | tf_op jit(solution)/shard_map/couple_gas/pallas_call | solution.py:611
  22.2 4.9 %all-to-all-start.1 = ((f32[16,8,128]{2,1,0:T(8,128)}), f32[16,8,128]{2,1,0:T(8,128)S(1)}, u32[]{:S(2)}, u32[]{:S(2)}) async-start(f32[16,8,128]{2,1,0:T(8,128)} %bitcast.9), calls=%async_computation.1 | async-start | bytes 131072 | tf_op jit(solution)/shard_map/all_to_all | solution.py:525
  27.1 0.0 collective-permute-done.2.refs_2_.ya.refs_1_
  27.1 0.0 collective-permute-done.3.refs_3_.yb.refs_2_
  27.2 0.0 copy-start.3
  27.2 1.3 %collective-permute-start.4 = (f32[2,64,128]{2,1,0:T(8,128)S(1)}, f32[2,64,128]{2,1,0:T(8,128)S(1)}, u32[]{:S(2)}, u32[]{:S(2)}) collective-permute-start(f32[2,64,128]{2,1,0:T(8,128)S(1)} %corner_planes.1), channel_id=1, source_target_pairs={{0,16},{16,0},{1,17},{17,1},{2,18},{18,2},{3,19},{19,3},{4,20},{20... | collective-permute-start | bytes 196616 | tf_op jit(solution)/shard_map/ppermute | solution.py:281
  28.4 0.0 collective-permute-done.refs_0_
  28.4 0.0 copy-done.3
  28.5 0.6 %z_message.1 = (f32[48,128]{1,0:T(8,128)S(1)}, f32[48,128]{1,0:T(8,128)S(1)}) custom-call(f32[32,64,128]{2,1,0:T(8,128)S(1)} %get-tuple-element.13.near_gas.gas, f32[8,64,128]{2,1,0:T(8,128)S(1)} %collective-permute-done.refs_0_, f32[8,64,128]{2,1,0:T(8,128)S(1)} %collective-permute-done.2.refs_2_.ya.refs_1_, ...), custom_call_target="tpu_custom_call" | custom-call | bytes 2214000 | tf_op jit(solution)/shard_map/z_message/pallas_call | solution.py:629
  29.0 0.6 %collective-permute-start.5 = (f32[48,128]{1,0:T(8,128)S(1)}, f32[48,128]{1,0:T(8,128)S(1)}, u32[]{:S(2)}, u32[]{:S(2)}) collective-permute-start(f32[48,128]{1,0:T(8,128)S(1)} %get-tuple-element.20.refs_1_), channel_id=1, source_target_pairs={{0,1},{2,3},{1,0},{3,2},{4,5},{6,7},{5,4},{7,6},{8,9},{10,11},{9,8... | collective-permute-start | bytes 73736 | tf_op jit(solution)/shard_map/ppermute | solution.py:281
  29.6 1.5 %collective-permute-start.6 = (f32[48,128]{1,0:T(8,128)S(1)}, f32[48,128]{1,0:T(8,128)S(1)}, u32[]{:S(2)}, u32[]{:S(2)}) collective-permute-start(f32[48,128]{1,0:T(8,128)S(1)} %get-tuple-element.21.refs_2_), channel_id=1, source_target_pairs={{1,2},{3,0},{2,1},{0,3},{5,6},{7,4},{6,5},{4,7},{9,10},{11,8},{10,... | collective-permute-start | bytes 73736 | tf_op jit(solution)/shard_map/ppermute | solution.py:281
  31.1 0.0 collective-permute-done.1.refs_1_
  31.1 1.7 %gas_steps.1.partial = f32[32,64,128]{2,1,0:T(8,128)S(1)} custom-call(f32[32,64,128]{2,1,0:T(8,128)S(1)} %get-tuple-element.13.near_gas.gas, f32[8,64,128]{2,1,0:T(8,128)S(1)} %collective-permute-done.refs_0_, f32[8,64,128]{2,1,0:T(8,128)S(1)} %collective-permute-done.1.refs_1_, f32[8,64,128]{2,1,0:T(8,128)S(1)} %collective-permute-done.2.refs_2_.ya.refs_1_, ...), custom_call_target="tpu_custom_call" | custom-call | bytes 8118000 | tf_op jit(solution)/shard_map/gas_steps/pallas_call | solution.py:638
  32.8 0.0 copy-start
  32.8 0.0 collective-permute-done.5.refs_3_
  32.8 0.4 %collective-permute-done.6.refs_4_ = f32[48,128]{1,0:T(8,128)S(1)} collective-permute-done((f32[48,128]{1,0:T(8,128)S(1)}, f32[48,128]{1,0:T(8,128)S(1)}, u32[]{:S(2)}, u32[]{:S(2)}) %collective-permute-start.6) | collective-permute-done | bytes 24608 | tf_op jit(solution)/shard_map/ppermute | solution.py:281
  33.2 0.0 collective-permute-done.4.refs_0_
  33.2 1.5 %close_gas_step.1._ = f32[64,32,128]{2,1,0:T(8,128)} custom-call(f32[32,64,128]{2,1,0:T(8,128)S(1)} %gas_steps.1.partial, f32[2,64,128]{2,1,0:T(8,128)S(1)} %collective-permute-done.4.refs_0_, f32[48,128]{1,0:T(8,128)S(1)} %get-tuple-element.20.refs_1_, f32[48,128]{1,0:T(8,128)S(1)} %get-tuple-element.21.refs_2_, ...), custom_call_target="tpu_custom_call" | custom-call | bytes 5535000 | tf_op jit(solution)/shard_map/close_gas_step/pallas_call | solution.py:652
  34.7 0.0 all-to-all-done.1
  34.7 0.0 copy-done
  34.7 1.7 %droplets.1 = f32[32,64,128]{2,1,0:T(8,128)} custom-call(f32[32,64,128]{2,1,0:T(8,128)S(1)} %copy-done, f32[128,128]{1,0:T(8,128)S(1)} %bitcast.12, s32[1,128]{1,0:T(1,128)S(1)} %get-tuple-element.23.slots, f32[1,64]{1,0:T(1,128)S(1)} %bitcast.15, f32[1,64]{1,0:T(1,128)S(1)} %bitcast.18, f32[64,32,128]{2,1,0:T(8,128)} %close_gas_step.1._), custom_call_target="tpu_custom_call" | custom-call | bytes 9225000 | tf_op jit(solution)/shard_map/droplets/pallas_call | solution.py:662
  (1 shorter events, 0.0 us)
Async XLA Ops:
  3.3 14.3 %all-to-all-start = ((f32[16,16,128]{2,1,0:T(8,128)}), f32[16,16,128]{2,1,0:T(8,128)S(1)}, u32[]{:S(2)}, u32[]{:S(2)}) async-start(f32[16,16,128]{2,1,0:T(8,128)} %bitcast.6), calls=%async_computation | async-start | bytes 262144 | tf_op jit(solution)/shard_map/all_to_all | solution.py:525
  11.5 15.6 %collective-permute-start.2 = (f32[8,64,128]{2,1,0:T(8,128)}, f32[8,64,128]{2,1,0:T(8,128)S(1)}, u32[]{:S(2)}, u32[]{:S(2)}) collective-permute-start(f32[8,64,128]{2,1,0:T(8,128)} %get-tuple-element.16), channel_id=1, source_target_pairs={{0,4},{1,5},{2,6},{3,7},{8,12},{9,13},{10,14},{11,15},{4,0},{5,1},... | collective-permute-start | bytes 786440 | tf_op jit(solution)/shard_map/ppermute | solution.py:281
  12.9 14.2 %collective-permute-start.3 = (f32[8,64,128]{2,1,0:T(8,128)}, f32[8,64,128]{2,1,0:T(8,128)S(1)}, u32[]{:S(2)}, u32[]{:S(2)}) collective-permute-start(f32[8,64,128]{2,1,0:T(8,128)} %get-tuple-element.17), channel_id=1, source_target_pairs={{4,8},{5,9},{6,10},{7,11},{0,1},{2,3},{12,13},{14,15},{8,4},{9,5},... | collective-permute-start | bytes 786440 | tf_op jit(solution)/shard_map/ppermute | solution.py:281
  13.6 14.9 %collective-permute-start = (f32[8,64,128]{2,1,0:T(8,128)}, f32[8,64,128]{2,1,0:T(8,128)S(1)}, u32[]{:S(2)}, u32[]{:S(2)}) collective-permute-start(f32[8,64,128]{2,1,0:T(8,128)} %get-tuple-element.14), channel_id=1, source_target_pairs={{0,16},{16,0},{1,17},{17,1},{2,18},{18,2},{3,19},{19,3},{4,20},{20... | collective-permute-start | bytes 786440 | tf_op jit(solution)/shard_map/ppermute | solution.py:281
  14.8 2.8 %copy-start.1 = (f32[64]{0:T(128)S(1)}, f32[64]{0:T(128)}, u32[]{:S(2)}) copy-start(f32[64]{0:T(128)} %param.15) | copy-start | bytes 772
  14.8 2.8 %copy-start.2 = (f32[64]{0:T(128)S(1)}, f32[64]{0:T(128)}, u32[]{:S(2)}) copy-start(f32[64]{0:T(128)} %param.16) | copy-start | bytes 772
  14.8 16.3 %collective-permute-start.1 = (f32[8,64,128]{2,1,0:T(8,128)S(1)}, f32[8,64,128]{2,1,0:T(8,128)S(1)}, u32[]{:S(2)}, u32[]{:S(2)}) collective-permute-start(f32[8,64,128]{2,1,0:T(8,128)S(1)} %get-tuple-element.15), channel_id=1, source_target_pairs={{0,16},{16,0},{1,17},{17,1},{2,18},{18,2},{3,19},{19,3},{4,20},{20... | collective-permute-start | bytes 786440 | tf_op jit(solution)/shard_map/ppermute | solution.py:281
  22.2 12.5 %all-to-all-start.1 = ((f32[16,8,128]{2,1,0:T(8,128)}), f32[16,8,128]{2,1,0:T(8,128)S(1)}, u32[]{:S(2)}, u32[]{:S(2)}) async-start(f32[16,8,128]{2,1,0:T(8,128)} %bitcast.9), calls=%async_computation.1 | async-start | bytes 131072 | tf_op jit(solution)/shard_map/all_to_all | solution.py:525
  27.2 1.3 %copy-start.3 = (f32[64]{0:T(128)S(1)}, f32[64]{0:T(128)}, u32[]{:S(2)}) copy-start(f32[64]{0:T(128)} %param.17) | copy-start | bytes 772
  27.2 6.0 %collective-permute-start.4 = (f32[2,64,128]{2,1,0:T(8,128)S(1)}, f32[2,64,128]{2,1,0:T(8,128)S(1)}, u32[]{:S(2)}, u32[]{:S(2)}) collective-permute-start(f32[2,64,128]{2,1,0:T(8,128)S(1)} %corner_planes.1), channel_id=1, source_target_pairs={{0,16},{16,0},{1,17},{17,1},{2,18},{18,2},{3,19},{19,3},{4,20},{20... | collective-permute-start | bytes 196616 | tf_op jit(solution)/shard_map/ppermute | solution.py:281
  29.0 3.7 %collective-permute-start.5 = (f32[48,128]{1,0:T(8,128)S(1)}, f32[48,128]{1,0:T(8,128)S(1)}, u32[]{:S(2)}, u32[]{:S(2)}) collective-permute-start(f32[48,128]{1,0:T(8,128)S(1)} %get-tuple-element.20.refs_1_), channel_id=1, source_target_pairs={{0,1},{2,3},{1,0},{3,2},{4,5},{6,7},{5,4},{7,6},{8,9},{10,11},{9,8... | collective-permute-start | bytes 73736 | tf_op jit(solution)/shard_map/ppermute | solution.py:281
  29.6 3.6 %collective-permute-start.6 = (f32[48,128]{1,0:T(8,128)S(1)}, f32[48,128]{1,0:T(8,128)S(1)}, u32[]{:S(2)}, u32[]{:S(2)}) collective-permute-start(f32[48,128]{1,0:T(8,128)S(1)} %get-tuple-element.21.refs_2_), channel_id=1, source_target_pairs={{1,2},{3,0},{2,1},{0,3},{5,6},{7,4},{6,5},{4,7},{9,10},{11,8},{10,... | collective-permute-start | bytes 73736 | tf_op jit(solution)/shard_map/ppermute | solution.py:281
  32.8 2.0 %copy-start = (f32[32,64,128]{2,1,0:T(8,128)S(1)}, f32[32,64,128]{2,1,0:T(8,128)}, u32[]{:S(2)}) copy-start(f32[32,64,128]{2,1,0:T(8,128)} %state_in.1) | copy-start | bytes 3145732

commit v9 on v8

--- a/solution.py
+++ b/solution.py
@@ -140,7 +140,7 @@
         send[0], send[1] = low_high(even_y, ya[x], second_round(even_y, below_y, above_y, yb[x]))
 
 
-def couple_kernel(cap, packed, rows, gas, liquid, surface, back, deposit, w_high, w_low):
+def couple_kernel(cap, packed, rows, gas, liquid, surface, back_out, deposit, w_high, w_low, back, sems):
     slots = rows.shape[0]
     species = liquid.shape[1]
     lines = gas.shape[0]
@@ -157,6 +157,7 @@
     cell = cell.astype(jnp.int32)
     high_rows, low_rows = split(whole)
     named = [jnp.broadcast_to(cell[k : k + 1], (tile, slots)).astype(jnp.int16) for k in range(STENCIL)]
+    first_cells = iota((tile, slots), 0).astype(jnp.int16)
     highs = [jnp.broadcast_to(high_rows[k : k + 1], (tile, slots)) for k in range(STENCIL)]
     lows = [jnp.broadcast_to(low_rows[k : k + 1], (tile, slots)) for k in range(STENCIL)]
 
@@ -167,7 +168,7 @@
     for line in range(0, lines, 2):
         for part in range(2):
             for z in range(0, LANES, tile):
-                along = (iota((tile, slots), 0) + ((line + part) * LANES + z)).astype(jnp.int16)
+                along = first_cells + jnp.int16((line + part) * LANES + z)
                 high = jnp.zeros((tile, slots), BF16)
                 low = jnp.zeros((tile, slots), BF16)
                 for k in range(STENCIL):
@@ -188,6 +189,8 @@
         back[...] = gas_rows.reshape(slots // 2, 2 * species)
     else:
         back[...] = jnp.concatenate([gas_rows, jnp.zeros((slots, LANES - species), F32)], axis=1)
+    save = pltpu.make_async_copy(back, back_out, sems.at[0])
+    save.start()
     response = surface_response(as_column(liquid[...]), as_column(surface[...]))
     s_high, s_low = split(table[:species] + mass * (response * gathered))
     s_all = jnp.concatenate([s_high, s_low], axis=0)
@@ -198,6 +201,7 @@
         for i in range(2):
             turned = jnp.transpose(both[i * LANES : (i + 1) * LANES])
             deposit[line + i] = turned[:species] + turned[species:]
+    save.wait()
 
 
 def droplet_kernel(
@@ -227,7 +231,7 @@
         at = pl.ds(i * block, block)
         return pltpu.make_async_copy(state_next.at[:, at], state_out.at[:, at], sems.at[i])
 
-    @pl.loop(0, species // block, unroll=4)
+    @pl.loop(0, species // block, unroll=8)
     def _(i):
         at = pl.ds(pl.multiple_of(i * block, block), block)
         pick = i * block + iota((block, species), 0) == iota((block, species), 1)
@@ -610,12 +614,14 @@
     w_shape = (lines, LANES, slots)
     back, deposit = pl.pallas_call(
         functools.partial(couple_kernel, cap, packed),
-        out_shape=[pltpu.VMEM((back_rows, LANES), F32), pltpu.VMEM(planes, F32)],
+        out_shape=[jax.ShapeDtypeStruct((back_rows, LANES), F32), pltpu.VMEM(planes, F32)],
         in_specs=[vmem] * 2 + [whole] * 2,
-        out_specs=[vmem, vmem],
+        out_specs=[hbm, vmem],
         scratch_shapes=[
             pltpu.VMEM(w_shape, BF16),
             pltpu.VMEM(w_shape, BF16),
+            pltpu.VMEM((back_rows, LANES), F32),
+            pltpu.SemaphoreType.DMA((1,)),
         ],
         compiler_params=pltpu.CompilerParams(vmem_limit_bytes=10 * MIB),
         cost_estimate=lasts(7.0),

time: 36.7 us -> 36.5 us (level)
  no operation moved by 1% of the time
where the time goes in v9:
time: 36.5 us; the launch traced here: 36.2 us
  starting transfers between devices  19.1 us (52%)
  Pallas kernels  13.4 us (37%)
  waiting for transfers between devices  3 us (8%)
  between operations  0.73 us (2%)
    all_to_all x2, starting transfers between devices, exchange(): lax.all_to_all(chunks, ('gy', 'gz'), split_axis=0, concat_axis=0, tiled=T...  12.3 us
    ppermute x7, starting transfers between devices, swap_all(): lax.ppermute(m, axes, pairs)  6.83 us
    pallas_call x1, Pallas kernels, on_device(): pl.pallas_call(functools.partial(couple_kernel, cap, packed), out_shape=[...  4.47 us
    pallas_call x1, Pallas kernels, on_device(): pl.pallas_call(functools.partial(pack_kernel, cap, size_x, size_y, turns_...  2.69 us
    all_to_all x2, waiting for transfers between devices, exchange(): lax.all_to_all(chunks, ('gy', 'gz'), split_axis=0, concat_axis=0, tiled=T...  2.56 us
    pallas_call x1, Pallas kernels, on_device(): pl.pallas_call(functools.partial(steps_kernel, size_x, size_y, turns_x),...  1.66 us
    pallas_call x1, Pallas kernels, on_device(): pl.pallas_call(functools.partial(droplet_kernel, cap, packed), out_shape=...  1.62 us
    pallas_call x1, Pallas kernels, on_device(): pl.pallas_call(functools.partial(close_kernel, size_x, size_y, turns_x),...  1.48 us
  transfers between devices with their start and end apart: 9, of which 2 were waited for; matrix products, arithmetic and copies ran while one was open for 0% of the time, Pallas kernels for 25%

profile of v9, /device:TPU:1, one launch (start us, length us, event | category | flops | bytes accessed | tf_op | source)
XLA Modules:
  0.0 36.2 jit_solution(16073794398751823845)
XLA Ops:
  0.6 2.7 %pack.1 = (f32[256,128]{1,0:T(8,128)}, s32[1,128]{1,0:T(1,128)S(1)}, f32[32,64,128]{2,1,0:T(8,128)S(1)}, f32[8,64,128]{2,1,0:T(8,128)}, f32[8,64,128]{2,1,0:T(8,128)S(1)}) custom-call(f32[32,64,128]{2,1,0:T(8,128)} %state_in.1, f32[64,32,128]{2,1,0:T(8,128)} %bitcast.23, s32[1,128]{1,0:T(1,128)} %bitcast.24, s32[8,128]{1,0:T(8,128)} %refs_1_.1, ...), custom_call_target="tpu_custom_call" | custom-call | bytes 9225000 | tf_op jit(solution)/shard_map/pack/pallas_call | solution.py:554
  3.3 7.4 %all-to-all-start = ((f32[16,16,128]{2,1,0:T(8,128)}), f32[16,16,128]{2,1,0:T(8,128)S(1)}, u32[]{:S(2)}, u32[]{:S(2)}) async-start(f32[16,16,128]{2,1,0:T(8,128)} %bitcast.6), calls=%async_computation | async-start | bytes 262144 | tf_op jit(solution)/shard_map/all_to_all | solution.py:529
  10.7 0.8 %y_faces.1 = (f32[8,64,128]{2,1,0:T(8,128)}, f32[8,64,128]{2,1,0:T(8,128)}) custom-call(f32[32,64,128]{2,1,0:T(8,128)S(1)} %get-tuple-element.13.near_gas.gas), custom_call_target="tpu_custom_call" | custom-call | bytes 2214000 | tf_op jit(solution)/shard_map/y_faces/pallas_call | solution.py:589
  11.5 1.4 %collective-permute-start.2 = (f32[8,64,128]{2,1,0:T(8,128)}, f32[8,64,128]{2,1,0:T(8,128)S(1)}, u32[]{:S(2)}, u32[]{:S(2)}) collective-permute-start(f32[8,64,128]{2,1,0:T(8,128)} %get-tuple-element.16), channel_id=1, source_target_pairs={{0,4},{1,5},{2,6},{3,7},{8,12},{9,13},{10,14},{11,15},{4,0},{5,1},... | collective-permute-start | bytes 786440 | tf_op jit(solution)/shard_map/ppermute | solution.py:285
  12.9 0.6 %collective-permute-start.3 = (f32[8,64,128]{2,1,0:T(8,128)}, f32[8,64,128]{2,1,0:T(8,128)S(1)}, u32[]{:S(2)}, u32[]{:S(2)}) collective-permute-start(f32[8,64,128]{2,1,0:T(8,128)} %get-tuple-element.17), channel_id=1, source_target_pairs={{4,8},{5,9},{6,10},{7,11},{0,1},{2,3},{12,13},{14,15},{8,4},{9,5},... | collective-permute-start | bytes 786440 | tf_op jit(solution)/shard_map/ppermute | solution.py:285
  13.6 1.2 %collective-permute-start = (f32[8,64,128]{2,1,0:T(8,128)}, f32[8,64,128]{2,1,0:T(8,128)S(1)}, u32[]{:S(2)}, u32[]{:S(2)}) collective-permute-start(f32[8,64,128]{2,1,0:T(8,128)} %get-tuple-element.14), channel_id=1, source_target_pairs={{0,16},{16,0},{1,17},{17,1},{2,18},{18,2},{3,19},{19,3},{4,20},{20... | collective-permute-start | bytes 786440 | tf_op jit(solution)/shard_map/ppermute | solution.py:285
  14.8 0.0 copy-start.1
  14.8 0.0 copy-start.2
  14.8 0.3 collective-permute-start.1
  15.0 2.6 %all-to-all-done = f32[16,16,128]{2,1,0:T(8,128)S(1)} async-done(((f32[16,16,128]{2,1,0:T(8,128)}), f32[16,16,128]{2,1,0:T(8,128)S(1)}, u32[]{:S(2)}, u32[]{:S(2)}) %all-to-all-start) | async-done | bytes 131104 | tf_op jit(solution)/shard_map/all_to_all | solution.py:529
  17.6 0.0 copy-done.1
  17.6 0.0 copy-done.2
  17.6 4.5 %couple_gas.1 = (f32[128,128]{1,0:T(8,128)}, f32[32,64,128]{2,1,0:T(8,128)S(1)}) custom-call(f32[256,128]{1,0:T(8,128)S(1)} %bitcast.11, f32[32,64,128]{2,1,0:T(8,128)S(1)} %get-tuple-element.13.near_gas.gas, f32[1,64]{1,0:T(1,128)S(1)} %bitcast.14, f32[1,64]{1,0:T(1,128)S(1)} %bitcast.17), custom_call_target="tpu_custom_call" | custom-call | bytes 25830000 | tf_op jit(solution)/shard_map/couple_gas/pallas_call | solution.py:615
  22.1 4.9 %all-to-all-start.1 = ((f32[16,8,128]{2,1,0:T(8,128)}), f32[16,8,128]{2,1,0:T(8,128)S(1)}, u32[]{:S(2)}, u32[]{:S(2)}) async-start(f32[16,8,128]{2,1,0:T(8,128)} %bitcast.9), calls=%async_computation.1 | async-start | bytes 131072 | tf_op jit(solution)/shard_map/all_to_all | solution.py:529
  27.0 0.0 collective-permute-done.2.refs_2_.ya.refs_1_
  27.0 0.0 collective-permute-done.3.refs_3_.yb.refs_2_
  27.0 0.0 copy-start.3
  27.0 1.3 %collective-permute-start.4 = (f32[2,64,128]{2,1,0:T(8,128)S(1)}, f32[2,64,128]{2,1,0:T(8,128)S(1)}, u32[]{:S(2)}, u32[]{:S(2)}) collective-permute-start(f32[2,64,128]{2,1,0:T(8,128)S(1)} %corner_planes.1), channel_id=1, source_target_pairs={{0,16},{16,0},{1,17},{17,1},{2,18},{18,2},{3,19},{19,3},{4,20},{20... | collective-permute-start | bytes 196616 | tf_op jit(solution)/shard_map/ppermute | solution.py:285
  28.3 0.0 collective-permute-done.refs_0_
  28.3 0.0 copy-done.3
  28.3 0.6 %z_message.1 = (f32[48,128]{1,0:T(8,128)S(1)}, f32[48,128]{1,0:T(8,128)S(1)}) custom-call(f32[32,64,128]{2,1,0:T(8,128)S(1)} %get-tuple-element.13.near_gas.gas, f32[8,64,128]{2,1,0:T(8,128)S(1)} %collective-permute-done.refs_0_, f32[8,64,128]{2,1,0:T(8,128)S(1)} %collective-permute-done.2.refs_2_.ya.refs_1_, ...), custom_call_target="tpu_custom_call" | custom-call | bytes 2214000 | tf_op jit(solution)/shard_map/z_message/pallas_call | solution.py:635
  28.9 0.6 %collective-permute-start.5 = (f32[48,128]{1,0:T(8,128)S(1)}, f32[48,128]{1,0:T(8,128)S(1)}, u32[]{:S(2)}, u32[]{:S(2)}) collective-permute-start(f32[48,128]{1,0:T(8,128)S(1)} %get-tuple-element.20.refs_1_), channel_id=1, source_target_pairs={{0,1},{2,3},{1,0},{3,2},{4,5},{6,7},{5,4},{7,6},{8,9},{10,11},{9,8... | collective-permute-start | bytes 73736 | tf_op jit(solution)/shard_map/ppermute | solution.py:285
  29.5 1.5 %collective-permute-start.6 = (f32[48,128]{1,0:T(8,128)S(1)}, f32[48,128]{1,0:T(8,128)S(1)}, u32[]{:S(2)}, u32[]{:S(2)}) collective-permute-start(f32[48,128]{1,0:T(8,128)S(1)} %get-tuple-element.21.refs_2_), channel_id=1, source_target_pairs={{1,2},{3,0},{2,1},{0,3},{5,6},{7,4},{6,5},{4,7},{9,10},{11,8},{10,... | collective-permute-start | bytes 73736 | tf_op jit(solution)/shard_map/ppermute | solution.py:285
  31.0 0.0 collective-permute-done.1.refs_1_
  31.0 1.7 %gas_steps.1.partial = f32[32,64,128]{2,1,0:T(8,128)S(1)} custom-call(f32[32,64,128]{2,1,0:T(8,128)S(1)} %get-tuple-element.13.near_gas.gas, f32[8,64,128]{2,1,0:T(8,128)S(1)} %collective-permute-done.refs_0_, f32[8,64,128]{2,1,0:T(8,128)S(1)} %collective-permute-done.1.refs_1_, f32[8,64,128]{2,1,0:T(8,128)S(1)} %collective-permute-done.2.refs_2_.ya.refs_1_, ...), custom_call_target="tpu_custom_call" | custom-call | bytes 8118000 | tf_op jit(solution)/shard_map/gas_steps/pallas_call | solution.py:644
  32.6 0.0 copy-start
  32.6 0.0 collective-permute-done.5.refs_3_
  32.7 0.4 %collective-permute-done.6.refs_4_ = f32[48,128]{1,0:T(8,128)S(1)} collective-permute-done((f32[48,128]{1,0:T(8,128)S(1)}, f32[48,128]{1,0:T(8,128)S(1)}, u32[]{:S(2)}, u32[]{:S(2)}) %collective-permute-start.6) | collective-permute-done | bytes 24608 | tf_op jit(solution)/shard_map/ppermute | solution.py:285
  33.1 0.0 collective-permute-done.4.refs_0_
  33.1 1.5 %close_gas_step.1._ = f32[64,32,128]{2,1,0:T(8,128)} custom-call(f32[32,64,128]{2,1,0:T(8,128)S(1)} %gas_steps.1.partial, f32[2,64,128]{2,1,0:T(8,128)S(1)} %collective-permute-done.4.refs_0_, f32[48,128]{1,0:T(8,128)S(1)} %get-tuple-element.20.refs_1_, f32[48,128]{1,0:T(8,128)S(1)} %get-tuple-element.21.refs_2_, ...), custom_call_target="tpu_custom_call" | custom-call | bytes 5535000 | tf_op jit(solution)/shard_map/close_gas_step/pallas_call | solution.py:658
  34.6 0.0 all-to-all-done.1
  34.6 0.0 copy-done
  34.6 1.6 %droplets.1 = f32[32,64,128]{2,1,0:T(8,128)} custom-call(f32[32,64,128]{2,1,0:T(8,128)S(1)} %copy-done, f32[128,128]{1,0:T(8,128)S(1)} %bitcast.12, s32[1,128]{1,0:T(1,128)S(1)} %get-tuple-element.23.slots, f32[1,64]{1,0:T(1,128)S(1)} %bitcast.15, f32[1,64]{1,0:T(1,128)S(1)} %bitcast.18, f32[64,32,128]{2,1,0:T(8,128)} %close_gas_step.1._), custom_call_target="tpu_custom_call" | custom-call | bytes 9225000 | tf_op jit(solution)/shard_map/droplets/pallas_call | solution.py:668
  (1 shorter events, 0.0 us)
Async XLA Ops:
  3.3 14.3 %all-to-all-start = ((f32[16,16,128]{2,1,0:T(8,128)}), f32[16,16,128]{2,1,0:T(8,128)S(1)}, u32[]{:S(2)}, u32[]{:S(2)}) async-start(f32[16,16,128]{2,1,0:T(8,128)} %bitcast.6), calls=%async_computation | async-start | bytes 262144 | tf_op jit(solution)/shard_map/all_to_all | solution.py:529
  11.5 15.5 %collective-permute-start.2 = (f32[8,64,128]{2,1,0:T(8,128)}, f32[8,64,128]{2,1,0:T(8,128)S(1)}, u32[]{:S(2)}, u32[]{:S(2)}) collective-permute-start(f32[8,64,128]{2,1,0:T(8,128)} %get-tuple-element.16), channel_id=1, source_target_pairs={{0,4},{1,5},{2,6},{3,7},{8,12},{9,13},{10,14},{11,15},{4,0},{5,1},... | collective-permute-start | bytes 786440 | tf_op jit(solution)/shard_map/ppermute | solution.py:285
  12.9 14.1 %collective-permute-start.3 = (f32[8,64,128]{2,1,0:T(8,128)}, f32[8,64,128]{2,1,0:T(8,128)S(1)}, u32[]{:S(2)}, u32[]{:S(2)}) collective-permute-start(f32[8,64,128]{2,1,0:T(8,128)} %get-tuple-element.17), channel_id=1, source_target_pairs={{4,8},{5,9},{6,10},{7,11},{0,1},{2,3},{12,13},{14,15},{8,4},{9,5},... | collective-permute-start | bytes 786440 | tf_op jit(solution)/shard_map/ppermute | solution.py:285
  13.6 14.8 %collective-permute-start = (f32[8,64,128]{2,1,0:T(8,128)}, f32[8,64,128]{2,1,0:T(8,128)S(1)}, u32[]{:S(2)}, u32[]{:S(2)}) collective-permute-start(f32[8,64,128]{2,1,0:T(8,128)} %get-tuple-element.14), channel_id=1, source_target_pairs={{0,16},{16,0},{1,17},{17,1},{2,18},{18,2},{3,19},{19,3},{4,20},{20... | collective-permute-start | bytes 786440 | tf_op jit(solution)/shard_map/ppermute | solution.py:285
  14.8 2.8 %copy-start.1 = (f32[64]{0:T(128)S(1)}, f32[64]{0:T(128)}, u32[]{:S(2)}) copy-start(f32[64]{0:T(128)} %param.15) | copy-start | bytes 772
  14.8 2.8 %copy-start.2 = (f32[64]{0:T(128)S(1)}, f32[64]{0:T(128)}, u32[]{:S(2)}) copy-start(f32[64]{0:T(128)} %param.16) | copy-start | bytes 772
  14.8 16.2 %collective-permute-start.1 = (f32[8,64,128]{2,1,0:T(8,128)S(1)}, f32[8,64,128]{2,1,0:T(8,128)S(1)}, u32[]{:S(2)}, u32[]{:S(2)}) collective-permute-start(f32[8,64,128]{2,1,0:T(8,128)S(1)} %get-tuple-element.15), channel_id=1, source_target_pairs={{0,16},{16,0},{1,17},{17,1},{2,18},{18,2},{3,19},{19,3},{4,20},{20... | collective-permute-start | bytes 786440 | tf_op jit(solution)/shard_map/ppermute | solution.py:285
  22.1 12.5 %all-to-all-start.1 = ((f32[16,8,128]{2,1,0:T(8,128)}), f32[16,8,128]{2,1,0:T(8,128)S(1)}, u32[]{:S(2)}, u32[]{:S(2)}) async-start(f32[16,8,128]{2,1,0:T(8,128)} %bitcast.9), calls=%async_computation.1 | async-start | bytes 131072 | tf_op jit(solution)/shard_map/all_to_all | solution.py:529
  27.0 1.3 %copy-start.3 = (f32[64]{0:T(128)S(1)}, f32[64]{0:T(128)}, u32[]{:S(2)}) copy-start(f32[64]{0:T(128)} %param.17) | copy-start | bytes 772
  27.0 6.0 %collective-permute-start.4 = (f32[2,64,128]{2,1,0:T(8,128)S(1)}, f32[2,64,128]{2,1,0:T(8,128)S(1)}, u32[]{:S(2)}, u32[]{:S(2)}) collective-permute-start(f32[2,64,128]{2,1,0:T(8,128)S(1)} %corner_planes.1), channel_id=1, source_target_pairs={{0,16},{16,0},{1,17},{17,1},{2,18},{18,2},{3,19},{19,3},{4,20},{20... | collective-permute-start | bytes 196616 | tf_op jit(solution)/shard_map/ppermute | solution.py:285
  28.9 3.7 %collective-permute-start.5 = (f32[48,128]{1,0:T(8,128)S(1)}, f32[48,128]{1,0:T(8,128)S(1)}, u32[]{:S(2)}, u32[]{:S(2)}) collective-permute-start(f32[48,128]{1,0:T(8,128)S(1)} %get-tuple-element.20.refs_1_), channel_id=1, source_target_pairs={{0,1},{2,3},{1,0},{3,2},{4,5},{6,7},{5,4},{7,6},{8,9},{10,11},{9,8... | collective-permute-start | bytes 73736 | tf_op jit(solution)/shard_map/ppermute | solution.py:285
  29.5 3.6 %collective-permute-start.6 = (f32[48,128]{1,0:T(8,128)S(1)}, f32[48,128]{1,0:T(8,128)S(1)}, u32[]{:S(2)}, u32[]{:S(2)}) collective-permute-start(f32[48,128]{1,0:T(8,128)S(1)} %get-tuple-element.21.refs_2_), channel_id=1, source_target_pairs={{1,2},{3,0},{2,1},{0,3},{5,6},{7,4},{6,5},{4,7},{9,10},{11,8},{10,... | collective-permute-start | bytes 73736 | tf_op jit(solution)/shard_map/ppermute | solution.py:285
  32.6 2.0 %copy-start = (f32[32,64,128]{2,1,0:T(8,128)S(1)}, f32[32,64,128]{2,1,0:T(8,128)}, u32[]{:S(2)}) copy-start(f32[32,64,128]{2,1,0:T(8,128)} %state_in.1) | copy-start | bytes 3145732

commit v10 on v9

--- a/solution.py
+++ b/solution.py
@@ -106,6 +106,9 @@
         ],
         axis=0,
     )
+    parts = jnp.concatenate(split_all(values), axis=0)
+    placed = lax.dot_general(place, parts, NT, preferred_element_type=F32)
+    send[...] = placed[:, :LANES] + placed[:, LANES : 2 * LANES] + placed[:, 2 * LANES :]
     for load in loads[small:]:
         load.wait()
     even_x, _, _ = place_on("gx")
@@ -116,9 +119,6 @@
         for y in range(size_y):
             x_sends[turn][y] = near_gas[near + y]
             x_sends[turns_x + turn][y] = near_gas[far + y]
-    parts = jnp.concatenate(split_all(values), axis=0)
-    placed = lax.dot_general(place, parts, NT, preferred_element_type=F32)
-    send[...] = placed[:, :LANES] + placed[:, LANES : 2 * LANES] + placed[:, 2 * LANES :]
 
 
 def y_faces_kernel(size_x, size_y, near_gas, ya, yb):

time: 36.5 us -> 36.3 us (level)
  no operation moved by 1% of the time
where the time goes in v10:
time: 36.3 us; the launch traced here: 36 us
  starting transfers between devices  19.1 us (53%)
  Pallas kernels  13.2 us (36%)
  waiting for transfers between devices  3 us (8%)
  between operations  0.73 us (2%)
    all_to_all x2, starting transfers between devices, exchange(): lax.all_to_all(chunks, ('gy', 'gz'), split_axis=0, concat_axis=0, tiled=T...  12.3 us
    ppermute x7, starting transfers between devices, swap_all(): lax.ppermute(m, axes, pairs)  6.83 us
    pallas_call x1, Pallas kernels, on_device(): pl.pallas_call(functools.partial(couple_kernel, cap, packed), out_shape=[...  4.47 us
    all_to_all x2, waiting for transfers between devices, exchange(): lax.all_to_all(chunks, ('gy', 'gz'), split_axis=0, concat_axis=0, tiled=T...  2.56 us
    pallas_call x1, Pallas kernels, on_device(): pl.pallas_call(functools.partial(pack_kernel, cap, size_x, size_y, turns_...  2.51 us
    pallas_call x1, Pallas kernels, on_device(): pl.pallas_call(functools.partial(steps_kernel, size_x, size_y, turns_x),...  1.66 us
    pallas_call x1, Pallas kernels, on_device(): pl.pallas_call(functools.partial(droplet_kernel, cap, packed), out_shape=...  1.62 us
    pallas_call x1, Pallas kernels, on_device(): pl.pallas_call(functools.partial(close_kernel, size_x, size_y, turns_x),...  1.48 us
  transfers between devices with their start and end apart: 9, of which 2 were waited for; matrix products, arithmetic and copies ran while one was open for 0% of the time, Pallas kernels for 25%

profile of v10, /device:TPU:1, one launch (start us, length us, event | category | flops | bytes accessed | tf_op | source)
XLA Modules:
  0.0 36.0 jit_solution(3084818665408140099)
XLA Ops:
  0.6 2.5 %pack.1 = (f32[256,128]{1,0:T(8,128)}, s32[1,128]{1,0:T(1,128)S(1)}, f32[32,64,128]{2,1,0:T(8,128)S(1)}, f32[8,64,128]{2,1,0:T(8,128)}, f32[8,64,128]{2,1,0:T(8,128)S(1)}) custom-call(f32[32,64,128]{2,1,0:T(8,128)} %state_in.1, f32[64,32,128]{2,1,0:T(8,128)} %bitcast.23, s32[1,128]{1,0:T(1,128)} %bitcast.24, s32[8,128]{1,0:T(8,128)} %refs_1_.1, ...), custom_call_target="tpu_custom_call" | custom-call | bytes 9225000 | tf_op jit(solution)/shard_map/pack/pallas_call | solution.py:554
  3.1 7.4 %all-to-all-start = ((f32[16,16,128]{2,1,0:T(8,128)}), f32[16,16,128]{2,1,0:T(8,128)S(1)}, u32[]{:S(2)}, u32[]{:S(2)}) async-start(f32[16,16,128]{2,1,0:T(8,128)} %bitcast.6), calls=%async_computation | async-start | bytes 262144 | tf_op jit(solution)/shard_map/all_to_all | solution.py:529
  10.5 0.8 %y_faces.1 = (f32[8,64,128]{2,1,0:T(8,128)}, f32[8,64,128]{2,1,0:T(8,128)}) custom-call(f32[32,64,128]{2,1,0:T(8,128)S(1)} %get-tuple-element.13.near_gas.gas), custom_call_target="tpu_custom_call" | custom-call | bytes 2214000 | tf_op jit(solution)/shard_map/y_faces/pallas_call | solution.py:589
  11.3 1.4 %collective-permute-start.2 = (f32[8,64,128]{2,1,0:T(8,128)}, f32[8,64,128]{2,1,0:T(8,128)S(1)}, u32[]{:S(2)}, u32[]{:S(2)}) collective-permute-start(f32[8,64,128]{2,1,0:T(8,128)} %get-tuple-element.16), channel_id=1, source_target_pairs={{0,4},{1,5},{2,6},{3,7},{8,12},{9,13},{10,14},{11,15},{4,0},{5,1},... | collective-permute-start | bytes 786440 | tf_op jit(solution)/shard_map/ppermute | solution.py:285
  12.7 0.6 %collective-permute-start.3 = (f32[8,64,128]{2,1,0:T(8,128)}, f32[8,64,128]{2,1,0:T(8,128)S(1)}, u32[]{:S(2)}, u32[]{:S(2)}) collective-permute-start(f32[8,64,128]{2,1,0:T(8,128)} %get-tuple-element.17), channel_id=1, source_target_pairs={{4,8},{5,9},{6,10},{7,11},{0,1},{2,3},{12,13},{14,15},{8,4},{9,5},... | collective-permute-start | bytes 786440 | tf_op jit(solution)/shard_map/ppermute | solution.py:285
  13.4 1.2 %collective-permute-start = (f32[8,64,128]{2,1,0:T(8,128)}, f32[8,64,128]{2,1,0:T(8,128)S(1)}, u32[]{:S(2)}, u32[]{:S(2)}) collective-permute-start(f32[8,64,128]{2,1,0:T(8,128)} %get-tuple-element.14), channel_id=1, source_target_pairs={{0,16},{16,0},{1,17},{17,1},{2,18},{18,2},{3,19},{19,3},{4,20},{20... | collective-permute-start | bytes 786440 | tf_op jit(solution)/shard_map/ppermute | solution.py:285
  14.6 0.0 copy-start.1
  14.6 0.0 copy-start.2
  14.6 0.3 collective-permute-start.1
  14.8 2.6 %all-to-all-done = f32[16,16,128]{2,1,0:T(8,128)S(1)} async-done(((f32[16,16,128]{2,1,0:T(8,128)}), f32[16,16,128]{2,1,0:T(8,128)S(1)}, u32[]{:S(2)}, u32[]{:S(2)}) %all-to-all-start) | async-done | bytes 131104 | tf_op jit(solution)/shard_map/all_to_all | solution.py:529
  17.4 0.0 copy-done.1
  17.4 0.0 copy-done.2
  17.4 4.5 %couple_gas.1 = (f32[128,128]{1,0:T(8,128)}, f32[32,64,128]{2,1,0:T(8,128)S(1)}) custom-call(f32[256,128]{1,0:T(8,128)S(1)} %bitcast.11, f32[32,64,128]{2,1,0:T(8,128)S(1)} %get-tuple-element.13.near_gas.gas, f32[1,64]{1,0:T(1,128)S(1)} %bitcast.14, f32[1,64]{1,0:T(1,128)S(1)} %bitcast.17), custom_call_target="tpu_custom_call" | custom-call | bytes 25830000 | tf_op jit(solution)/shard_map/couple_gas/pallas_call | solution.py:615
  21.9 4.9 %all-to-all-start.1 = ((f32[16,8,128]{2,1,0:T(8,128)}), f32[16,8,128]{2,1,0:T(8,128)S(1)}, u32[]{:S(2)}, u32[]{:S(2)}) async-start(f32[16,8,128]{2,1,0:T(8,128)} %bitcast.9), calls=%async_computation.1 | async-start | bytes 131072 | tf_op jit(solution)/shard_map/all_to_all | solution.py:529
  26.8 0.0 collective-permute-done.2.refs_2_.ya.refs_1_
  26.8 0.0 collective-permute-done.3.refs_3_.yb.refs_2_
  26.8 0.0 copy-start.3
  26.9 1.3 %collective-permute-start.4 = (f32[2,64,128]{2,1,0:T(8,128)S(1)}, f32[2,64,128]{2,1,0:T(8,128)S(1)}, u32[]{:S(2)}, u32[]{:S(2)}) collective-permute-start(f32[2,64,128]{2,1,0:T(8,128)S(1)} %corner_planes.1), channel_id=1, source_target_pairs={{0,16},{16,0},{1,17},{17,1},{2,18},{18,2},{3,19},{19,3},{4,20},{20... | collective-permute-start | bytes 196616 | tf_op jit(solution)/shard_map/ppermute | solution.py:285
  28.1 0.0 collective-permute-done.refs_0_
  28.1 0.0 copy-done.3
  28.1 0.6 %z_message.1 = (f32[48,128]{1,0:T(8,128)S(1)}, f32[48,128]{1,0:T(8,128)S(1)}) custom-call(f32[32,64,128]{2,1,0:T(8,128)S(1)} %get-tuple-element.13.near_gas.gas, f32[8,64,128]{2,1,0:T(8,128)S(1)} %collective-permute-done.refs_0_, f32[8,64,128]{2,1,0:T(8,128)S(1)} %collective-permute-done.2.refs_2_.ya.refs_1_, ...), custom_call_target="tpu_custom_call" | custom-call | bytes 2214000 | tf_op jit(solution)/shard_map/z_message/pallas_call | solution.py:635
  28.7 0.6 %collective-permute-start.5 = (f32[48,128]{1,0:T(8,128)S(1)}, f32[48,128]{1,0:T(8,128)S(1)}, u32[]{:S(2)}, u32[]{:S(2)}) collective-permute-start(f32[48,128]{1,0:T(8,128)S(1)} %get-tuple-element.20.refs_1_), channel_id=1, source_target_pairs={{0,1},{2,3},{1,0},{3,2},{4,5},{6,7},{5,4},{7,6},{8,9},{10,11},{9,8... | collective-permute-start | bytes 73736 | tf_op jit(solution)/shard_map/ppermute | solution.py:285
  29.3 1.5 %collective-permute-start.6 = (f32[48,128]{1,0:T(8,128)S(1)}, f32[48,128]{1,0:T(8,128)S(1)}, u32[]{:S(2)}, u32[]{:S(2)}) collective-permute-start(f32[48,128]{1,0:T(8,128)S(1)} %get-tuple-element.21.refs_2_), channel_id=1, source_target_pairs={{1,2},{3,0},{2,1},{0,3},{5,6},{7,4},{6,5},{4,7},{9,10},{11,8},{10,... | collective-permute-start | bytes 73736 | tf_op jit(solution)/shard_map/ppermute | solution.py:285
  30.8 0.0 collective-permute-done.1.refs_1_
  30.8 1.7 %gas_steps.1.partial = f32[32,64,128]{2,1,0:T(8,128)S(1)} custom-call(f32[32,64,128]{2,1,0:T(8,128)S(1)} %get-tuple-element.13.near_gas.gas, f32[8,64,128]{2,1,0:T(8,128)S(1)} %collective-permute-done.refs_0_, f32[8,64,128]{2,1,0:T(8,128)S(1)} %collective-permute-done.1.refs_1_, f32[8,64,128]{2,1,0:T(8,128)S(1)} %collective-permute-done.2.refs_2_.ya.refs_1_, ...), custom_call_target="tpu_custom_call" | custom-call | bytes 8118000 | tf_op jit(solution)/shard_map/gas_steps/pallas_call | solution.py:644
  32.4 0.0 copy-start
  32.5 0.0 collective-permute-done.5.refs_3_
  32.5 0.4 %collective-permute-done.6.refs_4_ = f32[48,128]{1,0:T(8,128)S(1)} collective-permute-done((f32[48,128]{1,0:T(8,128)S(1)}, f32[48,128]{1,0:T(8,128)S(1)}, u32[]{:S(2)}, u32[]{:S(2)}) %collective-permute-start.6) | collective-permute-done | bytes 24608 | tf_op jit(solution)/shard_map/ppermute | solution.py:285
  32.9 0.0 collective-permute-done.4.refs_0_
  32.9 1.5 %close_gas_step.1._ = f32[64,32,128]{2,1,0:T(8,128)} custom-call(f32[32,64,128]{2,1,0:T(8,128)S(1)} %gas_steps.1.partial, f32[2,64,128]{2,1,0:T(8,128)S(1)} %collective-permute-done.4.refs_0_, f32[48,128]{1,0:T(8,128)S(1)} %get-tuple-element.20.refs_1_, f32[48,128]{1,0:T(8,128)S(1)} %get-tuple-element.21.refs_2_, ...), custom_call_target="tpu_custom_call" | custom-call | bytes 5535000 | tf_op jit(solution)/shard_map/close_gas_step/pallas_call | solution.py:658
  34.4 0.0 all-to-all-done.1
  34.4 0.0 copy-done
  34.4 1.6 %droplets.1 = f32[32,64,128]{2,1,0:T(8,128)} custom-call(f32[32,64,128]{2,1,0:T(8,128)S(1)} %copy-done, f32[128,128]{1,0:T(8,128)S(1)} %bitcast.12, s32[1,128]{1,0:T(1,128)S(1)} %get-tuple-element.23.slots, f32[1,64]{1,0:T(1,128)S(1)} %bitcast.15, f32[1,64]{1,0:T(1,128)S(1)} %bitcast.18, f32[64,32,128]{2,1,0:T(8,128)} %close_gas_step.1._), custom_call_target="tpu_custom_call" | custom-call | bytes 9225000 | tf_op jit(solution)/shard_map/droplets/pallas_call | solution.py:668
  (1 shorter events, 0.0 us)
Async XLA Ops:
  3.1 14.3 %all-to-all-start = ((f32[16,16,128]{2,1,0:T(8,128)}), f32[16,16,128]{2,1,0:T(8,128)S(1)}, u32[]{:S(2)}, u32[]{:S(2)}) async-start(f32[16,16,128]{2,1,0:T(8,128)} %bitcast.6), calls=%async_computation | async-start | bytes 262144 | tf_op jit(solution)/shard_map/all_to_all | solution.py:529
  11.3 15.5 %collective-permute-start.2 = (f32[8,64,128]{2,1,0:T(8,128)}, f32[8,64,128]{2,1,0:T(8,128)S(1)}, u32[]{:S(2)}, u32[]{:S(2)}) collective-permute-start(f32[8,64,128]{2,1,0:T(8,128)} %get-tuple-element.16), channel_id=1, source_target_pairs={{0,4},{1,5},{2,6},{3,7},{8,12},{9,13},{10,14},{11,15},{4,0},{5,1},... | collective-permute-start | bytes 786440 | tf_op jit(solution)/shard_map/ppermute | solution.py:285
  12.7 14.1 %collective-permute-start.3 = (f32[8,64,128]{2,1,0:T(8,128)}, f32[8,64,128]{2,1,0:T(8,128)S(1)}, u32[]{:S(2)}, u32[]{:S(2)}) collective-permute-start(f32[8,64,128]{2,1,0:T(8,128)} %get-tuple-element.17), channel_id=1, source_target_pairs={{4,8},{5,9},{6,10},{7,11},{0,1},{2,3},{12,13},{14,15},{8,4},{9,5},... | collective-permute-start | bytes 786440 | tf_op jit(solution)/shard_map/ppermute | solution.py:285
  13.4 14.8 %collective-permute-start = (f32[8,64,128]{2,1,0:T(8,128)}, f32[8,64,128]{2,1,0:T(8,128)S(1)}, u32[]{:S(2)}, u32[]{:S(2)}) collective-permute-start(f32[8,64,128]{2,1,0:T(8,128)} %get-tuple-element.14), channel_id=1, source_target_pairs={{0,16},{16,0},{1,17},{17,1},{2,18},{18,2},{3,19},{19,3},{4,20},{20... | collective-permute-start | bytes 786440 | tf_op jit(solution)/shard_map/ppermute | solution.py:285
  14.6 2.8 %copy-start.1 = (f32[64]{0:T(128)S(1)}, f32[64]{0:T(128)}, u32[]{:S(2)}) copy-start(f32[64]{0:T(128)} %param.15) | copy-start | bytes 772
  14.6 2.8 %copy-start.2 = (f32[64]{0:T(128)S(1)}, f32[64]{0:T(128)}, u32[]{:S(2)}) copy-start(f32[64]{0:T(128)} %param.16) | copy-start | bytes 772
  14.6 16.2 %collective-permute-start.1 = (f32[8,64,128]{2,1,0:T(8,128)S(1)}, f32[8,64,128]{2,1,0:T(8,128)S(1)}, u32[]{:S(2)}, u32[]{:S(2)}) collective-permute-start(f32[8,64,128]{2,1,0:T(8,128)S(1)} %get-tuple-element.15), channel_id=1, source_target_pairs={{0,16},{16,0},{1,17},{17,1},{2,18},{18,2},{3,19},{19,3},{4,20},{20... | collective-permute-start | bytes 786440 | tf_op jit(solution)/shard_map/ppermute | solution.py:285
  21.9 12.5 %all-to-all-start.1 = ((f32[16,8,128]{2,1,0:T(8,128)}), f32[16,8,128]{2,1,0:T(8,128)S(1)}, u32[]{:S(2)}, u32[]{:S(2)}) async-start(f32[16,8,128]{2,1,0:T(8,128)} %bitcast.9), calls=%async_computation.1 | async-start | bytes 131072 | tf_op jit(solution)/shard_map/all_to_all | solution.py:529
  26.8 1.3 %copy-start.3 = (f32[64]{0:T(128)S(1)}, f32[64]{0:T(128)}, u32[]{:S(2)}) copy-start(f32[64]{0:T(128)} %param.17) | copy-start | bytes 772
  26.9 6.0 %collective-permute-start.4 = (f32[2,64,128]{2,1,0:T(8,128)S(1)}, f32[2,64,128]{2,1,0:T(8,128)S(1)}, u32[]{:S(2)}, u32[]{:S(2)}) collective-permute-start(f32[2,64,128]{2,1,0:T(8,128)S(1)} %corner_planes.1), channel_id=1, source_target_pairs={{0,16},{16,0},{1,17},{17,1},{2,18},{18,2},{3,19},{19,3},{4,20},{20... | collective-permute-start | bytes 196616 | tf_op jit(solution)/shard_map/ppermute | solution.py:285
  28.7 3.7 %collective-permute-start.5 = (f32[48,128]{1,0:T(8,128)S(1)}, f32[48,128]{1,0:T(8,128)S(1)}, u32[]{:S(2)}, u32[]{:S(2)}) collective-permute-start(f32[48,128]{1,0:T(8,128)S(1)} %get-tuple-element.20.refs_1_), channel_id=1, source_target_pairs={{0,1},{2,3},{1,0},{3,2},{4,5},{6,7},{5,4},{7,6},{8,9},{10,11},{9,8... | collective-permute-start | bytes 73736 | tf_op jit(solution)/shard_map/ppermute | solution.py:285
  29.3 3.6 %collective-permute-start.6 = (f32[48,128]{1,0:T(8,128)S(1)}, f32[48,128]{1,0:T(8,128)S(1)}, u32[]{:S(2)}, u32[]{:S(2)}) collective-permute-start(f32[48,128]{1,0:T(8,128)S(1)} %get-tuple-element.21.refs_2_), channel_id=1, source_target_pairs={{1,2},{3,0},{2,1},{0,3},{5,6},{7,4},{6,5},{4,7},{9,10},{11,8},{10,... | collective-permute-start | bytes 73736 | tf_op jit(solution)/shard_map/ppermute | solution.py:285
  32.4 2.0 %copy-start = (f32[32,64,128]{2,1,0:T(8,128)S(1)}, f32[32,64,128]{2,1,0:T(8,128)}, u32[]{:S(2)}) copy-start(f32[32,64,128]{2,1,0:T(8,128)} %state_in.1) | copy-start | bytes 3145732
